TPU v7x, 32 devices: a whole 2x2x4 slice. The times are simulated.
32 devices in a mesh: comp: 4 (over x, core), tile: 8 (over z, y).
Axes of the slice: x: 2, y: 2, z: 4, core: 2. Of those that a mesh axis runs over, the one named last changes fastest.
Arguments:
- forcing: float32 [4, 8, 16, 256, 128], P('comp', None, None, 'tile'), may hold values from -6 to 6
- kappa: float32 [4, 256, 128], P('comp', 'tile'), may hold values from 0.02 to 0.24
- col_blocks: int32 [4, 128, 4], P('comp', 'tile'), may hold values from 0 to 127, as said below
- remap_weights: bfloat16 [4, 128, 4, 256, 256], P('comp', 'tile'), may hold values from -0.1875 to 0.1875
Outputs:
- section_out: bfloat16 [4, 8, 16, 256, 128], P('comp', None, None, 'tile')
Inputs may be any that keep to these rules, and one draw needn't show every extreme that they name: `col_blocks`: the first column block of row block j is j itself; every column block lies within 8 blocks of its row block, cyclically over the 128 blocks; in every row block one lies exactly 8 blocks away.
All inputs are finite; a program needn't handle non-finite values.
Results may differ from a plain program's by a relative error of at most 0.0055.
Values may be sent and summed in bfloat16 or wider, within the bound.
No kernel may reach another device: no remote copies, remote signals or barrier semaphores. Data moves between devices by JAX's collectives and lax.ppermute only.
A program may use at most 64 MiB of HBM per device.

v0:
```python
import functools

import jax
import jax.numpy as jnp
from jax import lax
from jax.experimental import pallas as pl
from jax.experimental.pallas import tpu as pltpu
from jax.sharding import PartitionSpec as P

AXES = ("comp", "tile")
CHUNKS = 2
EDGE = 2
LIMIT = 24 << 20
HBM = pl.BlockSpec(memory_space=pltpu.HBM)
VMEM = pl.BlockSpec(memory_space=pltpu.VMEM)
SMEM = pl.BlockSpec(memory_space=pltpu.SMEM)


def start_all(copies):
    for copy in copies:
        copy.start()


def wait_all(copies):
    for copy in copies:
        copy.wait()


def prepare_kernel(forcing, by_row, narrow, *refs):
    edges, (f_v, n_v, in_sems, out_sems, n_sems) = refs[:-5], refs[-5:]
    rows = f_v.shape[0]
    halo, fields, _ = edges[0].shape
    loads = [pltpu.make_async_copy(forcing.at[:, y], f_v.at[y], in_sems.at[y]) for y in range(rows)]
    start_all(loads)
    stores = []
    for y in range(rows):
        loads[y].wait()
        stores.append(pltpu.make_async_copy(f_v.at[y], by_row.at[y], out_sems.at[y]))
        stores[-1].start()
        n_v[y] = f_v[y].astype(jnp.bfloat16)
    late = [pltpu.make_async_copy(n_v, narrow, n_sems.at[0])]
    for c in range(len(edges) // 2):
        mine = pl.ds(c * fields, fields)
        late.append(pltpu.make_async_copy(n_v.at[pl.ds(0, halo), mine], edges[2 * c], n_sems.at[2 * c + 1]))
        late.append(pltpu.make_async_copy(n_v.at[pl.ds(rows - halo, halo), mine], edges[2 * c + 1], n_sems.at[2 * c + 2]))
    start_all(late)
    wait_all(stores + late)


def prepare(fields, halo):
    total, rows, cells = fields.shape
    n = total // CHUNKS
    edge = jax.ShapeDtypeStruct((halo, n, cells), jnp.bfloat16)
    return pl.pallas_call(
        prepare_kernel,
        in_specs=[HBM],
        out_shape=[
            jax.ShapeDtypeStruct((rows, total, cells), jnp.float32),
            jax.ShapeDtypeStruct((rows, total, cells), jnp.bfloat16),
        ] + [edge] * (2 * CHUNKS),
        out_specs=[HBM] * (2 + 2 * CHUNKS),
        scratch_shapes=[
            pltpu.VMEM((rows, total, cells), jnp.float32),
            pltpu.VMEM((rows, total, cells), jnp.bfloat16),
            pltpu.SemaphoreType.DMA((rows,)),
            pltpu.SemaphoreType.DMA((rows,)),
            pltpu.SemaphoreType.DMA((2 * CHUNKS + 1,)),
        ],
        compiler_params=pltpu.CompilerParams(vmem_limit_bytes=LIMIT),
        cost_estimate=pl.CostEstimate(flops=0, bytes_accessed=fields.size * 12, transcendentals=0),
    )(fields)


def beside_matrix(cells):
    source = lax.broadcasted_iota(jnp.int32, (2 * cells, 2 * cells), 0)
    target = lax.broadcasted_iota(jnp.int32, (2 * cells, 2 * cells), 1)
    apart = (source - target + 2 * cells) % cells
    same = (source < cells) == (target < cells)
    return jnp.where(same & ((apart == 1) | (apart == cells - 1)), 1.0, 0.0).astype(jnp.bfloat16)


def section_kernel(chunk, has_incoming, has_next, flags, offsets, kappa, forcing, *refs):
    refs = list(refs)
    incoming = refs.pop(0) if has_incoming else None
    upper, lower = refs.pop(0), refs.pop(0)
    following = refs.pop(0) if has_next else None
    weights, own_out = refs.pop(0), refs.pop(0)
    if has_next:
        up_out, down_out = refs.pop(0), refs.pop(0)
    once, smooth = refs
    halo, fields, cells = upper.shape
    rows = forcing.shape[0]
    count, per_row = weights.shape[:2]
    block = weights.shape[-1]
    extent = rows + 2 * halo
    lo, hi = halo, halo + rows

    @pl.when(flags[0] == 1)
    def _():
        mine = slice(chunk * fields, (chunk + 1) * fields)
        beside = beside_matrix(cells)
        top = jnp.where(flags[1] == 1, 0.0, 1.0)
        bottom = jnp.where(flags[2] == 1, 0.0, 1.0)

        def entry(i):
            if i < lo:
                return upper[i].astype(jnp.float32)
            if i >= hi:
                return lower[i - hi].astype(jnp.float32)
            value = forcing[i - lo, mine]
            if has_incoming:
                value = value + incoming[i - lo].astype(jnp.float32)
            return value

        def step(i, here, north, south, east_west):
            if i == lo:
                north = north * top
            if i == lo - 1:
                south = south * top
            if i == hi:
                north = north * bottom
            if i == hi - 1:
                south = south * bottom
            return here + kappa[i:i + 1, :] * ((north + south) + (east_west - 4.0 * here))

        def pair_beside(first, second):
            joined = jnp.concatenate([first.astype(jnp.bfloat16), second.astype(jnp.bfloat16)], axis=1)
            total = jnp.dot(joined, beside, preferred_element_type=jnp.float32)
            return total[:, :cells], total[:, cells:]

        there, after = None, entry(0)
        for i in range(0, extent, 2):
            before, here, there = there, after, entry(i + 1)
            after = entry(i + 2) if i + 2 < extent else None
            ew_here, ew_there = pair_beside(here, there)
            if i > 0:
                once[i] = step(i, here, before, there, ew_here)
            if i + 2 < extent:
                once[i + 1] = step(i + 1, there, here, after, ew_there)
        for i in range(2, extent - 2, 2):
            here, there = once[i], once[i + 1]
            ew_here, ew_there = pair_beside(here, there)
            out = i // 2 - 1
            smooth[out, :, :cells] = step(i, here, once[i - 1], there, ew_here).astype(jnp.bfloat16)
            smooth[out, :, cells:] = step(i + 1, there, here, once[i + 2], ew_there).astype(jnp.bfloat16)

        half = (halo - EDGE) * cells // block
        block_rows = block // cells
        for j in range(count):
            total = None
            for k in range(per_row):
                source = smooth[offsets[j, k] + (j + half)]
                term = lax.dot_general(
                    source, weights[j, k], (((1,), (1,)), ((), ())), preferred_element_type=jnp.float32
                )
                total = term if total is None else total + term
            for r in range(block_rows):
                row = j * block_rows + r
                value = total[:, r * cells:(r + 1) * cells].astype(jnp.bfloat16)
                own_out[row] = value
                if has_next:
                    entry_next = value.astype(jnp.float32) + following[row, mine].astype(jnp.float32)
                    if row < halo:
                        up_out[row] = entry_next.astype(jnp.bfloat16)
                    if row >= rows - halo:
                        down_out[row - (rows - halo)] = entry_next.astype(jnp.bfloat16)


def section(chunk, flags, offsets, kappa, forcing, incoming, upper, lower, following, weights):
    rows, total, cells = forcing.shape
    halo, fields, _ = upper.shape
    count, per_row, block, _ = weights.shape
    has_incoming, has_next = incoming is not None, following is not None
    operands = [flags, offsets]
    for value in (kappa, forcing, incoming, upper, lower, following, weights):
        if value is not None:
            operands.append(value)
    outs = [jax.ShapeDtypeStruct((rows, fields, cells), jnp.bfloat16)]
    if has_next:
        outs.append(jax.ShapeDtypeStruct((halo, fields, cells), jnp.bfloat16))
        outs.append(jax.ShapeDtypeStruct((halo, fields, cells), jnp.bfloat16))
    extent = rows + 2 * halo
    return pl.pallas_call(
        functools.partial(section_kernel, chunk, has_incoming, has_next),
        in_specs=[SMEM] * 2 + [VMEM] * (len(operands) - 2),
        out_shape=outs,
        out_specs=[VMEM] * len(outs),
        scratch_shapes=[
            pltpu.VMEM((extent, fields, cells), jnp.float32),
            pltpu.VMEM(((extent - 2 * EDGE) * cells // block, fields, block), jnp.bfloat16),
        ],
        compiler_params=pltpu.CompilerParams(vmem_limit_bytes=LIMIT),
        cost_estimate=pl.CostEstimate(
            flops=2 * count * per_row * block * block * fields,
            bytes_accessed=weights.size * 2 + 8 * rows * fields * cells,
            transcendentals=0,
        ),
    )(*operands)


def local(forcing, kappa, col_blocks, remap_weights):
    n_tile = lax.axis_size("tile")
    n_section = lax.axis_size("comp")
    tile_pos = lax.axis_index("tile")
    section_pos = lax.axis_index("comp")
    weights = remap_weights[0]
    count, block = weights.shape[0], weights.shape[-1]
    rows, cells = forcing.shape[-2:]
    half = count // 2
    halo = half * block // cells + EDGE
    total_blocks = count * n_tile
    global_block = tile_pos * count + jnp.arange(count, dtype=jnp.int32)
    offsets = jnp.mod(col_blocks[0] - global_block[:, None] + half, total_blocks) - half

    def place(s, t):
        return s * n_tile + t % n_tile

    def send(value, source, target, shift):
        return lax.ppermute(value, AXES, [(place(source, t), place(target, t + shift)) for t in range(n_tile)])

    by_row, narrow, *edges = prepare(forcing.reshape(-1, rows, cells), halo)
    arrivals = []
    for c in range(CHUNKS):
        first, last = edges[2 * c:2 * c + 2]
        arrivals.append((None, send(last, 0, 0, 1), send(first, 0, 0, -1)))
    around = [(i, (i + 1) % n_tile) for i in range(n_tile)]
    back = [((i + 1) % n_tile, i) for i in range(n_tile)]
    k_here = kappa[0]
    k_all = jnp.concatenate([
        lax.ppermute(k_here[rows - halo:], "tile", around),
        k_here,
        lax.ppermute(k_here[:halo], "tile", back),
    ])
    following = lax.ppermute(
        narrow, AXES, [(place(s, t), place(s - 1, t)) for s in range(1, n_section) for t in range(n_tile)]
    )
    results = []
    for s in range(n_section):
        flags = jnp.stack([section_pos == s, tile_pos == 0, tile_pos == n_tile - 1]).astype(jnp.int32)
        last = s + 1 == n_section
        leaving = []
        for c in range(CHUNKS):
            incoming, upper, lower = arrivals[c]
            result = section(
                c, flags, offsets, k_all, by_row, incoming, upper, lower, None if last else following, weights
            )
            own = result[0]
            results.append(own if s == 0 else jnp.where(section_pos == s, own, results[-CHUNKS]))
            if not last:
                up, down = result[1:]
                leaving.append((send(own, s, s + 1, 0), send(down, s, s + 1, 1), send(up, s, s + 1, -1)))
        arrivals = leaving
    kept = jnp.concatenate(results[-CHUNKS:], axis=1)
    return jnp.transpose(kept, (1, 0, 2)).reshape(forcing.shape)


def solution(mesh):
    placed = (
        P("comp", None, None, "tile", None),
        P("comp", "tile", None),
        P("comp", "tile", None),
        P("comp", "tile", None, None, None),
    )
    return jax.shard_map(
        local,
        mesh=mesh,
        in_specs=placed,
        out_specs=P("comp", None, None, "tile", None),
        check_vma=False,
    )
```

profile of v0, /device:TPU:3, one launch (start us, length us, event | category | flops | bytes accessed | tf_op | source)
XLA Modules:
  0.0 123.5 jit_solution(15541588642509191060)
XLA Ops:
  0.0 1.6 %copy-done.5 = f32[1,8,16,32,128]{4,3,2,1,0:T(8,128)S(1)} copy-done((f32[1,8,16,32,128]{4,3,2,1,0:T(8,128)S(1)}, f32[1,8,16,32,128]{4,3,2,1,0:T(8,128)}, u32[]{:S(2)}) %copy-start.5) | copy-done | bytes 2097176
  1.6 6.8 %shard_map.46 = (f32[32,128,128]{2,1,0:T(8,128)S(1)}, bf16[32,128,128]{2,1,0:T(8,128)(2,1)}, bf16[18,64,128]{2,1,0:T(8,128)(2,1)S(1)}, bf16[18,64,128]{2,1,0:T(8...) custom-call(f32[128,32,128]{2,1,0:T(8,128)S(1)} %bitcast.25), custom_call_target="tpu_custom_call" | custom-call | bytes 6291456 | tf_op jit(solution)/shard_map/pallas_call | solution.py:54
  8.4 0.7 copy-done.6
  9.1 0.7 copy-done.7
  9.9 2.6 %collective-permute-start.4 = (bf16[32,128,128]{2,1,0:T(8,128)(2,1)}, bf16[32,128,128]{2,1,0:T(8,128)(2,1)S(1)}, u32[]{:S(2)}, u32[]{:S(2)}) collective-permute-start(bf16[32,128,128]{2,1,0:T(8,128)(2,1)} %get-tuple-element.32), channel_id=1, source_target_pairs={{8,0},{9,1},{10,2},{11,3},{12,4},{13,5},{14,6},{15,7},{16,8},{17,9... | collective-permute-start | bytes 3145736 | tf_op jit(solution)/shard_map/ppermute | solution.py:234
  12.5 4.3 %collective-permute-start.1 = (f32[18,128]{1,0:T(8,128)S(1)}, f32[18,128]{1,0:T(8,128)S(1)}, u32[]{:S(2)}, u32[]{:S(2)}) collective-permute-start(f32[18,128]{1,0:T(8,128)S(1)} %get-tuple-element.54), channel_id=1, source_target_pairs={{1,0},{2,1},{3,2},{4,3},{5,4},{6,5},{7,6},{0,7},{9,8},{10,9},{11,1... | collective-permute-start | bytes 27656 | tf_op jit(solution)/shard_map/ppermute | solution.py:232
  16.8 0.0 collective-permute-start
  16.9 0.7 collective-permute-start.14
  17.5 1.4 %collective-permute-start.15 = (bf16[18,64,128]{2,1,0:T(8,128)(2,1)}, bf16[18,64,128]{2,1,0:T(8,128)(2,1)}, u32[]{:S(2)}, u32[]{:S(2)}) collective-permute-start(bf16[18,64,128]{2,1,0:T(8,128)(2,1)} %get-tuple-element.43), channel_id=1, source_target_pairs={{0,7},{1,0},{2,1},{3,2},{4,3},{5,4},{6,5},{7,6}} | collective-permute-start | bytes 884744 | tf_op jit(solution)/shard_map/ppermute | solution.py:219
  18.9 0.1 copy.5
  19.0 0.1 fusion.1.offsets
  19.1 0.1 add_convert_fusion.3.flags
  19.2 0.7 collective-permute-start.2
  19.8 2.3 %collective-permute-done = f32[18,128]{1,0:T(8,128)S(1)} collective-permute-done((f32[18,128]{1,0:T(8,128)S(1)}, f32[18,128]{1,0:T(8,128)S(1)}, u32[]{:S(2)}, u32[]{:S(2)}) %collective-permute-start) | collective-permute-done | bytes 9248 | tf_op jit(solution)/shard_map/ppermute | solution.py:230
  22.1 0.7 collective-permute-start.3
  22.8 0.0 copy-start
  22.8 3.4 %copy-done = bf16[1,16,4,256,256]{4,3,2,1,0:T(8,128)(2,1)S(1)} copy-done((bf16[1,16,4,256,256]{4,3,2,1,0:T(8,128)(2,1)S(1)}, bf16[1,16,4,256,256]{4,3,2,1,0:T(8,128)(2,1)}, u32[]{:S(2)}) %copy-start) | copy-done | bytes 8388632
  26.2 2.1 %shard_map.51 = (bf16[32,64,128]{2,1,0:T(8,128)(2,1)}, bf16[18,64,128]{2,1,0:T(8,128)(2,1)}, bf16[18,64,128]{2,1,0:T(8,128)(2,1)}) custom-call(s32[3]{0:T(128)S(1)} %add_convert_fusion.3.flags, s32[16,4]{1,0:T(8,128)S(1)} %fusion.1.offsets, f32[68,128]{1,0:T(8,128)S(1)} %pad_maximum_fusion.1.kappa, f32[32,128,128]{2,1,0:T(8,128)S(1)} %get-tuple-element.29.forcing, ...), custom_call_target="tpu_custom_call" | custom-call | flops 536870912 | bytes 10485760 | tf_op jit(solution)/shard_map/pallas_call | solution.py:183
  28.3 1.6 %collective-permute-start.16 = (bf16[32,64,128]{2,1,0:T(8,128)(2,1)}, bf16[32,64,128]{2,1,0:T(8,128)(2,1)}, u32[]{:S(2)}, u32[]{:S(2)}) collective-permute-start(bf16[32,64,128]{2,1,0:T(8,128)(2,1)} %get-tuple-element.44), channel_id=1, source_target_pairs={{0,8},{1,9},{2,10},{3,11},{4,12},{5,13},{6,14},{7,15}} | collective-permute-start | bytes 1572872 | tf_op jit(solution)/shard_map/ppermute | solution.py:219
  29.9 0.7 collective-permute-start.17
  30.6 1.4 %collective-permute-start.18 = (bf16[18,64,128]{2,1,0:T(8,128)(2,1)}, bf16[18,64,128]{2,1,0:T(8,128)(2,1)}, u32[]{:S(2)}, u32[]{:S(2)}) collective-permute-start(bf16[18,64,128]{2,1,0:T(8,128)(2,1)} %get-tuple-element.46), channel_id=1, source_target_pairs={{0,15},{1,8},{2,9},{3,10},{4,11},{5,12},{6,13},{7,14}} | collective-permute-start | bytes 884744 | tf_op jit(solution)/shard_map/ppermute | solution.py:219
  32.0 1.5 %shard_map.47 = (bf16[32,64,128]{2,1,0:T(8,128)(2,1)}, bf16[18,64,128]{2,1,0:T(8,128)(2,1)S(1)}, bf16[18,64,128]{2,1,0:T(8,128)(2,1)S(1)}) custom-call(s32[3]{0:T(128)S(1)} %add_convert_fusion.3.flags, s32[16,4]{1,0:T(8,128)S(1)} %fusion.1.offsets, f32[68,128]{1,0:T(8,128)S(1)} %pad_maximum_fusion.1.kappa, f32[32,128,128]{2,1,0:T(8,128)S(1)} %get-tuple-element.29.forcing, ...), custom_call_target="tpu_custom_call" | custom-call | flops 536870912 | bytes 10485760 | tf_op jit(solution)/shard_map/pallas_call | solution.py:183
  33.5 0.7 copy-done.9
  34.2 0.7 copy-done.12
  35.0 1.5 %collective-permute-start.5 = (bf16[32,64,128]{2,1,0:T(8,128)(2,1)}, bf16[32,64,128]{2,1,0:T(8,128)(2,1)}, u32[]{:S(2)}, u32[]{:S(2)}) collective-permute-start(bf16[32,64,128]{2,1,0:T(8,128)(2,1)} %get-tuple-element.33), channel_id=1, source_target_pairs={{0,8},{1,9},{2,10},{3,11},{4,12},{5,13},{6,14},{7,15}} | collective-permute-start | bytes 1572872 | tf_op jit(solution)/shard_map/ppermute | solution.py:219
  36.4 0.7 collective-permute-start.6
  37.1 0.1 add_convert_fusion.2.flags
  37.2 0.7 collective-permute-start.7
  37.9 0.0 copy-start.2
  37.9 3.4 %copy-done.2 = bf16[1,16,4,256,256]{4,3,2,1,0:T(8,128)(2,1)S(1)} copy-done((bf16[1,16,4,256,256]{4,3,2,1,0:T(8,128)(2,1)S(1)}, bf16[1,16,4,256,256]{4,3,2,1,0:T(8,128)(2,1)}, u32[]{:S(2)}) %copy-start.2) | copy-done | bytes 8388632
  41.3 2.4 %shard_map.52 = (bf16[32,64,128]{2,1,0:T(8,128)(2,1)}, bf16[18,64,128]{2,1,0:T(8,128)(2,1)}, bf16[18,64,128]{2,1,0:T(8,128)(2,1)}) custom-call(s32[3]{0:T(128)S(1)} %add_convert_fusion.2.flags, s32[16,4]{1,0:T(8,128)S(1)} %fusion.1.offsets, f32[68,128]{1,0:T(8,128)S(1)} %pad_maximum_fusion.1.kappa, f32[32,128,128]{2,1,0:T(8,128)S(1)} %get-tuple-element.29.forcing, ...), custom_call_target="tpu_custom_call" | custom-call | flops 536870912 | bytes 10485760 | tf_op jit(solution)/shard_map/pallas_call | solution.py:183
  43.6 1.5 %collective-permute-start.19 = (bf16[32,64,128]{2,1,0:T(8,128)(2,1)}, bf16[32,64,128]{2,1,0:T(8,128)(2,1)}, u32[]{:S(2)}, u32[]{:S(2)}) collective-permute-start(bf16[32,64,128]{2,1,0:T(8,128)(2,1)} %get-tuple-element.47), channel_id=1, source_target_pairs={{8,16},{9,17},{10,18},{11,19},{12,20},{13,21},{14,22},{15,23}} | collective-permute-start | bytes 1572872 | tf_op jit(solution)/shard_map/ppermute | solution.py:219
  45.1 0.7 collective-permute-start.20
  45.8 1.4 %collective-permute-start.21 = (bf16[18,64,128]{2,1,0:T(8,128)(2,1)}, bf16[18,64,128]{2,1,0:T(8,128)(2,1)}, u32[]{:S(2)}, u32[]{:S(2)}) collective-permute-start(bf16[18,64,128]{2,1,0:T(8,128)(2,1)} %get-tuple-element.49), channel_id=1, source_target_pairs={{8,23},{9,16},{10,17},{11,18},{12,19},{13,20},{14,21},{15,22}} | collective-permute-start | bytes 884744 | tf_op jit(solution)/shard_map/ppermute | solution.py:219
  47.2 1.9 %shard_map.48 = (bf16[32,64,128]{2,1,0:T(8,128)(2,1)}, bf16[18,64,128]{2,1,0:T(8,128)(2,1)S(1)}, bf16[18,64,128]{2,1,0:T(8,128)(2,1)S(1)}) custom-call(s32[3]{0:T(128)S(1)} %add_convert_fusion.2.flags, s32[16,4]{1,0:T(8,128)S(1)} %fusion.1.offsets, f32[68,128]{1,0:T(8,128)S(1)} %pad_maximum_fusion.1.kappa, f32[32,128,128]{2,1,0:T(8,128)S(1)} %get-tuple-element.29.forcing, ...), custom_call_target="tpu_custom_call" | custom-call | flops 536870912 | bytes 10485760 | tf_op jit(solution)/shard_map/pallas_call | solution.py:183
  49.1 0.7 copy-done.8
  49.8 0.7 copy-done.11
  50.5 1.5 %collective-permute-start.8 = (bf16[32,64,128]{2,1,0:T(8,128)(2,1)}, bf16[32,64,128]{2,1,0:T(8,128)(2,1)}, u32[]{:S(2)}, u32[]{:S(2)}) collective-permute-start(bf16[32,64,128]{2,1,0:T(8,128)(2,1)} %get-tuple-element.36), channel_id=1, source_target_pairs={{8,16},{9,17},{10,18},{11,19},{12,20},{13,21},{14,22},{15,23}} | collective-permute-start | bytes 1572872 | tf_op jit(solution)/shard_map/ppermute | solution.py:219
  52.0 0.7 collective-permute-start.9
  52.7 0.1 add_convert_fusion.1.flags
  52.7 0.7 collective-permute-start.10
  53.4 0.0 copy-start.3
  53.5 3.4 %copy-done.3 = bf16[1,16,4,256,256]{4,3,2,1,0:T(8,128)(2,1)S(1)} copy-done((bf16[1,16,4,256,256]{4,3,2,1,0:T(8,128)(2,1)S(1)}, bf16[1,16,4,256,256]{4,3,2,1,0:T(8,128)(2,1)}, u32[]{:S(2)}) %copy-start.3) | copy-done | bytes 8388632
  56.8 2.1 %shard_map.53 = (bf16[32,64,128]{2,1,0:T(8,128)(2,1)}, bf16[18,64,128]{2,1,0:T(8,128)(2,1)}, bf16[18,64,128]{2,1,0:T(8,128)(2,1)}) custom-call(s32[3]{0:T(128)S(1)} %add_convert_fusion.1.flags, s32[16,4]{1,0:T(8,128)S(1)} %fusion.1.offsets, f32[68,128]{1,0:T(8,128)S(1)} %pad_maximum_fusion.1.kappa, f32[32,128,128]{2,1,0:T(8,128)S(1)} %get-tuple-element.29.forcing, ...), custom_call_target="tpu_custom_call" | custom-call | flops 536870912 | bytes 10485760 | tf_op jit(solution)/shard_map/pallas_call | solution.py:183
  59.0 1.3 %collective-permute-start.22 = (bf16[32,64,128]{2,1,0:T(8,128)(2,1)}, bf16[32,64,128]{2,1,0:T(8,128)(2,1)}, u32[]{:S(2)}, u32[]{:S(2)}) collective-permute-start(bf16[32,64,128]{2,1,0:T(8,128)(2,1)} %get-tuple-element.50), channel_id=1, source_target_pairs={{16,24},{17,25},{18,26},{19,27},{20,28},{21,29},{22,30},{23,31}} | collective-permute-start | bytes 1572872 | tf_op jit(solution)/shard_map/ppermute | solution.py:219
  60.2 1.3 %collective-permute-start.23 = (bf16[18,64,128]{2,1,0:T(8,128)(2,1)}, bf16[18,64,128]{2,1,0:T(8,128)(2,1)S(1)}, u32[]{:S(2)}, u32[]{:S(2)}) collective-permute-start(bf16[18,64,128]{2,1,0:T(8,128)(2,1)} %get-tuple-element.51), channel_id=1, source_target_pairs={{16,25},{17,26},{18,27},{19,28},{20,29},{21,30},{22,31},{23,24}} | collective-permute-start | bytes 884744 | tf_op jit(solution)/shard_map/ppermute | solution.py:219
  61.6 1.3 %collective-permute-start.24 = (bf16[18,64,128]{2,1,0:T(8,128)(2,1)}, bf16[18,64,128]{2,1,0:T(8,128)(2,1)}, u32[]{:S(2)}, u32[]{:S(2)}) collective-permute-start(bf16[18,64,128]{2,1,0:T(8,128)(2,1)} %get-tuple-element.52), channel_id=1, source_target_pairs={{16,31},{17,24},{18,25},{19,26},{20,27},{21,28},{22,29},{23,30}} | collective-permute-start | bytes 884744 | tf_op jit(solution)/shard_map/ppermute | solution.py:219
  62.9 1.9 %shard_map.49 = (bf16[32,64,128]{2,1,0:T(8,128)(2,1)}, bf16[18,64,128]{2,1,0:T(8,128)(2,1)S(1)}, bf16[18,64,128]{2,1,0:T(8,128)(2,1)S(1)}) custom-call(s32[3]{0:T(128)S(1)} %add_convert_fusion.1.flags, s32[16,4]{1,0:T(8,128)S(1)} %fusion.1.offsets, f32[68,128]{1,0:T(8,128)S(1)} %pad_maximum_fusion.1.kappa, f32[32,128,128]{2,1,0:T(8,128)S(1)} %get-tuple-element.29.forcing, ...), custom_call_target="tpu_custom_call" | custom-call | flops 536870912 | bytes 10485760 | tf_op jit(solution)/shard_map/pallas_call | solution.py:183
  64.8 0.7 copy-done.10
  65.5 0.7 copy-done.13
  66.2 1.3 %collective-permute-start.11 = (bf16[32,64,128]{2,1,0:T(8,128)(2,1)}, bf16[32,64,128]{2,1,0:T(8,128)(2,1)S(1)}, u32[]{:S(2)}, u32[]{:S(2)}) collective-permute-start(bf16[32,64,128]{2,1,0:T(8,128)(2,1)} %get-tuple-element.39), channel_id=1, source_target_pairs={{16,24},{17,25},{18,26},{19,27},{20,28},{21,29},{22,30},{23,31}} | collective-permute-start | bytes 1572872 | tf_op jit(solution)/shard_map/ppermute | solution.py:219
  67.5 0.1 add_convert_fusion.flags
  67.6 1.5 %collective-permute-start.12 = (bf16[18,64,128]{2,1,0:T(8,128)(2,1)}, bf16[18,64,128]{2,1,0:T(8,128)(2,1)S(1)}, u32[]{:S(2)}, u32[]{:S(2)}) collective-permute-start(bf16[18,64,128]{2,1,0:T(8,128)(2,1)} %copy-done.13), channel_id=1, source_target_pairs={{16,25},{17,26},{18,27},{19,28},{20,29},{21,30},{22,31},{23,24}} | collective-permute-start | bytes 884744 | tf_op jit(solution)/shard_map/ppermute | solution.py:219
  69.1 30.7 %collective-permute-done.23.refs_1_ = bf16[18,64,128]{2,1,0:T(8,128)(2,1)S(1)} collective-permute-done((bf16[18,64,128]{2,1,0:T(8,128)(2,1)}, bf16[18,64,128]{2,1,0:T(8,128)(2,1)S(1)}, u32[]{:S(2)}, u32[]{:S(2)}) %collective-permute-start.23) | collective-permute-done | bytes 294944 | tf_op jit(solution)/shard_map/ppermute | solution.py:219
  99.8 1.3 %collective-permute-start.13 = (bf16[18,64,128]{2,1,0:T(8,128)(2,1)}, bf16[18,64,128]{2,1,0:T(8,128)(2,1)S(1)}, u32[]{:S(2)}, u32[]{:S(2)}) collective-permute-start(bf16[18,64,128]{2,1,0:T(8,128)(2,1)} %copy-done.10), channel_id=1, source_target_pairs={{16,31},{17,24},{18,25},{19,26},{20,27},{21,28},{22,29},{23,30}} | collective-permute-start | bytes 884744 | tf_op jit(solution)/shard_map/ppermute | solution.py:219
  101.1 1.9 %collective-permute-done.24.refs_2_ = bf16[18,64,128]{2,1,0:T(8,128)(2,1)} collective-permute-done((bf16[18,64,128]{2,1,0:T(8,128)(2,1)}, bf16[18,64,128]{2,1,0:T(8,128)(2,1)}, u32[]{:S(2)}, u32[]{:S(2)}) %collective-permute-start.24) | collective-permute-done | bytes 294944 | tf_op jit(solution)/shard_map/ppermute | solution.py:219
  103.0 3.4 %copy-done.4 = bf16[1,16,4,256,256]{4,3,2,1,0:T(8,128)(2,1)S(1)} copy-done((bf16[1,16,4,256,256]{4,3,2,1,0:T(8,128)(2,1)S(1)}, bf16[1,16,4,256,256]{4,3,2,1,0:T(8,128)(2,1)}, u32[]{:S(2)}) %copy-start.4) | copy-done | bytes 8388632
  106.4 5.6 %shard_map.54 = bf16[32,64,128]{2,1,0:T(8,128)(2,1)S(1)} custom-call(s32[3]{0:T(128)S(1)} %add_convert_fusion.flags, s32[16,4]{1,0:T(8,128)S(1)} %fusion.1.offsets, f32[68,128]{1,0:T(8,128)S(1)} %pad_maximum_fusion.1.kappa, f32[32,128,128]{2,1,0:T(8,128)S(1)} %get-tuple-element.29.forcing, bf16[32,64,128]{2,1,0:T(8,128)(2,1)} %collective-permute-done.22.refs_0_, ...), custom_call_target="tpu_custom_call" | custom-call | flops 536870912 | bytes 10485760 | tf_op jit(solution)/shard_map/pallas_call | solution.py:183
  111.9 1.2 select_select_fusion
  113.2 2.2 %collective-permute-done.13.refs_2_ = bf16[18,64,128]{2,1,0:T(8,128)(2,1)S(1)} collective-permute-done((bf16[18,64,128]{2,1,0:T(8,128)(2,1)}, bf16[18,64,128]{2,1,0:T(8,128)(2,1)S(1)}, u32[]{:S(2)}, u32[]{:S(2)}) %collective-permute-start.13) | collective-permute-done | bytes 294944 | tf_op jit(solution)/shard_map/ppermute | solution.py:219
  115.4 5.1 %shard_map.50 = bf16[32,64,128]{2,1,0:T(8,128)(2,1)S(1)} custom-call(s32[3]{0:T(128)S(1)} %add_convert_fusion.flags, s32[16,4]{1,0:T(8,128)S(1)} %fusion.1.offsets, f32[68,128]{1,0:T(8,128)S(1)} %pad_maximum_fusion.1.kappa, f32[32,128,128]{2,1,0:T(8,128)S(1)} %get-tuple-element.29.forcing, bf16[32,64,128]{2,1,0:T(8,128)(2,1)S(1)} %collective-permute-done.11.refs_0_, ...), custom_call_target="tpu_custom_call" | custom-call | flops 536870912 | bytes 10485760 | tf_op jit(solution)/shard_map/pallas_call | solution.py:183
  120.5 1.2 select_select_fusion.1
  121.7 0.1 pad_maximum_fusion
  121.8 1.6 %copy.6 = bf16[1,8,16,32,128]{4,3,2,1,0:T(8,128)(2,1)} copy(bf16[1,8,16,32,128]{4,2,1,3,0:T(8,128)(2,1)S(1)} %bitcast.26) | data formatting | bytes 2097152 | tf_op jit(solution)/shard_map/reshape | solution.py:254
  (40 shorter events, 0.1 us)
Async XLA Ops:
  0.0 1.6 %copy-start.5 = (f32[1,8,16,32,128]{4,3,2,1,0:T(8,128)S(1)}, f32[1,8,16,32,128]{4,3,2,1,0:T(8,128)}, u32[]{:S(2)}) copy-start(f32[1,8,16,32,128]{4,3,2,1,0:T(8,128)} %param.4) | copy-start | bytes 6291460
  1.6 10.9 %copy-start.14 = (f32[1,32,128]{2,1,0:T(8,128)S(1)}, f32[1,32,128]{2,1,0:T(8,128)}, u32[]{:S(2)}) copy-start(f32[1,32,128]{2,1,0:T(8,128)} %param.5) | copy-start | bytes 49156
  1.6 17.3 %copy-start.15 = (s32[1,16,4]{1,2,0:T(4,128)S(1)}, s32[1,16,4]{1,2,0:T(4,128)}, u32[]{:S(2)}) copy-start(s32[1,16,4]{1,2,0:T(4,128)} %param.6) | copy-start | bytes 772
  8.4 0.7 copy-start.6
  9.1 0.7 copy-start.7
  9.9 13.0 %collective-permute-start.4 = (bf16[32,128,128]{2,1,0:T(8,128)(2,1)}, bf16[32,128,128]{2,1,0:T(8,128)(2,1)S(1)}, u32[]{:S(2)}, u32[]{:S(2)}) collective-permute-start(bf16[32,128,128]{2,1,0:T(8,128)(2,1)} %get-tuple-element.32), channel_id=1, source_target_pairs={{8,0},{9,1},{10,2},{11,3},{12,4},{13,5},{14,6},{15,7},{16,8},{17,9... | collective-permute-start | bytes 3145736 | tf_op jit(solution)/shard_map/ppermute | solution.py:234
  12.5 6.6 %collective-permute-start.1 = (f32[18,128]{1,0:T(8,128)S(1)}, f32[18,128]{1,0:T(8,128)S(1)}, u32[]{:S(2)}, u32[]{:S(2)}) collective-permute-start(f32[18,128]{1,0:T(8,128)S(1)} %get-tuple-element.54), channel_id=1, source_target_pairs={{1,0},{2,1},{3,2},{4,3},{5,4},{6,5},{7,6},{0,7},{9,8},{10,9},{11,1... | collective-permute-start | bytes 27656 | tf_op jit(solution)/shard_map/ppermute | solution.py:232
  16.8 5.2 %collective-permute-start = (f32[18,128]{1,0:T(8,128)S(1)}, f32[18,128]{1,0:T(8,128)S(1)}, u32[]{:S(2)}, u32[]{:S(2)}) collective-permute-start(f32[18,128]{1,0:T(8,128)S(1)} %get-tuple-element.53), channel_id=1, source_target_pairs={{0,1},{1,2},{2,3},{3,4},{4,5},{5,6},{6,7},{7,0},{8,9},{9,10},{10,1... | collective-permute-start | bytes 27656 | tf_op jit(solution)/shard_map/ppermute | solution.py:230
  16.9 5.9 %collective-permute-start.14 = (bf16[18,64,128]{2,1,0:T(8,128)(2,1)}, bf16[18,64,128]{2,1,0:T(8,128)(2,1)S(1)}, u32[]{:S(2)}, u32[]{:S(2)}) collective-permute-start(bf16[18,64,128]{2,1,0:T(8,128)(2,1)} %get-tuple-element.42), channel_id=1, source_target_pairs={{0,1},{1,2},{2,3},{3,4},{4,5},{5,6},{6,7},{7,0}} | collective-permute-start | bytes 884744 | tf_op jit(solution)/shard_map/ppermute | solution.py:219
  17.5 5.3 %collective-permute-start.15 = (bf16[18,64,128]{2,1,0:T(8,128)(2,1)}, bf16[18,64,128]{2,1,0:T(8,128)(2,1)}, u32[]{:S(2)}, u32[]{:S(2)}) collective-permute-start(bf16[18,64,128]{2,1,0:T(8,128)(2,1)} %get-tuple-element.43), channel_id=1, source_target_pairs={{0,7},{1,0},{2,1},{3,2},{4,3},{5,4},{6,5},{7,6}} | collective-permute-start | bytes 884744 | tf_op jit(solution)/shard_map/ppermute | solution.py:219
  19.2 12.9 %collective-permute-start.2 = (bf16[18,64,128]{2,1,0:T(8,128)(2,1)}, bf16[18,64,128]{2,1,0:T(8,128)(2,1)S(1)}, u32[]{:S(2)}, u32[]{:S(2)}) collective-permute-start(bf16[18,64,128]{2,1,0:T(8,128)(2,1)} %copy-done.7), channel_id=1, source_target_pairs={{0,1},{1,2},{2,3},{3,4},{4,5},{5,6},{6,7},{7,0}} | collective-permute-start | bytes 884744 | tf_op jit(solution)/shard_map/ppermute | solution.py:219
  22.1 9.9 %collective-permute-start.3 = (bf16[18,64,128]{2,1,0:T(8,128)(2,1)}, bf16[18,64,128]{2,1,0:T(8,128)(2,1)S(1)}, u32[]{:S(2)}, u32[]{:S(2)}) collective-permute-start(bf16[18,64,128]{2,1,0:T(8,128)(2,1)} %copy-done.6), channel_id=1, source_target_pairs={{0,7},{1,0},{2,1},{3,2},{4,3},{5,4},{6,5},{7,6}} | collective-permute-start | bytes 884744 | tf_op jit(solution)/shard_map/ppermute | solution.py:219
  22.8 3.4 %copy-start = (bf16[1,16,4,256,256]{4,3,2,1,0:T(8,128)(2,1)S(1)}, bf16[1,16,4,256,256]{4,3,2,1,0:T(8,128)(2,1)}, u32[]{:S(2)}) copy-start(bf16[1,16,4,256,256]{4,3,2,1,0:T(8,128)(2,1)} %param.7) | copy-start | bytes 25165828
  26.2 5.8 %copy-start.1 = (bf16[1,16,4,256,256]{4,3,2,1,0:T(8,128)(2,1)S(1)}, bf16[1,16,4,256,256]{4,3,2,1,0:T(8,128)(2,1)}, u32[]{:S(2)}) copy-start(bf16[1,16,4,256,256]{4,3,2,1,0:T(8,128)(2,1)} %param.7) | copy-start | bytes 25165828
  28.3 9.6 %collective-permute-start.16 = (bf16[32,64,128]{2,1,0:T(8,128)(2,1)}, bf16[32,64,128]{2,1,0:T(8,128)(2,1)}, u32[]{:S(2)}, u32[]{:S(2)}) collective-permute-start(bf16[32,64,128]{2,1,0:T(8,128)(2,1)} %get-tuple-element.44), channel_id=1, source_target_pairs={{0,8},{1,9},{2,10},{3,11},{4,12},{5,13},{6,14},{7,15}} | collective-permute-start | bytes 1572872 | tf_op jit(solution)/shard_map/ppermute | solution.py:219
  29.9 7.3 %collective-permute-start.17 = (bf16[18,64,128]{2,1,0:T(8,128)(2,1)}, bf16[18,64,128]{2,1,0:T(8,128)(2,1)S(1)}, u32[]{:S(2)}, u32[]{:S(2)}) collective-permute-start(bf16[18,64,128]{2,1,0:T(8,128)(2,1)} %get-tuple-element.45), channel_id=1, source_target_pairs={{0,9},{1,10},{2,11},{3,12},{4,13},{5,14},{6,15},{7,8}} | collective-permute-start | bytes 884744 | tf_op jit(solution)/shard_map/ppermute | solution.py:219
  30.6 7.3 %collective-permute-start.18 = (bf16[18,64,128]{2,1,0:T(8,128)(2,1)}, bf16[18,64,128]{2,1,0:T(8,128)(2,1)}, u32[]{:S(2)}, u32[]{:S(2)}) collective-permute-start(bf16[18,64,128]{2,1,0:T(8,128)(2,1)} %get-tuple-element.46), channel_id=1, source_target_pairs={{0,15},{1,8},{2,9},{3,10},{4,11},{5,12},{6,13},{7,14}} | collective-permute-start | bytes 884744 | tf_op jit(solution)/shard_map/ppermute | solution.py:219
  33.5 0.7 copy-start.9
  34.2 0.7 copy-start.12
  35.0 12.2 %collective-permute-start.5 = (bf16[32,64,128]{2,1,0:T(8,128)(2,1)}, bf16[32,64,128]{2,1,0:T(8,128)(2,1)}, u32[]{:S(2)}, u32[]{:S(2)}) collective-permute-start(bf16[32,64,128]{2,1,0:T(8,128)(2,1)} %get-tuple-element.33), channel_id=1, source_target_pairs={{0,8},{1,9},{2,10},{3,11},{4,12},{5,13},{6,14},{7,15}} | collective-permute-start | bytes 1572872 | tf_op jit(solution)/shard_map/ppermute | solution.py:219
  36.4 9.3 %collective-permute-start.6 = (bf16[18,64,128]{2,1,0:T(8,128)(2,1)}, bf16[18,64,128]{2,1,0:T(8,128)(2,1)S(1)}, u32[]{:S(2)}, u32[]{:S(2)}) collective-permute-start(bf16[18,64,128]{2,1,0:T(8,128)(2,1)} %copy-done.12), channel_id=1, source_target_pairs={{0,9},{1,10},{2,11},{3,12},{4,13},{5,14},{6,15},{7,8}} | collective-permute-start | bytes 884744 | tf_op jit(solution)/shard_map/ppermute | solution.py:219
  37.2 10.0 %collective-permute-start.7 = (bf16[18,64,128]{2,1,0:T(8,128)(2,1)}, bf16[18,64,128]{2,1,0:T(8,128)(2,1)S(1)}, u32[]{:S(2)}, u32[]{:S(2)}) collective-permute-start(bf16[18,64,128]{2,1,0:T(8,128)(2,1)} %copy-done.9), channel_id=1, source_target_pairs={{0,15},{1,8},{2,9},{3,10},{4,11},{5,12},{6,13},{7,14}} | collective-permute-start | bytes 884744 | tf_op jit(solution)/shard_map/ppermute | solution.py:219
  37.9 3.4 %copy-start.2 = (bf16[1,16,4,256,256]{4,3,2,1,0:T(8,128)(2,1)S(1)}, bf16[1,16,4,256,256]{4,3,2,1,0:T(8,128)(2,1)}, u32[]{:S(2)}) copy-start(bf16[1,16,4,256,256]{4,3,2,1,0:T(8,128)(2,1)} %param.7) | copy-start | bytes 25165828
  43.6 9.8 %collective-permute-start.19 = (bf16[32,64,128]{2,1,0:T(8,128)(2,1)}, bf16[32,64,128]{2,1,0:T(8,128)(2,1)}, u32[]{:S(2)}, u32[]{:S(2)}) collective-permute-start(bf16[32,64,128]{2,1,0:T(8,128)(2,1)} %get-tuple-element.47), channel_id=1, source_target_pairs={{8,16},{9,17},{10,18},{11,19},{12,20},{13,21},{14,22},{15,23}} | collective-permute-start | bytes 1572872 | tf_op jit(solution)/shard_map/ppermute | solution.py:219
  45.1 7.7 %collective-permute-start.20 = (bf16[18,64,128]{2,1,0:T(8,128)(2,1)}, bf16[18,64,128]{2,1,0:T(8,128)(2,1)S(1)}, u32[]{:S(2)}, u32[]{:S(2)}) collective-permute-start(bf16[18,64,128]{2,1,0:T(8,128)(2,1)} %get-tuple-element.48), channel_id=1, source_target_pairs={{8,17},{9,18},{10,19},{11,20},{12,21},{13,22},{14,23},{15,16}} | collective-permute-start | bytes 884744 | tf_op jit(solution)/shard_map/ppermute | solution.py:219
  45.8 7.6 %collective-permute-start.21 = (bf16[18,64,128]{2,1,0:T(8,128)(2,1)}, bf16[18,64,128]{2,1,0:T(8,128)(2,1)}, u32[]{:S(2)}, u32[]{:S(2)}) collective-permute-start(bf16[18,64,128]{2,1,0:T(8,128)(2,1)} %get-tuple-element.49), channel_id=1, source_target_pairs={{8,23},{9,16},{10,17},{11,18},{12,19},{13,20},{14,21},{15,22}} | collective-permute-start | bytes 884744 | tf_op jit(solution)/shard_map/ppermute | solution.py:219
  49.1 0.7 copy-start.8
  49.8 0.7 copy-start.11
  50.5 12.3 %collective-permute-start.8 = (bf16[32,64,128]{2,1,0:T(8,128)(2,1)}, bf16[32,64,128]{2,1,0:T(8,128)(2,1)}, u32[]{:S(2)}, u32[]{:S(2)}) collective-permute-start(bf16[32,64,128]{2,1,0:T(8,128)(2,1)} %get-tuple-element.36), channel_id=1, source_target_pairs={{8,16},{9,17},{10,18},{11,19},{12,20},{13,21},{14,22},{15,23}} | collective-permute-start | bytes 1572872 | tf_op jit(solution)/shard_map/ppermute | solution.py:219
  52.0 9.6 %collective-permute-start.9 = (bf16[18,64,128]{2,1,0:T(8,128)(2,1)}, bf16[18,64,128]{2,1,0:T(8,128)(2,1)S(1)}, u32[]{:S(2)}, u32[]{:S(2)}) collective-permute-start(bf16[18,64,128]{2,1,0:T(8,128)(2,1)} %copy-done.11), channel_id=1, source_target_pairs={{8,17},{9,18},{10,19},{11,20},{12,21},{13,22},{14,23},{15,16}} | collective-permute-start | bytes 884744 | tf_op jit(solution)/shard_map/ppermute | solution.py:219
  52.7 10.1 %collective-permute-start.10 = (bf16[18,64,128]{2,1,0:T(8,128)(2,1)}, bf16[18,64,128]{2,1,0:T(8,128)(2,1)S(1)}, u32[]{:S(2)}, u32[]{:S(2)}) collective-permute-start(bf16[18,64,128]{2,1,0:T(8,128)(2,1)} %copy-done.8), channel_id=1, source_target_pairs={{8,23},{9,16},{10,17},{11,18},{12,19},{13,20},{14,21},{15,22}} | collective-permute-start | bytes 884744 | tf_op jit(solution)/shard_map/ppermute | solution.py:219
  53.4 3.4 %copy-start.3 = (bf16[1,16,4,256,256]{4,3,2,1,0:T(8,128)(2,1)S(1)}, bf16[1,16,4,256,256]{4,3,2,1,0:T(8,128)(2,1)}, u32[]{:S(2)}) copy-start(bf16[1,16,4,256,256]{4,3,2,1,0:T(8,128)(2,1)} %param.7) | copy-start | bytes 25165828
  59.0 44.0 %collective-permute-start.22 = (bf16[32,64,128]{2,1,0:T(8,128)(2,1)}, bf16[32,64,128]{2,1,0:T(8,128)(2,1)}, u32[]{:S(2)}, u32[]{:S(2)}) collective-permute-start(bf16[32,64,128]{2,1,0:T(8,128)(2,1)} %get-tuple-element.50), channel_id=1, source_target_pairs={{16,24},{17,25},{18,26},{19,27},{20,28},{21,29},{22,30},{23,31}} | collective-permute-start | bytes 1572872 | tf_op jit(solution)/shard_map/ppermute | solution.py:219
  60.2 39.6 %collective-permute-start.23 = (bf16[18,64,128]{2,1,0:T(8,128)(2,1)}, bf16[18,64,128]{2,1,0:T(8,128)(2,1)S(1)}, u32[]{:S(2)}, u32[]{:S(2)}) collective-permute-start(bf16[18,64,128]{2,1,0:T(8,128)(2,1)} %get-tuple-element.51), channel_id=1, source_target_pairs={{16,25},{17,26},{18,27},{19,28},{20,29},{21,30},{22,31},{23,24}} | collective-permute-start | bytes 884744 | tf_op jit(solution)/shard_map/ppermute | solution.py:219
  61.6 41.4 %collective-permute-start.24 = (bf16[18,64,128]{2,1,0:T(8,128)(2,1)}, bf16[18,64,128]{2,1,0:T(8,128)(2,1)}, u32[]{:S(2)}, u32[]{:S(2)}) collective-permute-start(bf16[18,64,128]{2,1,0:T(8,128)(2,1)} %get-tuple-element.52), channel_id=1, source_target_pairs={{16,31},{17,24},{18,25},{19,26},{20,27},{21,28},{22,29},{23,30}} | collective-permute-start | bytes 884744 | tf_op jit(solution)/shard_map/ppermute | solution.py:219
  64.8 0.7 copy-start.10
  65.5 0.7 copy-start.13
  66.2 49.2 %collective-permute-start.11 = (bf16[32,64,128]{2,1,0:T(8,128)(2,1)}, bf16[32,64,128]{2,1,0:T(8,128)(2,1)S(1)}, u32[]{:S(2)}, u32[]{:S(2)}) collective-permute-start(bf16[32,64,128]{2,1,0:T(8,128)(2,1)} %get-tuple-element.39), channel_id=1, source_target_pairs={{16,24},{17,25},{18,26},{19,27},{20,28},{21,29},{22,30},{23,31}} | collective-permute-start | bytes 1572872 | tf_op jit(solution)/shard_map/ppermute | solution.py:219
  67.6 45.6 %collective-permute-start.12 = (bf16[18,64,128]{2,1,0:T(8,128)(2,1)}, bf16[18,64,128]{2,1,0:T(8,128)(2,1)S(1)}, u32[]{:S(2)}, u32[]{:S(2)}) collective-permute-start(bf16[18,64,128]{2,1,0:T(8,128)(2,1)} %copy-done.13), channel_id=1, source_target_pairs={{16,25},{17,26},{18,27},{19,28},{20,29},{21,30},{22,31},{23,24}} | collective-permute-start | bytes 884744 | tf_op jit(solution)/shard_map/ppermute | solution.py:219
  99.8 15.6 %collective-permute-start.13 = (bf16[18,64,128]{2,1,0:T(8,128)(2,1)}, bf16[18,64,128]{2,1,0:T(8,128)(2,1)S(1)}, u32[]{:S(2)}, u32[]{:S(2)}) collective-permute-start(bf16[18,64,128]{2,1,0:T(8,128)(2,1)} %copy-done.10), channel_id=1, source_target_pairs={{16,31},{17,24},{18,25},{19,26},{20,27},{21,28},{22,29},{23,30}} | collective-permute-start | bytes 884744 | tf_op jit(solution)/shard_map/ppermute | solution.py:219
  103.0 3.4 %copy-start.4 = (bf16[1,16,4,256,256]{4,3,2,1,0:T(8,128)(2,1)S(1)}, bf16[1,16,4,256,256]{4,3,2,1,0:T(8,128)(2,1)}, u32[]{:S(2)}) copy-start(bf16[1,16,4,256,256]{4,3,2,1,0:T(8,128)(2,1)} %param.7) | copy-start | bytes 25165828
where the time goes:
time: 124 us; the launch traced here: 123 us
  waiting for transfers between devices  37.2 us (30%)
  starting transfers between devices  31.1 us (25%)
  Pallas kernels  29.3 us (24%)
  local copies, waits for them, and re-layouts  22.6 us (18%)
  other arithmetic  2.93 us (2%)
    ppermute x22, waiting for transfers between devices, send(): lax.ppermute(value, AXES, [(place(source, t), place(target, t + shift)) f...  34.9 us
    ppermute x22, starting transfers between devices, send(): lax.ppermute(value, AXES, [(place(source, t), place(target, t + shift)) f...  24.1 us
    pallas_call x8, Pallas kernels, section(): pl.pallas_call(functools.partial(section_kernel, chunk, has_incoming, has...  22.5 us
    unnamed x32, local copies, waits for them, and re-layouts  20.9 us
    pallas_call x1, Pallas kernels, prepare(): pl.pallas_call(prepare_kernel, in_specs=[HBM], out_shape=[jax.ShapeDtypeS...  6.82 us
    ppermute x1, starting transfers between devices, local(): lax.ppermute(k_here[:halo], 'tile', back)  4.33 us
    ppermute x1, starting transfers between devices, local(): lax.ppermute(narrow, AXES, [(place(s, t), place(s - 1, t)) for s in range...  2.63 us
  transfers between devices with their start and end apart: 25, of which 4 were waited for; matrix products, arithmetic and copies ran while one was open for 1% of the time, Pallas kernels for 14%

commit v1 on v0

v1 whole, which is shorter than its diff:
```python
import functools

import jax
import jax.numpy as jnp
from jax import lax
from jax.experimental import pallas as pl
from jax.experimental.pallas import tpu as pltpu
from jax.sharding import PartitionSpec as P

AXES = ("comp", "tile")
CHUNKS = 2
EDGE = 2
LIMIT = 24 << 20
FLOPS = 20
HBM = pl.BlockSpec(memory_space=pltpu.HBM)
VMEM = pl.BlockSpec(memory_space=pltpu.VMEM)
ANY = pl.BlockSpec(memory_space=pl.ANY)
SMEM = pl.BlockSpec(memory_space=pltpu.SMEM)


def start_all(copies):
    for copy in copies:
        copy.start()


def wait_all(copies):
    for copy in copies:
        copy.wait()


def turn(forcing, f_v, sems, use):
    rows = f_v.shape[1]
    step = rows // sems.shape[0]
    loads = []
    for i in range(sems.shape[0]):
        part = pl.ds(i * step, step)
        loads.append(pltpu.make_async_copy(forcing.at[:, part], f_v.at[:, part], sems.at[i]))
    start_all(loads)
    for i, load in enumerate(loads):
        load.wait()
        use(i * step, jnp.swapaxes(f_v[:, i * step:(i + 1) * step, :], 0, 1))


def prepare_kernel(forcing, kappa, narrow, *refs):
    edges, (f_v, n_v, k_v, pack_v, pack, sems, out_sems) = refs[:-7], refs[-7:]
    total, rows, cells = f_v.shape
    halo, fields = edges[0].shape[0] - 1, edges[0].shape[1]

    def use(start, part):
        n_v[start:start + part.shape[0]] = part.astype(jnp.bfloat16)

    fetch = pltpu.make_async_copy(kappa, k_v, out_sems.at[0])
    fetch.start()
    turn(forcing, f_v, sems, use)
    fetch.wait()
    stores = []
    for c in range(len(edges) // 2):
        mine = pl.ds(c * fields, fields)
        for e, start in enumerate((0, rows - halo)):
            edge = edges[2 * c + e]
            stores.append((n_v.at[pl.ds(start, halo), mine], edge.at[pl.ds(0, halo)]))
            stores.append((pack.at[e, pl.ds(0, fields)], edge.at[halo]))
    stores.append((n_v, narrow.at[pl.ds(0, rows)]))
    stores.append((pack.at[2], narrow.at[rows]))
    stores = [pltpu.make_async_copy(*pair, out_sems.at[i]) for i, pair in enumerate(stores)]
    start_all(stores[0::2])
    parts = split(k_v[...])
    for e, (start, stop) in enumerate(((0, halo), (rows - halo, rows), (0, rows))):
        pack[e] = joined([part[start:stop] for part in parts], pack_v)
    start_all(stores[1::2])
    wait_all(stores)


def split(value):
    parts = []
    for _ in range(3):
        head = value.astype(jnp.bfloat16).astype(jnp.float32)
        parts.append(head)
        value = value - head
    return parts


def joined(parts, room):
    room[...] = jnp.zeros(room.shape, jnp.float32)
    at = 0
    for part in parts:
        room[at:at + part.shape[0], :] = part
        at += part.shape[0]
    return room[...].astype(jnp.bfloat16)


def prepare(fields, kappa, halo):
    total, rows, cells = fields.shape
    n = total // CHUNKS
    edge = pltpu.HBM((halo + 1, n, cells), jnp.bfloat16)
    return pl.pallas_call(
        prepare_kernel,
        in_specs=[HBM, HBM],
        out_shape=[pltpu.HBM((rows + 1, total, cells), jnp.bfloat16)] + [edge] * (2 * CHUNKS),
        out_specs=[HBM] * (1 + 2 * CHUNKS),
        scratch_shapes=[
            pltpu.VMEM((total, rows, cells), jnp.float32),
            pltpu.VMEM((rows, total, cells), jnp.bfloat16),
            pltpu.VMEM(kappa.shape, kappa.dtype),
            pltpu.VMEM((total, cells), jnp.float32),
            pltpu.VMEM((3, total, cells), jnp.bfloat16),
            pltpu.SemaphoreType.DMA((rows // 8,)),
            pltpu.SemaphoreType.DMA((2 + 4 * CHUNKS,)),
        ],
        compiler_params=pltpu.CompilerParams(vmem_limit_bytes=LIMIT),
        cost_estimate=pl.CostEstimate(flops=0, bytes_accessed=fields.size * 12, transcendentals=0),
    )(*(pltpu.with_memory_space_constraint(value, pltpu.HBM) for value in (fields, kappa)))


def load_kernel(weights, forcing, *refs):
    held, by_row, f_v, sems, sem = refs[-5:]
    copy = pltpu.make_async_copy(weights, held, sem)

    def use(start, part):
        by_row[start:start + part.shape[0]] = part
        if start == 0:
            copy.start()

    turn(forcing, f_v, sems, use)
    copy.wait()


def load(weights, fields, after):
    total, rows, cells = fields.shape
    return pl.pallas_call(
        load_kernel,
        in_specs=[HBM] * 2 + [ANY] * len(after),
        out_shape=[pltpu.VMEM(weights.shape, weights.dtype), pltpu.VMEM((rows, total, cells), fields.dtype)],
        out_specs=[VMEM, VMEM],
        scratch_shapes=[
            pltpu.VMEM((total, rows, cells), jnp.float32),
            pltpu.SemaphoreType.DMA((rows // 8,)),
            pltpu.SemaphoreType.DMA,
        ],
        compiler_params=pltpu.CompilerParams(vmem_limit_bytes=LIMIT),
        cost_estimate=pl.CostEstimate(flops=0, bytes_accessed=weights.size * 4, transcendentals=0),
    )(*(pltpu.with_memory_space_constraint(value, pltpu.HBM) for value in (weights, fields)), *after)


def beside_matrix(cells):
    source = lax.broadcasted_iota(jnp.int32, (2 * cells, 2 * cells), 0)
    target = lax.broadcasted_iota(jnp.int32, (2 * cells, 2 * cells), 1)
    apart = (source - target + 2 * cells) % cells
    same = (source < cells) == (target < cells)
    return jnp.where(same & ((apart == 1) | (apart == cells - 1)), 1.0, 0.0).astype(jnp.bfloat16)


def section_kernel(number, chunk, halo, has_incoming, has_next, hands_on, n_saved, flags, offsets, kappa, forcing, *refs):
    refs = list(refs)
    incoming = refs.pop(0) if has_incoming else None
    upper, lower = refs.pop(0), refs.pop(0)
    following = refs.pop(0) if has_next else None
    weights = refs.pop(0)
    given = refs.pop(0) if hands_on else None
    saved = [] if has_next else [refs.pop(0) for _ in range(n_saved)]
    if has_next:
        own_out, up_out, down_out = refs.pop(0), refs.pop(0), refs.pop(0)
        passed, given_v = (refs.pop(0), refs.pop()) if hands_on else (None, None)
        k_v, once, smooth, own_v, up_s, down_s, pack_v, sems = refs
    else:
        if chunk:
            refs.pop(0)
        result, k_v, once, smooth, own_v, turned, sems = refs
    fields, cells = upper.shape[1:]
    rows = forcing.shape[0]
    count, per_row = weights.shape[:2]
    block = weights.shape[-1]
    extent = rows + 2 * halo
    lo, hi = halo, halo + rows

    if hands_on:
        @pl.when(flags[0] != number)
        def _():
            for copy in (
                pltpu.make_async_copy(given, given_v, sems.at[0]), pltpu.make_async_copy(given_v, passed, sems.at[1])
            ):
                copy.start()
                copy.wait()

    @pl.when(flags[0] == number)
    def _():
        mine = slice(chunk * fields, (chunk + 1) * fields)
        beside = beside_matrix(cells)
        top = jnp.where(flags[1] == 1, 0.0, 1.0)
        bottom = jnp.where(flags[2] == 1, 0.0, 1.0)
        for edge, start in ((upper, 0), (lower, hi)):
            parts = edge[halo].astype(jnp.float32)
            k_v[start:start + halo, :] = parts[:halo] + parts[halo:2 * halo] + parts[2 * halo:3 * halo]
        k_v[lo:hi, :] = kappa[...]

        def entry(i):
            if i < lo:
                return upper[i].astype(jnp.float32)
            if i >= hi:
                return lower[i - hi].astype(jnp.float32)
            value = forcing[i - lo, mine]
            if has_incoming:
                value = value + incoming[i - lo].astype(jnp.float32)
            return value

        def step(i, here, north, south, east_west):
            if i == lo:
                north = north * top
            if i == lo - 1:
                south = south * top
            if i == hi:
                north = north * bottom
            if i == hi - 1:
                south = south * bottom
            return here + k_v[i:i + 1, :] * ((north + south) + (east_west - 4.0 * here))

        def pair_beside(first, second):
            joined = jnp.concatenate([first.astype(jnp.bfloat16), second.astype(jnp.bfloat16)], axis=1)
            total = jnp.dot(joined, beside, preferred_element_type=jnp.float32)
            return total[:, :cells], total[:, cells:]

        there, after = None, entry(0)
        for i in range(0, extent, 2):
            before, here, there = there, after, entry(i + 1)
            after = entry(i + 2) if i + 2 < extent else None
            ew_here, ew_there = pair_beside(here, there)
            if i > 0:
                once[i] = step(i, here, before, there, ew_here)
            if i + 2 < extent:
                once[i + 1] = step(i + 1, there, here, after, ew_there)
        for i in range(2, extent - 2, 2):
            here, there = once[i], once[i + 1]
            ew_here, ew_there = pair_beside(here, there)
            out = i // 2 - 1
            smooth[out, :, :cells] = step(i, here, once[i - 1], there, ew_here).astype(jnp.bfloat16)
            smooth[out, :, cells:] = step(i + 1, there, here, once[i + 2], ew_there).astype(jnp.bfloat16)

        half = (halo - EDGE) * cells // block
        block_rows = block // cells
        stores = []
        if has_next:
            parts = following[rows].astype(jnp.float32)
            parts = [parts[p * rows:(p + 1) * rows] for p in range(3)]
            up_s[halo] = joined([part[:halo] for part in parts], pack_v)
            down_s[halo] = joined([part[rows - halo:] for part in parts], pack_v)
        for j in range(count):
            total = None
            for k in range(per_row):
                source = smooth[offsets[j, k] + (j + half)]
                term = lax.dot_general(
                    source, weights[j, k], (((1,), (1,)), ((), ())), preferred_element_type=jnp.float32
                )
                total = term if total is None else total + term
            for r in range(block_rows):
                row = j * block_rows + r
                value = total[:, r * cells:(r + 1) * cells].astype(jnp.bfloat16)
                own_v[row] = value
                if has_next:
                    entry_next = value.astype(jnp.float32) + following[row, mine].astype(jnp.float32)
                    if row < halo:
                        up_s[row] = entry_next.astype(jnp.bfloat16)
                    if row >= rows - halo:
                        down_s[row - (rows - halo)] = entry_next.astype(jnp.bfloat16)
                    if row == halo - 1:
                        stores.append(pltpu.make_async_copy(up_s, up_out, sems.at[0]))
                        stores[-1].start()
        if has_next:
            ends = [
                pltpu.make_async_copy(down_s, down_out, sems.at[1]),
                pltpu.make_async_copy(own_v, own_out, sems.at[2]),
            ]
            start_all(ends)
            wait_all(stores + ends)

    if not has_next:
        for i, kept in enumerate(saved):
            @pl.when(flags[0] == i)
            def _(kept=kept):
                copy = pltpu.make_async_copy(kept, own_v, sems.at[0])
                copy.start()
                copy.wait()

        lanes = 16
        for y in range(0, rows, lanes):
            turned[:, y:y + lanes, :] = jnp.swapaxes(own_v[y:y + lanes], 0, 1)
        copy = pltpu.make_async_copy(turned, result.at[pl.ds(chunk * fields, fields)], sems.at[1])
        copy.start()
        copy.wait()


def section(number, chunk, halo, flags, offsets, kappa, forcing, incoming, upper, lower, following, weights, given, saved, result):
    rows, total, cells = forcing.shape
    fields = upper.shape[1]
    count, per_row, block, _ = weights.shape
    has_incoming, has_next = incoming is not None, following is not None
    operands = [flags, offsets]
    forcing, weights = (pltpu.with_memory_space_constraint(value, pltpu.VMEM) for value in (forcing, weights))
    for value in (kappa, forcing, incoming, upper, lower, following, weights):
        if value is not None:
            operands.append(value)
    specs = [SMEM] * 2 + [VMEM] * (len(operands) - 2)
    if given is not None:
        operands.append(pltpu.with_memory_space_constraint(given, pltpu.HBM))
        specs.append(HBM)
    extent = rows + 2 * halo
    scratch = [
        pltpu.VMEM((extent, cells), jnp.float32),
        pltpu.VMEM((extent, fields, cells), jnp.float32),
        pltpu.VMEM(((extent - 2 * EDGE) * cells // block, fields, block), jnp.bfloat16),
        pltpu.VMEM((rows, fields, cells), jnp.bfloat16),
    ]
    aliases = {}
    if has_next:
        outs = [jax.ShapeDtypeStruct((n, fields, cells), jnp.bfloat16) for n in (rows, halo + 1, halo + 1)]
        if given is not None:
            outs.append(pltpu.HBM(given.shape, given.dtype))
        scratch += [pltpu.VMEM((halo + 1, fields, cells), jnp.bfloat16)] * 2 + [pltpu.VMEM((fields, cells), jnp.float32)]
    else:
        outs = [jax.ShapeDtypeStruct((total, rows, cells), jnp.bfloat16)]
        scratch += [pltpu.VMEM((fields, rows, cells), jnp.bfloat16)]
        operands += [pltpu.with_memory_space_constraint(value, pltpu.HBM) for value in saved]
        specs += [HBM] * len(saved)
        if result is not None:
            aliases = {len(operands): 0}
            operands.append(result)
            specs.append(HBM)
    return pl.pallas_call(
        functools.partial(section_kernel, number, chunk, halo, has_incoming, has_next, given is not None, len(saved)),
        in_specs=specs,
        out_shape=outs,
        out_specs=[ANY] * 3 + [HBM] * (len(outs) - 3) if has_next else [HBM],
        input_output_aliases=aliases,
        scratch_shapes=scratch + [pltpu.SemaphoreType.DMA((3,))] + (
            [pltpu.VMEM(given.shape, given.dtype)] if given is not None else []
        ),
        compiler_params=pltpu.CompilerParams(vmem_limit_bytes=LIMIT),
        cost_estimate=pl.CostEstimate(
            flops=FLOPS * 2 * count * per_row * block * block * fields, bytes_accessed=weights.size * 2, transcendentals=0,
        ),
    )(*operands)


def local(forcing, kappa, col_blocks, remap_weights):
    n_tile = lax.axis_size("tile")
    n_section = lax.axis_size("comp")
    tile_pos = lax.axis_index("tile")
    section_pos = lax.axis_index("comp")
    weights = remap_weights[0]
    count, block = weights.shape[0], weights.shape[-1]
    rows, cells = forcing.shape[-2:]
    half = count // 2
    halo = half * block // cells + EDGE
    total_blocks = count * n_tile
    global_block = tile_pos * count + jnp.arange(count, dtype=jnp.int32)
    offsets = jnp.mod(col_blocks[0] - global_block[:, None] + half, total_blocks) - half

    def place(s, t):
        return s * n_tile + t % n_tile

    def send(value, source, target, shift, swap=True):
        pairs = [(place(source, t), place(target, t + shift)) for t in range(n_tile)]
        others = [s for s in range(n_section) if s not in (source, target)]
        if swap and source == target:
            rest = list(zip(others, others[1:] + others[:1]))
        elif swap and source ^ 1 == target and n_section % 2 == 0:
            rest = [(target, source)] + [(s, s ^ 1) for s in others]
        else:
            rest = []
        pairs += [(place(s, t), place(to, t)) for s, to in rest for t in range(n_tile)]
        return lax.ppermute(value, AXES, pairs)

    fields = forcing.reshape(-1, rows, cells)
    flags = jnp.stack([section_pos, tile_pos == 0, tile_pos == n_tile - 1]).astype(jnp.int32)
    k_here = kappa[0]
    narrow, *edges = prepare(fields, k_here, halo)
    arrivals = []
    for c in range(CHUNKS):
        arrivals.append((None, send(edges[2 * c + 1], 0, 0, 1), send(edges[2 * c], 0, 0, -1)))
    weights, by_row = load(weights, fields, (flags, offsets))
    following = [lax.ppermute(narrow, "comp", [(s, s ^ 1) for s in range(n_section) if s ^ 1 < n_section])]
    owns = [[] for _ in range(CHUNKS)]
    result = None
    for s in range(n_section):
        last = s + 1 == n_section
        leaving = []
        for c in range(CHUNKS):
            incoming, upper, lower = arrivals[c]
            parts = section(
                s, c, halo, flags, offsets, k_here, by_row, incoming, upper, lower,
                None if last else following[s % 2], weights, narrow if s + c == 0 else None,
                owns[c] if last else [], result,
            )
            if last:
                result = parts[0]
            else:
                own, up, down, *passed = parts
                if passed:
                    following.append(lax.ppermute(passed[0], "comp", [(i + 1, i) for i in range(1, n_section - 1, 2)]))
                owns[c].append(own)
                sent = [send(part, s, s + 1, shift, c == 0) for part, shift in ((own, 0), (down, 1), (up, -1))]
                leaving.append(sent)
        arrivals = leaving
    return result.reshape(forcing.shape)


def solution(mesh):
    placed = (
        P("comp", None, None, "tile", None),
        P("comp", "tile", None),
        P("comp", "tile", None),
        P("comp", "tile", None, None, None),
    )
    return jax.shard_map(
        local,
        mesh=mesh,
        in_specs=placed,
        out_specs=P("comp", None, None, "tile", None),
        check_vma=False,
    )
```

time: 124 us -> 97.3 us (0.78)
  starting transfers between devices: 31.1 us -> 56.7 us
  waiting for transfers between devices: 37.2 us -> 12.4 us
  local copies, waits for them, and re-layouts: 22.6 us -> 0.12 us
  other arithmetic: 2.93 us -> 0.16 us
  Pallas kernels: 29.3 us -> 26.9 us
    ppermute x25 -> x24, starting transfers between devices: 31.1 us -> 56.7 us  [the longest x22 55.2 us: send(): return lax.ppermute(value, AXES, pairs)]
    ppermute x25 -> x24, waiting for transfers between devices: 37.2 us -> 12.4 us  [the longest x22 12.4 us: send(): return lax.ppermute(value, AXES, pairs)]
    unnamed x32 -> x16, local copies, waits for them, and re-layouts: 20.9 us -> 0.03 us
    select_n x2 -> x0, other arithmetic: 2.45 us -> none  [local(): jnp.where(section_pos == s, own, results[-CHUNKS])]
    pallas_call x9 -> x10, Pallas kernels: 29.3 us -> 26.9 us  [the longest x8 19.1 us: section(): pl.pallas_call(functools.partial(section_kernel, number, chunk, halo, has...]
    reshape x1 -> x0, local copies, waits for them, and re-layouts: 1.65 us -> none  [local(): return jnp.transpose(kept, (1, 0, 2)).reshape(forcing.shape)]
  transfers between devices with their start and end apart: 25 -> 24, of which waited for: 4 -> 5; matrix products, arithmetic and copies ran while one was open for 1% -> 0% of each run, Pallas kernels for 14% -> 18%
where the time goes in v1:
time: 97.3 us; the launch traced here: 96.8 us
  starting transfers between devices  56.7 us (58%)
  Pallas kernels  26.9 us (28%)
  waiting for transfers between devices  12.4 us (13%)
    ppermute x22, starting transfers between devices, send(): return lax.ppermute(value, AXES, pairs)  55.2 us
    pallas_call x8, Pallas kernels, section(): pl.pallas_call(functools.partial(section_kernel, number, chunk, halo, has...  19.1 us
    ppermute x22, waiting for transfers between devices, send(): return lax.ppermute(value, AXES, pairs)  12.4 us
    pallas_call x1, Pallas kernels, load(): pl.pallas_call(load_kernel, in_specs=[HBM] * 2 + [ANY] * len(after), out_...  4.6 us
    pallas_call x1, Pallas kernels, prepare(): pl.pallas_call(prepare_kernel, in_specs=[HBM, HBM], out_shape=[pltpu.HBM(...  3.23 us
  transfers between devices with their start and end apart: 24, of which 5 were waited for; matrix products, arithmetic and copies ran while one was open for 0% of the time, Pallas kernels for 18%

profile of v1, /device:TPU:3, one launch (start us, length us, event | category | flops | bytes accessed | tf_op | source)
XLA Modules:
  0.0 96.8 jit_solution(16033089348565889088)
XLA Ops:
  0.0 3.2 %shard_map.47 = (bf16[33,128,128]{2,1,0:T(8,128)(2,1)}, bf16[19,64,128]{2,1,0:T(8,128)(2,1)}, bf16[19,64,128]{2,1,0:T(8,128)(2,1)}, bf16[19,64,128]{2,1,0:T(8,128)(2,1)}, bf16[19,64,128]{2,1,0:T(8,128)(2,1)}) custom-call(f32[128,32,128]{2,1,0:T(8,128)} %bitcast.18, f32[32,128]{1,0:T(8,128)} %bitcast.8), custom_call_target="tpu_custom_call" | custom-call | bytes 6291456 | tf_op jit(solution)/shard_map/pallas_call | solution.py:96
  3.2 0.7 collective-permute-start.2
  4.0 0.0 collective-permute-start.6
  4.0 1.4 %collective-permute-start.7 = (bf16[19,64,128]{2,1,0:T(8,128)(2,1)}, bf16[19,64,128]{2,1,0:T(8,128)(2,1)S(1)}, u32[]{:S(2)}, u32[]{:S(2)}) collective-permute-start(bf16[19,64,128]{2,1,0:T(8,128)(2,1)} %get-tuple-element.40), channel_id=1, source_target_pairs={{0,7},{1,0},{2,1},{3,2},{4,3},{5,4},{6,5},{7,6},{8,16},{9,17},{10,... | collective-permute-start | bytes 933896 | tf_op jit(solution)/shard_map/ppermute | solution.py:370
  5.4 0.4 collective-permute-start
  5.8 0.0 collective-permute-start.1
  5.9 0.1 copy.6
  6.0 0.1 pad_add_fusion.refs_0_.flags
  6.1 0.1 fusion.1.refs_1_.offsets
  6.1 4.6 %shard_map.46 = (bf16[16,4,256,256]{3,2,1,0:T(8,128)(2,1)S(1)}, f32[32,128,128]{2,1,0:T(8,128)S(1)}) custom-call(bf16[16,4,256,256]{3,2,1,0:T(8,128)(2,1)} %bitcast.17, f32[128,32,128]{2,1,0:T(8,128)} %bitcast.19, s32[3]{0:T(128)S(1)} %pad_add_fusion.refs_0_.flags, s32[16,4]{1,0:T(8,128)S(1)} %fusion.1.refs_1_.offsets), custom_call_target="tpu_custom_call" | custom-call | bytes 16777216 | tf_op jit(solution)/shard_map/pallas_call | solution.py:130
  10.7 0.0 collective-permute-done.6.refs_0_
  10.8 0.7 collective-permute-done.7.refs_1_
  11.5 0.0 collective-permute-done.2.refs_2_.refs_3_
  11.5 0.0 copy-done
  11.5 2.9 %shard_map.49 = (bf16[32,64,128]{2,1,0:T(8,128)(2,1)S(1)}, bf16[19,64,128]{2,1,0:T(8,128)(2,1)S(1)}, bf16[19,64,128]{2,1,0:T(8,128)(2,1)S(1)}, bf16[33,128,128]{2,1,0:T(8,128)(2,1)}) custom-call(s32[3]{0:T(128)S(1)} %pad_add_fusion.refs_0_.flags, s32[16,4]{1,0:T(8,128)S(1)} %fusion.1.refs_1_.offsets, f32[32,128]{1,0:T(8,128)S(1)} %bitcast.9, ...), custom_call_target="tpu_custom_call" | custom-call | flops 10737418240 | bytes 8388608 | tf_op jit(solution)/shard_map/pallas_call | solution.py:327
  14.4 0.7 collective-permute-start.8
  15.2 3.8 %collective-permute-start.15 = (bf16[32,64,128]{2,1,0:T(8,128)(2,1)S(1)}, bf16[32,64,128]{2,1,0:T(8,128)(2,1)S(1)}, u32[]{:S(2)}, u32[]{:S(2)}) collective-permute-start(bf16[32,64,128]{2,1,0:T(8,128)(2,1)S(1)} %get-tuple-element.48.refs_4_), channel_id=1, source_target_pairs={{0,8},{1,9},{2,10},{3,11},{4,12},{5,13},{6,14},{7,15},{8,0},{9,1},... | collective-permute-start | bytes 1572872 | tf_op jit(solution)/shard_map/ppermute | solution.py:370
  19.0 0.1 collective-permute-start.16
  19.0 0.0 collective-permute-done.refs_0_
  19.0 0.4 collective-permute-start.17
  19.5 0.0 collective-permute-done.1.refs_1_
  19.5 0.7 shard_map.48
  20.2 0.7 collective-permute-start.3
  20.9 0.0 collective-permute-done.16.refs_1_
  20.9 0.7 collective-permute-start.4
  21.6 0.0 collective-permute-done.17.refs_2_
  21.6 0.7 collective-permute-start.5
  22.3 0.0 collective-permute-done.15.refs_0_
  22.3 0.0 collective-permute-done.8.refs_3_
  22.3 0.9 shard_map.52
  23.2 0.7 collective-permute-start.18
  24.0 0.7 collective-permute-start.19
  24.6 0.0 collective-permute-done.4.refs_1_
  24.6 0.7 collective-permute-start.20
  25.3 0.0 collective-permute-done.5.refs_2_
  25.3 0.0 collective-permute-done.3.refs_0_
  25.4 0.7 shard_map.50
  26.1 0.0 copy-done.3
  26.1 0.0 copy-start.4
  26.1 0.7 collective-permute-start.9
  26.8 0.7 collective-permute-start.10
  27.5 0.0 collective-permute-done.19.refs_1_
  27.5 0.7 collective-permute-start.11
  28.2 0.0 collective-permute-done.20.refs_2_
  28.2 0.0 collective-permute-done.18.refs_0_
  28.2 0.7 shard_map.53
  28.9 36.1 %collective-permute-start.21 = (bf16[32,64,128]{2,1,0:T(8,128)(2,1)S(1)}, bf16[32,64,128]{2,1,0:T(8,128)(2,1)S(1)}, u32[]{:S(2)}, u32[]{:S(2)}) collective-permute-start(bf16[32,64,128]{2,1,0:T(8,128)(2,1)S(1)} %get-tuple-element.54.refs_6_), channel_id=1, source_target_pairs={{16,24},{17,25},{18,26},{19,27},{20,28},{21,29},{22,30},{23,31},{2... | collective-permute-start | bytes 1572872 | tf_op jit(solution)/shard_map/ppermute | solution.py:370
  65.0 0.1 collective-permute-start.22
  65.1 0.0 collective-permute-done.10.refs_1_
  65.1 2.9 %collective-permute-start.23 = (bf16[19,64,128]{2,1,0:T(8,128)(2,1)S(1)}, bf16[19,64,128]{2,1,0:T(8,128)(2,1)S(1)}, u32[]{:S(2)}, u32[]{:S(2)}) collective-permute-start(bf16[19,64,128]{2,1,0:T(8,128)(2,1)S(1)} %get-tuple-element.56), channel_id=1, source_target_pairs={{16,31},{17,24},{18,25},{19,26},{20,27},{21,28},{22,29},{23,30},{2... | collective-permute-start | bytes 933896 | tf_op jit(solution)/shard_map/ppermute | solution.py:370
  67.9 0.0 collective-permute-done.11.refs_2_
  67.9 0.0 collective-permute-done.9.refs_0_
  67.9 0.9 shard_map.51
  68.9 1.3 %collective-permute-start.12 = (bf16[32,64,128]{2,1,0:T(8,128)(2,1)S(1)}, bf16[32,64,128]{2,1,0:T(8,128)(2,1)S(1)}, u32[]{:S(2)}, u32[]{:S(2)}) collective-permute-start(bf16[32,64,128]{2,1,0:T(8,128)(2,1)S(1)} %get-tuple-element.45.refs_6_), channel_id=1, source_target_pairs={{16,24},{17,25},{18,26},{19,27},{20,28},{21,29},{22,30},{23,31}} | collective-permute-start | bytes 1572872 | tf_op jit(solution)/shard_map/ppermute | solution.py:370
  70.2 1.3 %collective-permute-start.13 = (bf16[19,64,128]{2,1,0:T(8,128)(2,1)S(1)}, bf16[19,64,128]{2,1,0:T(8,128)(2,1)S(1)}, u32[]{:S(2)}, u32[]{:S(2)}) collective-permute-start(bf16[19,64,128]{2,1,0:T(8,128)(2,1)S(1)} %get-tuple-element.46), channel_id=1, source_target_pairs={{16,25},{17,26},{18,27},{19,28},{20,29},{21,30},{22,31},{23,24}} | collective-permute-start | bytes 933896 | tf_op jit(solution)/shard_map/ppermute | solution.py:370
  71.5 2.6 %collective-permute-done.22.refs_1_ = bf16[19,64,128]{2,1,0:T(8,128)(2,1)S(1)} collective-permute-done((bf16[19,64,128]{2,1,0:T(8,128)(2,1)S(1)}, bf16[19,64,128]{2,1,0:T(8,128)(2,1)S(1)}, u32[]{:S(2)}, u32[]{:S(2)}) %collective-permute-start.22) | collective-permute-done | bytes 311328 | tf_op jit(solution)/shard_map/ppermute | solution.py:370
  74.1 1.3 %collective-permute-start.14 = (bf16[19,64,128]{2,1,0:T(8,128)(2,1)S(1)}, bf16[19,64,128]{2,1,0:T(8,128)(2,1)S(1)}, u32[]{:S(2)}, u32[]{:S(2)}) collective-permute-start(bf16[19,64,128]{2,1,0:T(8,128)(2,1)S(1)} %get-tuple-element.47), channel_id=1, source_target_pairs={{16,31},{17,24},{18,25},{19,26},{20,27},{21,28},{22,29},{23,30}} | collective-permute-start | bytes 933896 | tf_op jit(solution)/shard_map/ppermute | solution.py:370
  75.4 2.0 %collective-permute-done.23.refs_2_ = bf16[19,64,128]{2,1,0:T(8,128)(2,1)S(1)} collective-permute-done((bf16[19,64,128]{2,1,0:T(8,128)(2,1)S(1)}, bf16[19,64,128]{2,1,0:T(8,128)(2,1)S(1)}, u32[]{:S(2)}, u32[]{:S(2)}) %collective-permute-start.23) | collective-permute-done | bytes 311328 | tf_op jit(solution)/shard_map/ppermute | solution.py:370
  77.5 0.0 collective-permute-done.21.refs_0_
  77.5 6.1 %shard_map.54.refs_7_ = bf16[128,32,128]{2,1,0:T(8,128)(2,1)} custom-call(s32[3]{0:T(128)S(1)} %pad_add_fusion.refs_0_.flags, s32[16,4]{1,0:T(8,128)S(1)} %fusion.1.refs_1_.offsets, f32[32,128]{1,0:T(8,128)S(1)} %bitcast.15, f32[32,128,128]{2,1,0:T(8,128)S(1)} %get-tuple-element.31.forcing, bf16[32,64,128]{2,1,0:T(8,128)(2,1)S(1)} %collective-permute-done.21.refs_0_, ...), custom_call_target="tpu_custom_call" | custom-call | flops 10737418240 | bytes 8388608 | tf_op jit(solution)/shard_map/pallas_call | solution.py:327
  83.6 4.2 %collective-permute-done.13.refs_1_ = bf16[19,64,128]{2,1,0:T(8,128)(2,1)S(1)} collective-permute-done((bf16[19,64,128]{2,1,0:T(8,128)(2,1)S(1)}, bf16[19,64,128]{2,1,0:T(8,128)(2,1)S(1)}, u32[]{:S(2)}, u32[]{:S(2)}) %collective-permute-start.13) | collective-permute-done | bytes 311328 | tf_op jit(solution)/shard_map/ppermute | solution.py:370
  87.8 2.7 %collective-permute-done.14.refs_2_ = bf16[19,64,128]{2,1,0:T(8,128)(2,1)S(1)} collective-permute-done((bf16[19,64,128]{2,1,0:T(8,128)(2,1)S(1)}, bf16[19,64,128]{2,1,0:T(8,128)(2,1)S(1)}, u32[]{:S(2)}, u32[]{:S(2)}) %collective-permute-start.14) | collective-permute-done | bytes 311328 | tf_op jit(solution)/shard_map/ppermute | solution.py:370
  90.5 0.0 collective-permute-done.12.refs_0_
  90.5 6.1 %shard_map.55 = bf16[128,32,128]{2,1,0:T(8,128)(2,1)} custom-call(s32[3]{0:T(128)S(1)} %pad_add_fusion.refs_0_.flags, s32[16,4]{1,0:T(8,128)S(1)} %fusion.1.refs_1_.offsets, f32[32,128]{1,0:T(8,128)S(1)} %bitcast.16, f32[32,128,128]{2,1,0:T(8,128)S(1)} %get-tuple-element.31.forcing, ...), custom_call_target="tpu_custom_call", output_to_operand_aliasing={{}: (11, {})} | custom-call | flops 10737418240 | bytes 8388608 | tf_op jit(solution)/shard_map/pallas_call | solution.py:327
  (14 shorter events, 0.0 us)
Async XLA Ops:
  0.0 5.9 %copy-start.7 = (s32[1,16,4]{1,2,0:T(4,128)S(1)}, s32[1,16,4]{1,2,0:T(4,128)}, u32[]{:S(2)}) copy-start(s32[1,16,4]{1,2,0:T(4,128)} %param.6) | copy-start | bytes 772
  3.2 8.2 %collective-permute-start.2 = (bf16[33,128,128]{2,1,0:T(8,128)(2,1)}, bf16[33,128,128]{2,1,0:T(8,128)(2,1)S(1)}, u32[]{:S(2)}, u32[]{:S(2)}) collective-permute-start(bf16[33,128,128]{2,1,0:T(8,128)(2,1)} %get-tuple-element.34.refs_4_), channel_id=1, source_target_pairs={{0,8},{8,0},{16,24},{24,16},{1,9},{9,1},{17,25},{25,17},{2,10},{10... | collective-permute-start | bytes 3244040 | tf_op jit(solution)/shard_map/ppermute | solution.py:380
  4.0 6.8 %collective-permute-start.6 = (bf16[19,64,128]{2,1,0:T(8,128)(2,1)}, bf16[19,64,128]{2,1,0:T(8,128)(2,1)S(1)}, u32[]{:S(2)}, u32[]{:S(2)}) collective-permute-start(bf16[19,64,128]{2,1,0:T(8,128)(2,1)} %get-tuple-element.39), channel_id=1, source_target_pairs={{0,1},{1,2},{2,3},{3,4},{4,5},{5,6},{6,7},{7,0},{8,16},{9,17},{10,... | collective-permute-start | bytes 933896 | tf_op jit(solution)/shard_map/ppermute | solution.py:370
  4.0 7.5 %collective-permute-start.7 = (bf16[19,64,128]{2,1,0:T(8,128)(2,1)}, bf16[19,64,128]{2,1,0:T(8,128)(2,1)S(1)}, u32[]{:S(2)}, u32[]{:S(2)}) collective-permute-start(bf16[19,64,128]{2,1,0:T(8,128)(2,1)} %get-tuple-element.40), channel_id=1, source_target_pairs={{0,7},{1,0},{2,1},{3,2},{4,3},{5,4},{6,5},{7,6},{8,16},{9,17},{10,... | collective-permute-start | bytes 933896 | tf_op jit(solution)/shard_map/ppermute | solution.py:370
  5.4 13.6 %collective-permute-start = (bf16[19,64,128]{2,1,0:T(8,128)(2,1)}, bf16[19,64,128]{2,1,0:T(8,128)(2,1)S(1)}, u32[]{:S(2)}, u32[]{:S(2)}) collective-permute-start(bf16[19,64,128]{2,1,0:T(8,128)(2,1)} %get-tuple-element.32), channel_id=1, source_target_pairs={{0,1},{1,2},{2,3},{3,4},{4,5},{5,6},{6,7},{7,0},{8,16},{9,17},{10,... | collective-permute-start | bytes 933896 | tf_op jit(solution)/shard_map/ppermute | solution.py:370
  5.8 13.6 %collective-permute-start.1 = (bf16[19,64,128]{2,1,0:T(8,128)(2,1)}, bf16[19,64,128]{2,1,0:T(8,128)(2,1)S(1)}, u32[]{:S(2)}, u32[]{:S(2)}) collective-permute-start(bf16[19,64,128]{2,1,0:T(8,128)(2,1)} %get-tuple-element.33), channel_id=1, source_target_pairs={{0,7},{1,0},{2,1},{3,2},{4,3},{5,4},{6,5},{7,6},{8,16},{9,17},{10,... | collective-permute-start | bytes 933896 | tf_op jit(solution)/shard_map/ppermute | solution.py:370
  6.1 5.3 %copy-start = (f32[1,32,128]{2,1,0:T(8,128)S(1)}, f32[1,32,128]{2,1,0:T(8,128)}, u32[]{:S(2)}) copy-start(f32[1,32,128]{2,1,0:T(8,128)} %param.5) | copy-start | bytes 49156
  14.4 5.8 %copy-start.1 = (bf16[32,64,128]{2,1,0:T(8,128)(2,1)}, bf16[32,64,128]{2,1,0:T(8,128)(2,1)S(1)}, u32[]{:S(2)}) copy-start(bf16[32,64,128]{2,1,0:T(8,128)(2,1)S(1)} %get-tuple-element.48.refs_4_) | copy-start | bytes 1572868
  14.4 7.9 %collective-permute-start.8 = (bf16[33,128,128]{2,1,0:T(8,128)(2,1)}, bf16[33,128,128]{2,1,0:T(8,128)(2,1)S(1)}, u32[]{:S(2)}, u32[]{:S(2)}) collective-permute-start(bf16[33,128,128]{2,1,0:T(8,128)(2,1)} %get-tuple-element.41), channel_id=1, source_target_pairs={{16,8},{17,9},{18,10},{19,11},{20,12},{21,13},{22,14},{23,15}} | collective-permute-start | bytes 3244040 | tf_op jit(solution)/shard_map/ppermute | solution.py:398
  15.2 7.2 %collective-permute-start.15 = (bf16[32,64,128]{2,1,0:T(8,128)(2,1)S(1)}, bf16[32,64,128]{2,1,0:T(8,128)(2,1)S(1)}, u32[]{:S(2)}, u32[]{:S(2)}) collective-permute-start(bf16[32,64,128]{2,1,0:T(8,128)(2,1)S(1)} %get-tuple-element.48.refs_4_), channel_id=1, source_target_pairs={{0,8},{1,9},{2,10},{3,11},{4,12},{5,13},{6,14},{7,15},{8,0},{9,1},... | collective-permute-start | bytes 1572872 | tf_op jit(solution)/shard_map/ppermute | solution.py:370
  19.0 2.0 %collective-permute-start.16 = (bf16[19,64,128]{2,1,0:T(8,128)(2,1)S(1)}, bf16[19,64,128]{2,1,0:T(8,128)(2,1)S(1)}, u32[]{:S(2)}, u32[]{:S(2)}) collective-permute-start(bf16[19,64,128]{2,1,0:T(8,128)(2,1)S(1)} %get-tuple-element.49), channel_id=1, source_target_pairs={{0,9},{1,10},{2,11},{3,12},{4,13},{5,14},{6,15},{7,8},{8,0},{9,1},... | collective-permute-start | bytes 933896 | tf_op jit(solution)/shard_map/ppermute | solution.py:370
  19.0 2.6 %collective-permute-start.17 = (bf16[19,64,128]{2,1,0:T(8,128)(2,1)S(1)}, bf16[19,64,128]{2,1,0:T(8,128)(2,1)S(1)}, u32[]{:S(2)}, u32[]{:S(2)}) collective-permute-start(bf16[19,64,128]{2,1,0:T(8,128)(2,1)S(1)} %get-tuple-element.50), channel_id=1, source_target_pairs={{0,15},{1,8},{2,9},{3,10},{4,11},{5,12},{6,13},{7,14},{8,0},{9,1},... | collective-permute-start | bytes 933896 | tf_op jit(solution)/shard_map/ppermute | solution.py:370
  20.2 3.0 %copy-start.2 = (bf16[32,64,128]{2,1,0:T(8,128)(2,1)}, bf16[32,64,128]{2,1,0:T(8,128)(2,1)S(1)}, u32[]{:S(2)}) copy-start(bf16[32,64,128]{2,1,0:T(8,128)(2,1)S(1)} %get-tuple-element.36.refs_4_) | copy-start | bytes 1572868
  20.2 5.1 %collective-permute-start.3 = (bf16[32,64,128]{2,1,0:T(8,128)(2,1)S(1)}, bf16[32,64,128]{2,1,0:T(8,128)(2,1)S(1)}, u32[]{:S(2)}, u32[]{:S(2)}) collective-permute-start(bf16[32,64,128]{2,1,0:T(8,128)(2,1)S(1)} %get-tuple-element.36.refs_4_), channel_id=1, source_target_pairs={{0,8},{1,9},{2,10},{3,11},{4,12},{5,13},{6,14},{7,15}} | collective-permute-start | bytes 1572872 | tf_op jit(solution)/shard_map/ppermute | solution.py:370
  20.9 3.7 %collective-permute-start.4 = (bf16[19,64,128]{2,1,0:T(8,128)(2,1)S(1)}, bf16[19,64,128]{2,1,0:T(8,128)(2,1)S(1)}, u32[]{:S(2)}, u32[]{:S(2)}) collective-permute-start(bf16[19,64,128]{2,1,0:T(8,128)(2,1)S(1)} %get-tuple-element.37), channel_id=1, source_target_pairs={{0,9},{1,10},{2,11},{3,12},{4,13},{5,14},{6,15},{7,8}} | collective-permute-start | bytes 933896 | tf_op jit(solution)/shard_map/ppermute | solution.py:370
  21.6 3.7 %collective-permute-start.5 = (bf16[19,64,128]{2,1,0:T(8,128)(2,1)S(1)}, bf16[19,64,128]{2,1,0:T(8,128)(2,1)S(1)}, u32[]{:S(2)}, u32[]{:S(2)}) collective-permute-start(bf16[19,64,128]{2,1,0:T(8,128)(2,1)S(1)} %get-tuple-element.38), channel_id=1, source_target_pairs={{0,15},{1,8},{2,9},{3,10},{4,11},{5,12},{6,13},{7,14}} | collective-permute-start | bytes 933896 | tf_op jit(solution)/shard_map/ppermute | solution.py:370
  23.2 2.8 %copy-start.3 = (bf16[32,64,128]{2,1,0:T(8,128)(2,1)}, bf16[32,64,128]{2,1,0:T(8,128)(2,1)S(1)}, u32[]{:S(2)}) copy-start(bf16[32,64,128]{2,1,0:T(8,128)(2,1)S(1)} %get-tuple-element.51.refs_5_) | copy-start | bytes 1572868
  23.2 5.0 %collective-permute-start.18 = (bf16[32,64,128]{2,1,0:T(8,128)(2,1)S(1)}, bf16[32,64,128]{2,1,0:T(8,128)(2,1)S(1)}, u32[]{:S(2)}, u32[]{:S(2)}) collective-permute-start(bf16[32,64,128]{2,1,0:T(8,128)(2,1)S(1)} %get-tuple-element.51.refs_5_), channel_id=1, source_target_pairs={{8,16},{9,17},{10,18},{11,19},{12,20},{13,21},{14,22},{15,23}} | collective-permute-start | bytes 1572872 | tf_op jit(solution)/shard_map/ppermute | solution.py:370
  24.0 3.5 %collective-permute-start.19 = (bf16[19,64,128]{2,1,0:T(8,128)(2,1)S(1)}, bf16[19,64,128]{2,1,0:T(8,128)(2,1)S(1)}, u32[]{:S(2)}, u32[]{:S(2)}) collective-permute-start(bf16[19,64,128]{2,1,0:T(8,128)(2,1)S(1)} %get-tuple-element.52), channel_id=1, source_target_pairs={{8,17},{9,18},{10,19},{11,20},{12,21},{13,22},{14,23},{15,16}} | collective-permute-start | bytes 933896 | tf_op jit(solution)/shard_map/ppermute | solution.py:370
  24.6 3.5 %collective-permute-start.20 = (bf16[19,64,128]{2,1,0:T(8,128)(2,1)S(1)}, bf16[19,64,128]{2,1,0:T(8,128)(2,1)S(1)}, u32[]{:S(2)}, u32[]{:S(2)}) collective-permute-start(bf16[19,64,128]{2,1,0:T(8,128)(2,1)S(1)} %get-tuple-element.53), channel_id=1, source_target_pairs={{8,23},{9,16},{10,17},{11,18},{12,19},{13,20},{14,21},{15,22}} | collective-permute-start | bytes 933896 | tf_op jit(solution)/shard_map/ppermute | solution.py:370
  26.1 2.8 %copy-start.4 = (bf16[32,64,128]{2,1,0:T(8,128)(2,1)}, bf16[32,64,128]{2,1,0:T(8,128)(2,1)S(1)}, u32[]{:S(2)}) copy-start(bf16[32,64,128]{2,1,0:T(8,128)(2,1)S(1)} %get-tuple-element.42.refs_5_) | copy-start | bytes 1572868
  26.1 41.8 %collective-permute-start.9 = (bf16[32,64,128]{2,1,0:T(8,128)(2,1)S(1)}, bf16[32,64,128]{2,1,0:T(8,128)(2,1)S(1)}, u32[]{:S(2)}, u32[]{:S(2)}) collective-permute-start(bf16[32,64,128]{2,1,0:T(8,128)(2,1)S(1)} %get-tuple-element.42.refs_5_), channel_id=1, source_target_pairs={{8,16},{9,17},{10,18},{11,19},{12,20},{13,21},{14,22},{15,23}} | collective-permute-start | bytes 1572872 | tf_op jit(solution)/shard_map/ppermute | solution.py:370
  26.8 38.3 %collective-permute-start.10 = (bf16[19,64,128]{2,1,0:T(8,128)(2,1)S(1)}, bf16[19,64,128]{2,1,0:T(8,128)(2,1)S(1)}, u32[]{:S(2)}, u32[]{:S(2)}) collective-permute-start(bf16[19,64,128]{2,1,0:T(8,128)(2,1)S(1)} %get-tuple-element.43), channel_id=1, source_target_pairs={{8,17},{9,18},{10,19},{11,20},{12,21},{13,22},{14,23},{15,16}} | collective-permute-start | bytes 933896 | tf_op jit(solution)/shard_map/ppermute | solution.py:370
  27.5 40.4 %collective-permute-start.11 = (bf16[19,64,128]{2,1,0:T(8,128)(2,1)S(1)}, bf16[19,64,128]{2,1,0:T(8,128)(2,1)S(1)}, u32[]{:S(2)}, u32[]{:S(2)}) collective-permute-start(bf16[19,64,128]{2,1,0:T(8,128)(2,1)S(1)} %get-tuple-element.44), channel_id=1, source_target_pairs={{8,23},{9,16},{10,17},{11,18},{12,19},{13,20},{14,21},{15,22}} | collective-permute-start | bytes 933896 | tf_op jit(solution)/shard_map/ppermute | solution.py:370
  28.9 39.9 %copy-start.5 = (bf16[32,64,128]{2,1,0:T(8,128)(2,1)}, bf16[32,64,128]{2,1,0:T(8,128)(2,1)S(1)}, u32[]{:S(2)}) copy-start(bf16[32,64,128]{2,1,0:T(8,128)(2,1)S(1)} %get-tuple-element.54.refs_6_) | copy-start | bytes 1572868
  28.9 48.5 %collective-permute-start.21 = (bf16[32,64,128]{2,1,0:T(8,128)(2,1)S(1)}, bf16[32,64,128]{2,1,0:T(8,128)(2,1)S(1)}, u32[]{:S(2)}, u32[]{:S(2)}) collective-permute-start(bf16[32,64,128]{2,1,0:T(8,128)(2,1)S(1)} %get-tuple-element.54.refs_6_), channel_id=1, source_target_pairs={{16,24},{17,25},{18,26},{19,27},{20,28},{21,29},{22,30},{23,31},{2... | collective-permute-start | bytes 1572872 | tf_op jit(solution)/shard_map/ppermute | solution.py:370
  65.0 9.1 %collective-permute-start.22 = (bf16[19,64,128]{2,1,0:T(8,128)(2,1)S(1)}, bf16[19,64,128]{2,1,0:T(8,128)(2,1)S(1)}, u32[]{:S(2)}, u32[]{:S(2)}) collective-permute-start(bf16[19,64,128]{2,1,0:T(8,128)(2,1)S(1)} %get-tuple-element.55), channel_id=1, source_target_pairs={{16,25},{17,26},{18,27},{19,28},{20,29},{21,30},{22,31},{23,24},{2... | collective-permute-start | bytes 933896 | tf_op jit(solution)/shard_map/ppermute | solution.py:370
  65.1 12.4 %collective-permute-start.23 = (bf16[19,64,128]{2,1,0:T(8,128)(2,1)S(1)}, bf16[19,64,128]{2,1,0:T(8,128)(2,1)S(1)}, u32[]{:S(2)}, u32[]{:S(2)}) collective-permute-start(bf16[19,64,128]{2,1,0:T(8,128)(2,1)S(1)} %get-tuple-element.56), channel_id=1, source_target_pairs={{16,31},{17,24},{18,25},{19,26},{20,27},{21,28},{22,29},{23,30},{2... | collective-permute-start | bytes 933896 | tf_op jit(solution)/shard_map/ppermute | solution.py:370
  68.9 14.7 %copy-start.6 = (bf16[32,64,128]{2,1,0:T(8,128)(2,1)}, bf16[32,64,128]{2,1,0:T(8,128)(2,1)S(1)}, u32[]{:S(2)}) copy-start(bf16[32,64,128]{2,1,0:T(8,128)(2,1)S(1)} %get-tuple-element.45.refs_6_) | copy-start | bytes 1572868
  68.9 21.6 %collective-permute-start.12 = (bf16[32,64,128]{2,1,0:T(8,128)(2,1)S(1)}, bf16[32,64,128]{2,1,0:T(8,128)(2,1)S(1)}, u32[]{:S(2)}, u32[]{:S(2)}) collective-permute-start(bf16[32,64,128]{2,1,0:T(8,128)(2,1)S(1)} %get-tuple-element.45.refs_6_), channel_id=1, source_target_pairs={{16,24},{17,25},{18,26},{19,27},{20,28},{21,29},{22,30},{23,31}} | collective-permute-start | bytes 1572872 | tf_op jit(solution)/shard_map/ppermute | solution.py:370
  70.2 17.6 %collective-permute-start.13 = (bf16[19,64,128]{2,1,0:T(8,128)(2,1)S(1)}, bf16[19,64,128]{2,1,0:T(8,128)(2,1)S(1)}, u32[]{:S(2)}, u32[]{:S(2)}) collective-permute-start(bf16[19,64,128]{2,1,0:T(8,128)(2,1)S(1)} %get-tuple-element.46), channel_id=1, source_target_pairs={{16,25},{17,26},{18,27},{19,28},{20,29},{21,30},{22,31},{23,24}} | collective-permute-start | bytes 933896 | tf_op jit(solution)/shard_map/ppermute | solution.py:370
  74.1 16.4 %collective-permute-start.14 = (bf16[19,64,128]{2,1,0:T(8,128)(2,1)S(1)}, bf16[19,64,128]{2,1,0:T(8,128)(2,1)S(1)}, u32[]{:S(2)}, u32[]{:S(2)}) collective-permute-start(bf16[19,64,128]{2,1,0:T(8,128)(2,1)S(1)} %get-tuple-element.47), channel_id=1, source_target_pairs={{16,31},{17,24},{18,25},{19,26},{20,27},{21,28},{22,29},{23,30}} | collective-permute-start | bytes 933896 | tf_op jit(solution)/shard_map/ppermute | solution.py:370

commit v2 on v1

v2 whole, which is shorter than its diff:
```python
import functools

import jax
import jax.numpy as jnp
from jax import lax
from jax.experimental import pallas as pl
from jax.experimental.pallas import tpu as pltpu
from jax.sharding import PartitionSpec as P

AXES = ("comp", "tile")
SHARES = (1, 1)
EDGE = 2
LIMIT = 24 << 20
WEIGHT = 20
HBM = pl.BlockSpec(memory_space=pltpu.HBM)
VMEM = pl.BlockSpec(memory_space=pltpu.VMEM)
SMEM = pl.BlockSpec(memory_space=pltpu.SMEM)
ANY = pl.BlockSpec(memory_space=pl.ANY)


def start_all(copies):
    for copy in copies:
        copy.start()


def wait_all(copies):
    for copy in copies:
        copy.wait()


def in_hbm(value):
    return pltpu.with_memory_space_constraint(value, pltpu.HBM)


def in_vmem(value):
    return pltpu.with_memory_space_constraint(value, pltpu.VMEM)


def split(value):
    parts = []
    for _ in range(3):
        head = value.astype(jnp.bfloat16).astype(jnp.float32)
        parts.append(head)
        value = value - head
    return parts


def joined(parts, room):
    at = 0
    for part in parts:
        room[at:at + part.shape[0], :] = part
        at += part.shape[0]
    room[at:, :] = jnp.zeros((room.shape[0] - at, room.shape[1]), jnp.float32)
    return room[...].astype(jnp.bfloat16)


def prepare_kernel(flags, columns, forcing, kappa, *refs):
    offsets, by_row, narrow, again, first, last, c_v, f_v, k_v, pack, sems, k_sem, c_sem = refs
    total, rows, cells = f_v.shape
    halo = first.shape[0] - 1
    step = rows // sems.shape[0]
    loads = []
    for i in range(sems.shape[0]):
        part = pl.ds(i * step, step)
        loads.append(pltpu.make_async_copy(forcing.at[:, part], f_v.at[:, part], sems.at[i]))
    fetch = pltpu.make_async_copy(kappa, k_v, k_sem)
    take = pltpu.make_async_copy(columns, c_v, c_sem)
    take.start()
    fetch.start()
    start_all(loads)
    take.wait()
    count = columns.shape[1]
    ahead = c_v[...] - (flags[1] * count + lax.broadcasted_iota(jnp.int32, columns.shape, 1)) + count // 2
    every = flags[2] * count
    ahead = jnp.where(ahead < 0, ahead + every, jnp.where(ahead >= every, ahead - every, ahead))
    offsets[...] = ahead - count // 2
    fetch.wait()
    parts = split(k_v[...])
    narrow[rows] = joined(parts, pack)
    again[rows] = narrow[rows]
    first[halo] = joined([part[:halo] for part in parts], pack)
    last[halo] = joined([part[rows - halo:] for part in parts], pack)
    for i, load in enumerate(loads):
        load.wait()
        turned = jnp.swapaxes(f_v[:, i * step:(i + 1) * step, :], 0, 1)
        by_row[i * step:(i + 1) * step] = turned
        for r in range(step):
            y = i * step + r
            value = turned[r].astype(jnp.bfloat16)
            narrow[y] = value
            again[y] = value
            if y < halo:
                first[y] = value
            if y >= rows - halo:
                last[y - (rows - halo)] = value


def prepare(flags, columns, fields, kappa, halo):
    total, rows, cells = fields.shape
    return pl.pallas_call(
        prepare_kernel,
        in_specs=[SMEM, HBM, HBM, HBM],
        out_shape=[
            jax.ShapeDtypeStruct(columns.shape, columns.dtype),
            pltpu.VMEM((rows, total, cells), jnp.float32),
        ] + [jax.ShapeDtypeStruct((n + 1, total, cells), jnp.bfloat16) for n in (rows, rows, halo, halo)],
        out_specs=[VMEM] * 6,
        scratch_shapes=[
            pltpu.VMEM(columns.shape, columns.dtype),
            pltpu.VMEM((total, rows, cells), jnp.float32),
            pltpu.VMEM(kappa.shape, kappa.dtype),
            pltpu.VMEM((total, cells), jnp.float32),
            pltpu.SemaphoreType.DMA((rows // 8,)),
            pltpu.SemaphoreType.DMA,
            pltpu.SemaphoreType.DMA,
        ],
        compiler_params=pltpu.CompilerParams(vmem_limit_bytes=LIMIT),
        cost_estimate=pl.CostEstimate(flops=0, bytes_accessed=fields.size * 12, transcendentals=0),
    )(flags, in_hbm(columns), in_hbm(fields), in_hbm(kappa))


def load_kernel(flags, weights, *refs):
    held, sems = refs[-3], refs[-1]
    count, per_row = weights.shape[:2]
    loads = [pltpu.make_async_copy(weights.at[j], held.at[j], sems.at[j]) for j in range(count)]
    start_all(loads)
    wait_all(loads)

    @pl.when(flags[0] != 0)
    def _():
        def turn(i, _):
            j, k = i // per_row, i % per_row
            held[j, k] = held[j, k].T
            return 0

        lax.fori_loop(0, count * per_row, turn, 0, unroll=4)


def load(flags, weights, passed):
    return pl.pallas_call(
        load_kernel,
        in_specs=[SMEM, HBM, ANY],
        out_shape=[pltpu.VMEM(weights.shape, weights.dtype), jax.ShapeDtypeStruct(passed.shape, passed.dtype)],
        out_specs=[VMEM, ANY],
        input_output_aliases={2: 1},
        scratch_shapes=[pltpu.SemaphoreType.DMA((weights.shape[0],))],
        compiler_params=pltpu.CompilerParams(vmem_limit_bytes=LIMIT),
        cost_estimate=pl.CostEstimate(flops=0, bytes_accessed=weights.size * 4, transcendentals=0),
    )(flags, in_hbm(weights), passed)


def beside_matrix(cells):
    source = lax.broadcasted_iota(jnp.int32, (2 * cells, 2 * cells), 0)
    target = lax.broadcasted_iota(jnp.int32, (2 * cells, 2 * cells), 1)
    apart = (source - target + 2 * cells) % cells
    same = (source < cells) == (target < cells)
    return jnp.where(same & ((apart == 1) | (apart == cells - 1)), 1.0, 0.0).astype(jnp.bfloat16)


def section_kernel(number, bounds, halo, n_saved, has_next, flags, offsets, kappa, forcing, *refs):
    refs = list(refs)
    incoming = refs.pop(0) if number else None
    upper, lower = refs.pop(0), refs.pop(0)
    following = refs.pop(0) if has_next else None
    weights = refs.pop(0)
    saved = [refs.pop(0) for _ in range(n_saved)]
    if has_next:
        own_out, up_out, down_out = refs.pop(0), refs.pop(0), refs.pop(0)
    else:
        if bounds[0]:
            refs.pop(0)
        result = refs.pop(0)
    k_v, once, smooth, own_v, *rest, sems = refs
    rows, _, cells = forcing.shape
    fields = bounds[1] - bounds[0]
    count, per_row = weights.shape[:2]
    block = weights.shape[-1]
    extent = rows + 2 * halo
    lo, hi = halo, halo + rows

    @pl.when(flags[0] == number)
    def _():
        mine = slice(*bounds)
        theirs = slice(None) if number else mine
        beside = beside_matrix(cells)
        top = jnp.where(flags[1] == 0, 0.0, 1.0)
        bottom = jnp.where(flags[1] == flags[2] - 1, 0.0, 1.0)
        for edge, start in ((upper, 0), (lower, hi)):
            parts = edge[halo:].astype(jnp.float32).reshape(-1, cells)
            k_v[start:start + halo, :] = parts[:halo] + parts[halo:2 * halo] + parts[2 * halo:3 * halo]
        k_v[lo:hi, :] = kappa[...]

        def entry(i):
            if i < lo:
                return upper[i, theirs].astype(jnp.float32)
            if i >= hi:
                return lower[i - hi, theirs].astype(jnp.float32)
            value = forcing[i - lo, mine]
            if number:
                value = value + incoming[i - lo].astype(jnp.float32)
            return value

        def step(i, here, north, south, east_west):
            if i == lo:
                north = north * top
            if i == lo - 1:
                south = south * top
            if i == hi:
                north = north * bottom
            if i == hi - 1:
                south = south * bottom
            return here + k_v[i:i + 1, :] * ((north + south) + (east_west - 4.0 * here))

        def pair_beside(a, b):
            both = jnp.concatenate([a.astype(jnp.bfloat16), b.astype(jnp.bfloat16)], axis=1)
            total = jnp.dot(both, beside, preferred_element_type=jnp.float32)
            return total[:, :cells], total[:, cells:]

        there, after = None, entry(0)
        for i in range(0, extent, 2):
            before, here, there = there, after, entry(i + 1)
            after = entry(i + 2) if i + 2 < extent else None
            ew_here, ew_there = pair_beside(here, there)
            if i > 0:
                once[i] = step(i, here, before, there, ew_here)
            if i + 2 < extent:
                once[i + 1] = step(i + 1, there, here, after, ew_there)
        for i in range(2, extent - 2, 2):
            here, there = once[i], once[i + 1]
            ew_here, ew_there = pair_beside(here, there)
            out = i // 2 - 1
            smooth[out, :, :cells] = step(i, here, once[i - 1], there, ew_here).astype(jnp.bfloat16)
            smooth[out, :, cells:] = step(i + 1, there, here, once[i + 2], ew_there).astype(jnp.bfloat16)

        half = (halo - EDGE) * cells // block
        block_rows = block // cells
        stores = []
        if has_next:
            up_s, down_s, pack = rest
            parts = following[rows].astype(jnp.float32)
            parts = [parts[p * rows:(p + 1) * rows] for p in range(3)]
            tail = (up_s.shape[0] - halo, fields, cells)
            up_s[halo:] = joined([part[:halo] for part in parts], pack).reshape(tail)
            down_s[halo:] = joined([part[rows - halo:] for part in parts], pack).reshape(tail)
        for j in range(count):
            total = None
            for k in range(per_row):
                source = smooth[offsets[k, j] + (j + half)]
                term = lax.dot_general(
                    source, weights[j, k], (((1,), (0 if number else 1,)), ((), ())),
                    preferred_element_type=jnp.float32,
                )
                total = term if total is None else total + term
            for r in range(block_rows):
                row = j * block_rows + r
                value = total[:, r * cells:(r + 1) * cells].astype(jnp.bfloat16)
                own_v[row] = value
                if has_next:
                    entry_next = value.astype(jnp.float32) + following[row, mine].astype(jnp.float32)
                    if row < halo:
                        up_s[row] = entry_next.astype(jnp.bfloat16)
                    if row >= rows - halo:
                        down_s[row - (rows - halo)] = entry_next.astype(jnp.bfloat16)
                    if row == halo - 1:
                        stores.append(pltpu.make_async_copy(up_s, up_out, sems.at[0]))
                        stores[-1].start()
        if has_next:
            ends = [
                pltpu.make_async_copy(down_s, down_out, sems.at[1]),
                pltpu.make_async_copy(own_v, own_out, sems.at[2]),
            ]
            start_all(ends)
            wait_all(stores + ends)

    if not has_next:
        turned, = rest
        for i, kept in enumerate(saved):
            @pl.when(flags[0] == i)
            def _(kept=kept):
                copy = pltpu.make_async_copy(kept, own_v, sems.at[0])
                copy.start()
                copy.wait()

        step_rows = 16
        for y in range(0, rows, step_rows):
            turned[:, y:y + step_rows, :] = jnp.swapaxes(own_v[y:y + step_rows], 0, 1)
        copy = pltpu.make_async_copy(turned, result.at[pl.ds(bounds[0], fields)], sems.at[1])
        copy.start()
        copy.wait()


def section(number, bounds, halo, flags, offsets, kappa, forcing, arrived, following, weights, saved, result):
    rows, total, cells = forcing.shape
    fields = bounds[1] - bounds[0]
    count, per_row, block, _ = weights.shape
    has_next = following is not None
    operands = [flags, offsets, kappa, in_vmem(forcing)] + arrived
    if has_next:
        operands.append(following)
    specs = [SMEM] * 2 + [VMEM] * (len(operands) - 2)
    operands.append(in_vmem(weights))
    specs.append(VMEM)
    extent = rows + 2 * halo
    packed = -(-3 * halo // fields)
    scratch = [
        pltpu.VMEM((extent, cells), jnp.float32),
        pltpu.VMEM((extent, fields, cells), jnp.float32),
        pltpu.VMEM(((extent - 2 * EDGE) * cells // block, fields, block), jnp.bfloat16),
        pltpu.VMEM((rows, fields, cells), jnp.bfloat16),
    ]
    aliases = {}
    if has_next:
        outs = [jax.ShapeDtypeStruct((n, fields, cells), jnp.bfloat16) for n in (rows, halo + packed, halo + packed)]
        out_specs = [ANY] * 3
        scratch += [pltpu.VMEM((halo + packed, fields, cells), jnp.bfloat16)] * 2
        scratch.append(pltpu.VMEM((packed * fields, cells), jnp.float32))
    else:
        outs = [jax.ShapeDtypeStruct((total, rows, cells), jnp.bfloat16)]
        out_specs = [HBM]
        scratch += [pltpu.VMEM((fields, rows, cells), jnp.bfloat16)]
        operands += [in_hbm(value) for value in saved]
        specs += [HBM] * len(saved)
        if result is not None:
            aliases = {len(operands): 0}
            operands.append(result)
            specs.append(HBM)
    scratch.append(pltpu.SemaphoreType.DMA((3,)))
    return pl.pallas_call(
        functools.partial(section_kernel, number, bounds, halo, len(saved), has_next),
        in_specs=specs,
        out_shape=outs,
        out_specs=out_specs,
        input_output_aliases=aliases,
        scratch_shapes=scratch,
        compiler_params=pltpu.CompilerParams(vmem_limit_bytes=LIMIT),
        cost_estimate=pl.CostEstimate(
            flops=WEIGHT * 2 * count * per_row * block * block * fields, bytes_accessed=weights.size * 2, transcendentals=0
        ),
    )(*operands)


def local(forcing, kappa, col_blocks, remap_weights):
    n_tile = lax.axis_size("tile")
    n_section = lax.axis_size("comp")
    tile_pos = lax.axis_index("tile")
    section_pos = lax.axis_index("comp")
    weights = remap_weights[0]
    count, block = weights.shape[0], weights.shape[-1]
    rows, cells = forcing.shape[-2:]
    half = count // 2
    halo = half * block // cells + EDGE
    flags = jnp.stack([section_pos, tile_pos, jnp.full_like(tile_pos, n_tile)]).astype(jnp.int32)

    def place(s, t):
        return s * n_tile + t % n_tile

    def send(value, source, target, shift):
        pairs = [(place(source, t), place(target, t + shift)) for t in range(n_tile)]
        others = [s for s in range(n_section) if s not in (source, target)]
        if source == target:
            rest = list(zip(others, others[1:] + others[:1]))
        elif source ^ 1 == target and n_section % 2 == 0:
            rest = [(target, source)] + [(s, s ^ 1) for s in others]
        else:
            rest = []
        pairs += [(place(s, t), place(to, t)) for s, to in rest for t in range(n_tile)]
        return lax.ppermute(value, AXES, pairs)

    offsets, by_row, narrow, again, first, last = prepare(
        flags, col_blocks[0].T, forcing.reshape(-1, rows, cells), kappa[0], halo
    )
    total = by_row.shape[1]
    marks = [total * sum(SHARES[:c]) // sum(SHARES) for c in range(len(SHARES) + 1)]
    chunks = list(zip(marks[:-1], marks[1:]))
    arrivals = [[send(last, 0, 0, 1), send(first, 0, 0, -1)]] * len(chunks)
    weights, again = load(flags, weights, again)
    following = [
        lax.ppermute(narrow, "comp", [(s, s ^ 1) for s in range(n_section) if s ^ 1 < n_section]),
        lax.ppermute(again, "comp", [(s + 1, s) for s in range(1, n_section - 1, 2)]),
    ]
    owns = [[] for _ in chunks]
    result = None
    for s in range(n_section):
        last = s + 1 == n_section
        leaving = []
        for c, bounds in enumerate(chunks):
            parts = section(
                s, bounds, halo, flags, offsets, kappa[0], by_row, arrivals[c], None if last else following[s % 2],
                weights, owns[c] if last else [], result,
            )
            if last:
                result = parts[0]
                continue
            own, up, down = parts
            owns[c].append(own)
            leaving.append([send(part, s, s + 1, shift) for part, shift in ((own, 0), (down, 1), (up, -1))])
        arrivals = leaving
    return result.reshape(forcing.shape)


def solution(mesh):
    placed = (
        P("comp", None, None, "tile", None),
        P("comp", "tile", None),
        P("comp", "tile", None),
        P("comp", "tile", None, None, None),
    )
    return jax.shard_map(
        local,
        mesh=mesh,
        in_specs=placed,
        out_specs=P("comp", None, None, "tile", None),
        check_vma=False,
    )
```

time: 97.3 us -> 89.6 us (0.921)
  waiting for transfers between devices: 12.4 us -> 4.15 us
  starting transfers between devices: 56.7 us -> 58.2 us
    ppermute x22 -> x20, waiting for transfers between devices: 12.4 us -> 4.14 us  [send(): return lax.ppermute(value, AXES, pairs)]
    ppermute x22 -> x20, starting transfers between devices: 55.2 us -> 56.7 us  [send(): return lax.ppermute(value, AXES, pairs)]
  transfers between devices with their start and end apart: 24 -> 22, of which waited for: 5 -> 2; matrix products, arithmetic and copies ran while one was open for 0% -> 0% of each run, Pallas kernels for 18% -> 21%
where the time goes in v2:
time: 89.6 us; the launch traced here: 89.3 us
  starting transfers between devices  58.2 us (65%)
  Pallas kernels  26.4 us (29%)
  waiting for transfers between devices  4.15 us (5%)
    ppermute x20, starting transfers between devices, send(): return lax.ppermute(value, AXES, pairs)  56.7 us
    pallas_call x8, Pallas kernels, section(): pl.pallas_call(functools.partial(section_kernel, number, bounds, halo, le...  14.1 us
    pallas_call x1, Pallas kernels, load(): pl.pallas_call(load_kernel, in_specs=[SMEM, HBM, ANY], out_shape=[pltpu.V...  9.7 us
    ppermute x20, waiting for transfers between devices, send(): return lax.ppermute(value, AXES, pairs)  4.14 us
    pallas_call x1, Pallas kernels, prepare(): pl.pallas_call(prepare_kernel, in_specs=[SMEM, HBM, HBM, HBM], out_shape=...  2.63 us
  transfers between devices with their start and end apart: 22, of which 2 were waited for; matrix products, arithmetic and copies ran while one was open for 0% of the time, Pallas kernels for 21%

profile of v2, /device:TPU:3, one launch (start us, length us, event | category | flops | bytes accessed | tf_op | source)
XLA Modules:
  0.0 89.3 jit_solution(1502538472309200290)
XLA Ops:
  0.0 0.1 pad_add_fusion.flags
  0.1 2.6 %shard_map.46 = (s32[4,16]{1,0:T(4,128)S(1)}, f32[32,128,128]{2,1,0:T(8,128)S(1)}, bf16[33,128,128]{2,1,0:T(8,128)(2,1)S(1)}, bf16[33,128,128]{2,1,0:T(8,128)(2,...) custom-call(s32[3]{0:T(128)S(1)} %pad_add_fusion.flags, s32[4,16]{1,0:T(4,128)} %bitcast.20, ...), custom_call_target="tpu_custom_call" | custom-call | bytes 6291456 | tf_op jit(solution)/shard_map/pallas_call | solution.py:100
  2.7 0.7 collective-permute-start.2
  3.5 0.0 collective-permute-start
  3.5 1.4 %collective-permute-start.1 = (bf16[19,128,128]{2,1,0:T(8,128)(2,1)S(1)}, bf16[19,128,128]{2,1,0:T(8,128)(2,1)S(1)}, u32[]{:S(2)}, u32[]{:S(2)}) collective-permute-start(bf16[19,128,128]{2,1,0:T(8,128)(2,1)S(1)} %get-tuple-element.34), channel_id=1, source_target_pairs={{0,7},{1,0},{2,1},{3,2},{4,3},{5,4},{6,5},{7,6},{8,16},{9,17},{10,... | collective-permute-start | bytes 1867784 | tf_op jit(solution)/shard_map/ppermute | solution.py:367
  4.9 9.7 %shard_map.47 = (bf16[16,4,256,256]{3,2,1,0:T(8,128)(2,1)S(1)}, bf16[33,128,128]{2,1,0:T(8,128)(2,1)S(1)}) custom-call(s32[3]{0:T(128)S(1)} %pad_add_fusion.flags, bf16[16,4,256,256]{3,2,1,0:T(8,128)(2,1)} %bitcast.18, bf16[33,128,128]{2,1,0:T(8,128)(2,1)S(1)} %get-tuple-element.36.refs_0_), custom_call_target="tpu_custom_call", output_to_operand_aliasing={{1}: (2, {})} | custom-call | bytes 16777216 | tf_op jit(solution)/shard_map/pallas_call | solution.py:140
  14.6 0.7 collective-permute-start.6
  15.3 0.0 collective-permute-done.refs_0_
  15.3 2.0 %collective-permute-done.1.refs_1_ = bf16[19,128,128]{2,1,0:T(8,128)(2,1)S(1)} collective-permute-done((bf16[19,128,128]{2,1,0:T(8,128)(2,1)S(1)}, bf16[19,128,128]{2,1,0:T(8,128)(2,1)S(1)}, u32[]{:S(2)}, u32[]{:S(2)}) %collective-permute-start.1) | collective-permute-done | bytes 622624 | tf_op jit(solution)/shard_map/ppermute | solution.py:367
  17.3 0.0 collective-permute-done.2.refs_2_.refs_3_
  17.3 0.0 copy-done
  17.3 0.6 shard_map.51
  17.9 0.0 copy-start.2
  17.9 2.6 %collective-permute-start.14 = (bf16[19,64,128]{2,1,0:T(8,128)(2,1)S(1)}, bf16[19,64,128]{2,1,0:T(8,128)(2,1)S(1)}, u32[]{:S(2)}, u32[]{:S(2)}) collective-permute-start(bf16[19,64,128]{2,1,0:T(8,128)(2,1)S(1)} %get-tuple-element.49), channel_id=1, source_target_pairs={{0,9},{1,10},{2,11},{3,12},{4,13},{5,14},{6,15},{7,8},{8,0},{9,1},... | collective-permute-start | bytes 933896 | tf_op jit(solution)/shard_map/ppermute | solution.py:367
  20.5 0.1 collective-permute-start.15
  20.6 0.4 collective-permute-start.13
  21.0 0.6 shard_map.48
  21.7 0.0 copy-done.2
  21.7 0.0 copy-start.1
  21.7 0.1 collective-permute-start.4
  21.8 0.0 collective-permute-done.6.refs_3_
  21.8 8.2 %collective-permute-start.5 = (bf16[19,64,128]{2,1,0:T(8,128)(2,1)S(1)}, bf16[19,64,128]{2,1,0:T(8,128)(2,1)S(1)}, u32[]{:S(2)}, u32[]{:S(2)}) collective-permute-start(bf16[19,64,128]{2,1,0:T(8,128)(2,1)S(1)} %get-tuple-element.40), channel_id=1, source_target_pairs={{0,15},{1,8},{2,9},{3,10},{4,11},{5,12},{6,13},{7,14},{8,0},{9,1},... | collective-permute-start | bytes 933896 | tf_op jit(solution)/shard_map/ppermute | solution.py:367
  30.0 0.0 collective-permute-done.14.refs_1_
  30.0 0.0 collective-permute-start.3
  30.0 0.0 collective-permute-done.15.refs_2_
  30.0 0.0 collective-permute-done.13.refs_0_
  30.0 0.6 shard_map.52
  30.6 0.0 copy-done.1
  30.6 0.0 copy-start.3
  30.6 0.7 collective-permute-start.17
  31.3 0.7 collective-permute-start.18
  32.0 0.0 collective-permute-done.4.refs_1_
  32.0 0.7 collective-permute-start.16
  32.7 0.0 collective-permute-done.5.refs_2_
  32.7 0.0 collective-permute-done.3.refs_0_
  32.8 0.8 shard_map.49
  33.6 0.7 collective-permute-start.8
  34.3 0.7 collective-permute-start.9
  34.9 0.0 collective-permute-done.17.refs_1_
  35.0 0.7 collective-permute-start.7
  35.7 0.0 collective-permute-done.18.refs_2_
  35.7 0.0 collective-permute-done.16.refs_0_
  35.7 0.6 shard_map.53
  36.3 29.8 %collective-permute-start.20 = (bf16[19,64,128]{2,1,0:T(8,128)(2,1)S(1)}, bf16[19,64,128]{2,1,0:T(8,128)(2,1)S(1)}, u32[]{:S(2)}, u32[]{:S(2)}) collective-permute-start(bf16[19,64,128]{2,1,0:T(8,128)(2,1)S(1)} %get-tuple-element.55), channel_id=1, source_target_pairs={{16,25},{17,26},{18,27},{19,28},{20,29},{21,30},{22,31},{23,24},{2... | collective-permute-start | bytes 933896 | tf_op jit(solution)/shard_map/ppermute | solution.py:367
  66.1 0.1 collective-permute-start.21
  66.2 0.0 collective-permute-done.8.refs_1_
  66.2 1.6 %collective-permute-start.19 = (bf16[32,64,128]{2,1,0:T(8,128)(2,1)S(1)}, bf16[32,64,128]{2,1,0:T(8,128)(2,1)S(1)}, u32[]{:S(2)}, u32[]{:S(2)}) collective-permute-start(bf16[32,64,128]{2,1,0:T(8,128)(2,1)S(1)} %get-tuple-element.54.refs_6_), channel_id=1, source_target_pairs={{16,24},{17,25},{18,26},{19,27},{20,28},{21,29},{22,30},{23,31},{2... | collective-permute-start | bytes 1572872 | tf_op jit(solution)/shard_map/ppermute | solution.py:367
  67.8 0.0 collective-permute-done.9.refs_2_
  67.8 0.0 collective-permute-done.7.refs_0_
  67.8 0.6 shard_map.50
  68.4 0.0 copy-done.5
  68.4 0.0 copy-start.6
  68.4 6.7 %collective-permute-start.11 = (bf16[19,64,128]{2,1,0:T(8,128)(2,1)S(1)}, bf16[19,64,128]{2,1,0:T(8,128)(2,1)S(1)}, u32[]{:S(2)}, u32[]{:S(2)}) collective-permute-start(bf16[19,64,128]{2,1,0:T(8,128)(2,1)S(1)} %get-tuple-element.46), channel_id=1, source_target_pairs={{16,25},{17,26},{18,27},{19,28},{20,29},{21,30},{22,31},{23,24},{2... | collective-permute-start | bytes 933896 | tf_op jit(solution)/shard_map/ppermute | solution.py:367
  75.1 0.1 collective-permute-start.12
  75.1 0.0 collective-permute-done.20.refs_1_
  75.1 1.6 %collective-permute-start.10 = (bf16[32,64,128]{2,1,0:T(8,128)(2,1)S(1)}, bf16[32,64,128]{2,1,0:T(8,128)(2,1)S(1)}, u32[]{:S(2)}, u32[]{:S(2)}) collective-permute-start(bf16[32,64,128]{2,1,0:T(8,128)(2,1)S(1)} %get-tuple-element.45.refs_6_), channel_id=1, source_target_pairs={{16,24},{17,25},{18,26},{19,27},{20,28},{21,29},{22,30},{23,31},{2... | collective-permute-start | bytes 1572872 | tf_op jit(solution)/shard_map/ppermute | solution.py:367
  76.7 0.0 collective-permute-done.21.refs_2_
  76.7 0.0 collective-permute-done.19.refs_0_
  76.7 5.2 %shard_map.54.refs_7_ = bf16[128,32,128]{2,1,0:T(8,128)(2,1)} custom-call(s32[3]{0:T(128)S(1)} %pad_add_fusion.flags, s32[4,16]{1,0:T(4,128)S(1)} %get-tuple-element.31.offsets, f32[32,128]{1,0:T(8,128)S(1)} %bitcast.16, f32[32,128,128]{2,1,0:T(8,128)S(1)} %get-tuple-element.32.forcing, bf16[32,64,128]{2,1,0:T(8,128)(2,1)S(1)} %collective-permute-done.19.refs_0_, ...), custom_call_target="tpu_custom_call" | custom-call | flops 10737418240 | bytes 8388608 | tf_op jit(solution)/shard_map/pallas_call | solution.py:328
  82.0 0.0 copy-done.6
  82.0 0.0 collective-permute-done.11.refs_1_
  82.0 2.1 %collective-permute-done.12.refs_2_ = bf16[19,64,128]{2,1,0:T(8,128)(2,1)S(1)} collective-permute-done((bf16[19,64,128]{2,1,0:T(8,128)(2,1)S(1)}, bf16[19,64,128]{2,1,0:T(8,128)(2,1)S(1)}, u32[]{:S(2)}, u32[]{:S(2)}) %collective-permute-start.12) | collective-permute-done | bytes 311328 | tf_op jit(solution)/shard_map/ppermute | solution.py:367
  84.1 0.0 collective-permute-done.10.refs_0_
  84.1 5.0 %shard_map.55 = bf16[128,32,128]{2,1,0:T(8,128)(2,1)} custom-call(s32[3]{0:T(128)S(1)} %pad_add_fusion.flags, s32[4,16]{1,0:T(4,128)S(1)} %get-tuple-element.31.offsets, f32[32,128]{1,0:T(8,128)S(1)} %bitcast.17, f32[32,128,128]{2,1,0:T(8,128)S(1)} %get-tuple-element.32.forcing, ...), custom_call_target="tpu_custom_call", output_to_operand_aliasing={{}: (11, {})} | custom-call | flops 10737418240 | bytes 8388608 | tf_op jit(solution)/shard_map/pallas_call | solution.py:328
  (5 shorter events, 0.0 us)
Async XLA Ops:
  2.7 14.6 %collective-permute-start.2 = (bf16[33,128,128]{2,1,0:T(8,128)(2,1)S(1)}, bf16[33,128,128]{2,1,0:T(8,128)(2,1)S(1)}, u32[]{:S(2)}, u32[]{:S(2)}) collective-permute-start(bf16[33,128,128]{2,1,0:T(8,128)(2,1)S(1)} %get-tuple-element.35), channel_id=1, source_target_pairs={{0,8},{8,0},{16,24},{24,16},{1,9},{9,1},{17,25},{25,17},{2,10},{10... | collective-permute-start | bytes 3244040 | tf_op jit(solution)/shard_map/ppermute | solution.py:378
  3.5 11.9 %collective-permute-start = (bf16[19,128,128]{2,1,0:T(8,128)(2,1)S(1)}, bf16[19,128,128]{2,1,0:T(8,128)(2,1)S(1)}, u32[]{:S(2)}, u32[]{:S(2)}) collective-permute-start(bf16[19,128,128]{2,1,0:T(8,128)(2,1)S(1)} %get-tuple-element.33), channel_id=1, source_target_pairs={{0,1},{1,2},{2,3},{3,4},{4,5},{5,6},{6,7},{7,0},{8,16},{9,17},{10,... | collective-permute-start | bytes 1867784 | tf_op jit(solution)/shard_map/ppermute | solution.py:367
  3.5 13.8 %collective-permute-start.1 = (bf16[19,128,128]{2,1,0:T(8,128)(2,1)S(1)}, bf16[19,128,128]{2,1,0:T(8,128)(2,1)S(1)}, u32[]{:S(2)}, u32[]{:S(2)}) collective-permute-start(bf16[19,128,128]{2,1,0:T(8,128)(2,1)S(1)} %get-tuple-element.34), channel_id=1, source_target_pairs={{0,7},{1,0},{2,1},{3,2},{4,3},{5,4},{6,5},{7,6},{8,16},{9,17},{10,... | collective-permute-start | bytes 1867784 | tf_op jit(solution)/shard_map/ppermute | solution.py:367
  4.9 12.4 %copy-start = (f32[1,32,128]{2,1,0:T(8,128)S(1)}, f32[1,32,128]{2,1,0:T(8,128)}, u32[]{:S(2)}) copy-start(f32[1,32,128]{2,1,0:T(8,128)} %param.5) | copy-start | bytes 49156
  14.6 7.2 %collective-permute-start.6 = (bf16[33,128,128]{2,1,0:T(8,128)(2,1)S(1)}, bf16[33,128,128]{2,1,0:T(8,128)(2,1)S(1)}, u32[]{:S(2)}, u32[]{:S(2)}) collective-permute-start(bf16[33,128,128]{2,1,0:T(8,128)(2,1)S(1)} %get-tuple-element.41), channel_id=1, source_target_pairs={{16,8},{17,9},{18,10},{19,11},{20,12},{21,13},{22,14},{23,15}} | collective-permute-start | bytes 3244040 | tf_op jit(solution)/shard_map/ppermute | solution.py:379
  17.9 3.7 %copy-start.2 = (bf16[32,64,128]{2,1,0:T(8,128)(2,1)}, bf16[32,64,128]{2,1,0:T(8,128)(2,1)S(1)}, u32[]{:S(2)}) copy-start(bf16[32,64,128]{2,1,0:T(8,128)(2,1)S(1)} %get-tuple-element.48.refs_4_) | copy-start | bytes 1572868
  17.9 12.1 %collective-permute-start.14 = (bf16[19,64,128]{2,1,0:T(8,128)(2,1)S(1)}, bf16[19,64,128]{2,1,0:T(8,128)(2,1)S(1)}, u32[]{:S(2)}, u32[]{:S(2)}) collective-permute-start(bf16[19,64,128]{2,1,0:T(8,128)(2,1)S(1)} %get-tuple-element.49), channel_id=1, source_target_pairs={{0,9},{1,10},{2,11},{3,12},{4,13},{5,14},{6,15},{7,8},{8,0},{9,1},... | collective-permute-start | bytes 933896 | tf_op jit(solution)/shard_map/ppermute | solution.py:367
  20.5 9.5 %collective-permute-start.15 = (bf16[19,64,128]{2,1,0:T(8,128)(2,1)S(1)}, bf16[19,64,128]{2,1,0:T(8,128)(2,1)S(1)}, u32[]{:S(2)}, u32[]{:S(2)}) collective-permute-start(bf16[19,64,128]{2,1,0:T(8,128)(2,1)S(1)} %get-tuple-element.50), channel_id=1, source_target_pairs={{0,15},{1,8},{2,9},{3,10},{4,11},{5,12},{6,13},{7,14},{8,0},{9,1},... | collective-permute-start | bytes 933896 | tf_op jit(solution)/shard_map/ppermute | solution.py:367
  20.6 9.4 %collective-permute-start.13 = (bf16[32,64,128]{2,1,0:T(8,128)(2,1)S(1)}, bf16[32,64,128]{2,1,0:T(8,128)(2,1)S(1)}, u32[]{:S(2)}, u32[]{:S(2)}) collective-permute-start(bf16[32,64,128]{2,1,0:T(8,128)(2,1)S(1)} %get-tuple-element.48.refs_4_), channel_id=1, source_target_pairs={{0,8},{1,9},{2,10},{3,11},{4,12},{5,13},{6,14},{7,15},{8,0},{9,1},... | collective-permute-start | bytes 1572872 | tf_op jit(solution)/shard_map/ppermute | solution.py:367
  21.7 9.0 %copy-start.1 = (bf16[32,64,128]{2,1,0:T(8,128)(2,1)}, bf16[32,64,128]{2,1,0:T(8,128)(2,1)S(1)}, u32[]{:S(2)}) copy-start(bf16[32,64,128]{2,1,0:T(8,128)(2,1)S(1)} %get-tuple-element.38.refs_4_) | copy-start | bytes 1572868
  21.7 10.3 %collective-permute-start.4 = (bf16[19,64,128]{2,1,0:T(8,128)(2,1)S(1)}, bf16[19,64,128]{2,1,0:T(8,128)(2,1)S(1)}, u32[]{:S(2)}, u32[]{:S(2)}) collective-permute-start(bf16[19,64,128]{2,1,0:T(8,128)(2,1)S(1)} %get-tuple-element.39), channel_id=1, source_target_pairs={{0,9},{1,10},{2,11},{3,12},{4,13},{5,14},{6,15},{7,8},{8,0},{9,1},... | collective-permute-start | bytes 933896 | tf_op jit(solution)/shard_map/ppermute | solution.py:367
  21.8 10.9 %collective-permute-start.5 = (bf16[19,64,128]{2,1,0:T(8,128)(2,1)S(1)}, bf16[19,64,128]{2,1,0:T(8,128)(2,1)S(1)}, u32[]{:S(2)}, u32[]{:S(2)}) collective-permute-start(bf16[19,64,128]{2,1,0:T(8,128)(2,1)S(1)} %get-tuple-element.40), channel_id=1, source_target_pairs={{0,15},{1,8},{2,9},{3,10},{4,11},{5,12},{6,13},{7,14},{8,0},{9,1},... | collective-permute-start | bytes 933896 | tf_op jit(solution)/shard_map/ppermute | solution.py:367
  30.0 2.8 %collective-permute-start.3 = (bf16[32,64,128]{2,1,0:T(8,128)(2,1)S(1)}, bf16[32,64,128]{2,1,0:T(8,128)(2,1)S(1)}, u32[]{:S(2)}, u32[]{:S(2)}) collective-permute-start(bf16[32,64,128]{2,1,0:T(8,128)(2,1)S(1)} %get-tuple-element.38.refs_4_), channel_id=1, source_target_pairs={{0,8},{1,9},{2,10},{3,11},{4,12},{5,13},{6,14},{7,15},{8,0},{9,1},... | collective-permute-start | bytes 1572872 | tf_op jit(solution)/shard_map/ppermute | solution.py:367
  30.6 2.9 %copy-start.3 = (bf16[32,64,128]{2,1,0:T(8,128)(2,1)}, bf16[32,64,128]{2,1,0:T(8,128)(2,1)S(1)}, u32[]{:S(2)}) copy-start(bf16[32,64,128]{2,1,0:T(8,128)(2,1)S(1)} %get-tuple-element.51.refs_5_) | copy-start | bytes 1572868
  30.6 4.3 %collective-permute-start.17 = (bf16[19,64,128]{2,1,0:T(8,128)(2,1)S(1)}, bf16[19,64,128]{2,1,0:T(8,128)(2,1)S(1)}, u32[]{:S(2)}, u32[]{:S(2)}) collective-permute-start(bf16[19,64,128]{2,1,0:T(8,128)(2,1)S(1)} %get-tuple-element.52), channel_id=1, source_target_pairs={{8,17},{9,18},{10,19},{11,20},{12,21},{13,22},{14,23},{15,16}} | collective-permute-start | bytes 933896 | tf_op jit(solution)/shard_map/ppermute | solution.py:367
  31.3 4.3 %collective-permute-start.18 = (bf16[19,64,128]{2,1,0:T(8,128)(2,1)S(1)}, bf16[19,64,128]{2,1,0:T(8,128)(2,1)S(1)}, u32[]{:S(2)}, u32[]{:S(2)}) collective-permute-start(bf16[19,64,128]{2,1,0:T(8,128)(2,1)S(1)} %get-tuple-element.53), channel_id=1, source_target_pairs={{8,23},{9,16},{10,17},{11,18},{12,19},{13,20},{14,21},{15,22}} | collective-permute-start | bytes 933896 | tf_op jit(solution)/shard_map/ppermute | solution.py:367
  32.0 3.6 %collective-permute-start.16 = (bf16[32,64,128]{2,1,0:T(8,128)(2,1)S(1)}, bf16[32,64,128]{2,1,0:T(8,128)(2,1)S(1)}, u32[]{:S(2)}, u32[]{:S(2)}) collective-permute-start(bf16[32,64,128]{2,1,0:T(8,128)(2,1)S(1)} %get-tuple-element.51.refs_5_), channel_id=1, source_target_pairs={{8,16},{9,17},{10,18},{11,19},{12,20},{13,21},{14,22},{15,23}} | collective-permute-start | bytes 1572872 | tf_op jit(solution)/shard_map/ppermute | solution.py:367
  33.6 2.7 %copy-start.4 = (bf16[32,64,128]{2,1,0:T(8,128)(2,1)}, bf16[32,64,128]{2,1,0:T(8,128)(2,1)S(1)}, u32[]{:S(2)}) copy-start(bf16[32,64,128]{2,1,0:T(8,128)(2,1)S(1)} %get-tuple-element.42.refs_5_) | copy-start | bytes 1572868
  33.6 32.6 %collective-permute-start.8 = (bf16[19,64,128]{2,1,0:T(8,128)(2,1)S(1)}, bf16[19,64,128]{2,1,0:T(8,128)(2,1)S(1)}, u32[]{:S(2)}, u32[]{:S(2)}) collective-permute-start(bf16[19,64,128]{2,1,0:T(8,128)(2,1)S(1)} %get-tuple-element.43), channel_id=1, source_target_pairs={{8,17},{9,18},{10,19},{11,20},{12,21},{13,22},{14,23},{15,16}} | collective-permute-start | bytes 933896 | tf_op jit(solution)/shard_map/ppermute | solution.py:367
  34.3 33.5 %collective-permute-start.9 = (bf16[19,64,128]{2,1,0:T(8,128)(2,1)S(1)}, bf16[19,64,128]{2,1,0:T(8,128)(2,1)S(1)}, u32[]{:S(2)}, u32[]{:S(2)}) collective-permute-start(bf16[19,64,128]{2,1,0:T(8,128)(2,1)S(1)} %get-tuple-element.44), channel_id=1, source_target_pairs={{8,23},{9,16},{10,17},{11,18},{12,19},{13,20},{14,21},{15,22}} | collective-permute-start | bytes 933896 | tf_op jit(solution)/shard_map/ppermute | solution.py:367
  35.0 32.8 %collective-permute-start.7 = (bf16[32,64,128]{2,1,0:T(8,128)(2,1)S(1)}, bf16[32,64,128]{2,1,0:T(8,128)(2,1)S(1)}, u32[]{:S(2)}, u32[]{:S(2)}) collective-permute-start(bf16[32,64,128]{2,1,0:T(8,128)(2,1)S(1)} %get-tuple-element.42.refs_5_), channel_id=1, source_target_pairs={{8,16},{9,17},{10,18},{11,19},{12,20},{13,21},{14,22},{15,23}} | collective-permute-start | bytes 1572872 | tf_op jit(solution)/shard_map/ppermute | solution.py:367
  36.3 32.1 %copy-start.5 = (bf16[32,64,128]{2,1,0:T(8,128)(2,1)}, bf16[32,64,128]{2,1,0:T(8,128)(2,1)S(1)}, u32[]{:S(2)}) copy-start(bf16[32,64,128]{2,1,0:T(8,128)(2,1)S(1)} %get-tuple-element.54.refs_6_) | copy-start | bytes 1572868
  36.3 38.8 %collective-permute-start.20 = (bf16[19,64,128]{2,1,0:T(8,128)(2,1)S(1)}, bf16[19,64,128]{2,1,0:T(8,128)(2,1)S(1)}, u32[]{:S(2)}, u32[]{:S(2)}) collective-permute-start(bf16[19,64,128]{2,1,0:T(8,128)(2,1)S(1)} %get-tuple-element.55), channel_id=1, source_target_pairs={{16,25},{17,26},{18,27},{19,28},{20,29},{21,30},{22,31},{23,24},{2... | collective-permute-start | bytes 933896 | tf_op jit(solution)/shard_map/ppermute | solution.py:367
  66.1 10.6 %collective-permute-start.21 = (bf16[19,64,128]{2,1,0:T(8,128)(2,1)S(1)}, bf16[19,64,128]{2,1,0:T(8,128)(2,1)S(1)}, u32[]{:S(2)}, u32[]{:S(2)}) collective-permute-start(bf16[19,64,128]{2,1,0:T(8,128)(2,1)S(1)} %get-tuple-element.56), channel_id=1, source_target_pairs={{16,31},{17,24},{18,25},{19,26},{20,27},{21,28},{22,29},{23,30},{2... | collective-permute-start | bytes 933896 | tf_op jit(solution)/shard_map/ppermute | solution.py:367
  66.2 10.5 %collective-permute-start.19 = (bf16[32,64,128]{2,1,0:T(8,128)(2,1)S(1)}, bf16[32,64,128]{2,1,0:T(8,128)(2,1)S(1)}, u32[]{:S(2)}, u32[]{:S(2)}) collective-permute-start(bf16[32,64,128]{2,1,0:T(8,128)(2,1)S(1)} %get-tuple-element.54.refs_6_), channel_id=1, source_target_pairs={{16,24},{17,25},{18,26},{19,27},{20,28},{21,29},{22,30},{23,31},{2... | collective-permute-start | bytes 1572872 | tf_op jit(solution)/shard_map/ppermute | solution.py:367
  68.4 13.6 %copy-start.6 = (bf16[32,64,128]{2,1,0:T(8,128)(2,1)}, bf16[32,64,128]{2,1,0:T(8,128)(2,1)S(1)}, u32[]{:S(2)}) copy-start(bf16[32,64,128]{2,1,0:T(8,128)(2,1)S(1)} %get-tuple-element.45.refs_6_) | copy-start | bytes 1572868
  68.4 13.6 %collective-permute-start.11 = (bf16[19,64,128]{2,1,0:T(8,128)(2,1)S(1)}, bf16[19,64,128]{2,1,0:T(8,128)(2,1)S(1)}, u32[]{:S(2)}, u32[]{:S(2)}) collective-permute-start(bf16[19,64,128]{2,1,0:T(8,128)(2,1)S(1)} %get-tuple-element.46), channel_id=1, source_target_pairs={{16,25},{17,26},{18,27},{19,28},{20,29},{21,30},{22,31},{23,24},{2... | collective-permute-start | bytes 933896 | tf_op jit(solution)/shard_map/ppermute | solution.py:367
  75.1 9.1 %collective-permute-start.12 = (bf16[19,64,128]{2,1,0:T(8,128)(2,1)S(1)}, bf16[19,64,128]{2,1,0:T(8,128)(2,1)S(1)}, u32[]{:S(2)}, u32[]{:S(2)}) collective-permute-start(bf16[19,64,128]{2,1,0:T(8,128)(2,1)S(1)} %get-tuple-element.47), channel_id=1, source_target_pairs={{16,31},{17,24},{18,25},{19,26},{20,27},{21,28},{22,29},{23,30},{2... | collective-permute-start | bytes 933896 | tf_op jit(solution)/shard_map/ppermute | solution.py:367
  75.1 9.0 %collective-permute-start.10 = (bf16[32,64,128]{2,1,0:T(8,128)(2,1)S(1)}, bf16[32,64,128]{2,1,0:T(8,128)(2,1)S(1)}, u32[]{:S(2)}, u32[]{:S(2)}) collective-permute-start(bf16[32,64,128]{2,1,0:T(8,128)(2,1)S(1)} %get-tuple-element.45.refs_6_), channel_id=1, source_target_pairs={{16,24},{17,25},{18,26},{19,27},{20,28},{21,29},{22,30},{23,31},{2... | collective-permute-start | bytes 1572872 | tf_op jit(solution)/shard_map/ppermute | solution.py:367

commit v3 on v2

--- a/solution.py
+++ b/solution.py
@@ -54,10 +54,9 @@
     return room[...].astype(jnp.bfloat16)
 
 
-def prepare_kernel(flags, columns, forcing, kappa, *refs):
-    offsets, by_row, narrow, again, first, last, c_v, f_v, k_v, pack, sems, k_sem, c_sem = refs
+def prepare_kernel(halo, marks, flags, columns, forcing, kappa, *refs):
+    offsets, by_row, narrow, *edges, c_v, f_v, k_v, pack, sems, k_sem, c_sem = refs
     total, rows, cells = f_v.shape
-    halo = first.shape[0] - 1
     step = rows // sems.shape[0]
     loads = []
     for i in range(sems.shape[0]):
@@ -77,9 +76,11 @@
     fetch.wait()
     parts = split(k_v[...])
     narrow[rows] = joined(parts, pack)
-    again[rows] = narrow[rows]
-    first[halo] = joined([part[:halo] for part in parts], pack)
-    last[halo] = joined([part[rows - halo:] for part in parts], pack)
+    for e, start in enumerate((0, rows - halo)):
+        row = joined([part[start:start + halo] for part in parts], pack)
+        for edge in edges[e::2]:
+            tail = (edge.shape[0] - halo, *edge.shape[1:])
+            edge[halo:] = row[:tail[0] * tail[1]].reshape(tail)
     for i, load in enumerate(loads):
         load.wait()
         turned = jnp.swapaxes(f_v[:, i * step:(i + 1) * step, :], 0, 1)
@@ -88,23 +89,28 @@
             y = i * step + r
             value = turned[r].astype(jnp.bfloat16)
             narrow[y] = value
-            again[y] = value
-            if y < halo:
-                first[y] = value
-            if y >= rows - halo:
-                last[y - (rows - halo)] = value
-
-
-def prepare(flags, columns, fields, kappa, halo):
+            for edge_first, edge_last, start, stop in zip(edges[0::2], edges[1::2], marks[:-1], marks[1:]):
+                if y < halo:
+                    edge_first[y] = value[start:stop]
+                if y >= rows - halo:
+                    edge_last[y - (rows - halo)] = value[start:stop]
+
+
+def prepare(flags, columns, fields, kappa, halo, marks):
+    edges = [
+        jax.ShapeDtypeStruct((halo - (-3 * halo // (stop - start)), stop - start, kappa.shape[1]), jnp.bfloat16)
+        for start, stop in zip(marks[:-1], marks[1:]) for _ in range(2)
+    ]
     total, rows, cells = fields.shape
     return pl.pallas_call(
-        prepare_kernel,
+        functools.partial(prepare_kernel, halo, marks),
         in_specs=[SMEM, HBM, HBM, HBM],
         out_shape=[
             jax.ShapeDtypeStruct(columns.shape, columns.dtype),
             pltpu.VMEM((rows, total, cells), jnp.float32),
-        ] + [jax.ShapeDtypeStruct((n + 1, total, cells), jnp.bfloat16) for n in (rows, rows, halo, halo)],
-        out_specs=[VMEM] * 6,
+            jax.ShapeDtypeStruct((rows + 1, total, cells), jnp.bfloat16),
+        ] + edges,
+        out_specs=[VMEM] * (3 + len(edges)),
         scratch_shapes=[
             pltpu.VMEM(columns.shape, columns.dtype),
             pltpu.VMEM((total, rows, cells), jnp.float32),
@@ -119,8 +125,8 @@
     )(flags, in_hbm(columns), in_hbm(fields), in_hbm(kappa))
 
 
-def load_kernel(flags, weights, *refs):
-    held, sems = refs[-3], refs[-1]
+def load_kernel(n_passed, flags, weights, *refs):
+    held, sems = refs[n_passed], refs[-1]
     count, per_row = weights.shape[:2]
     loads = [pltpu.make_async_copy(weights.at[j], held.at[j], sems.at[j]) for j in range(count)]
     start_all(loads)
@@ -138,15 +144,15 @@
 
 def load(flags, weights, passed):
     return pl.pallas_call(
-        load_kernel,
-        in_specs=[SMEM, HBM, ANY],
-        out_shape=[pltpu.VMEM(weights.shape, weights.dtype), jax.ShapeDtypeStruct(passed.shape, passed.dtype)],
-        out_specs=[VMEM, ANY],
-        input_output_aliases={2: 1},
+        functools.partial(load_kernel, len(passed)),
+        in_specs=[SMEM, HBM] + [ANY] * len(passed),
+        out_shape=[pltpu.VMEM(weights.shape, weights.dtype)] + [jax.ShapeDtypeStruct(p.shape, p.dtype) for p in passed],
+        out_specs=[VMEM] + [ANY] * len(passed),
+        input_output_aliases={2 + i: 1 + i for i in range(len(passed))},
         scratch_shapes=[pltpu.SemaphoreType.DMA((weights.shape[0],))],
         compiler_params=pltpu.CompilerParams(vmem_limit_bytes=LIMIT),
         cost_estimate=pl.CostEstimate(flops=0, bytes_accessed=weights.size * 4, transcendentals=0),
-    )(flags, in_hbm(weights), passed)
+    )(flags, in_hbm(weights), *passed)
 
 
 def beside_matrix(cells):
@@ -157,11 +163,13 @@
     return jnp.where(same & ((apart == 1) | (apart == cells - 1)), 1.0, 0.0).astype(jnp.bfloat16)
 
 
-def section_kernel(number, bounds, halo, n_saved, has_next, flags, offsets, kappa, forcing, *refs):
+def section_kernel(turned_edges, number, bounds, halo, n_saved, has_next, flags, offsets, kappa, forcing, *refs):
     refs = list(refs)
     incoming = refs.pop(0) if number else None
     upper, lower = refs.pop(0), refs.pop(0)
-    following = refs.pop(0) if has_next else None
+    if turned_edges:
+        upper, lower = lower, upper
+    ahead = [refs.pop(0) for _ in range(2 if number else 1)] if has_next else []
     weights = refs.pop(0)
     saved = [refs.pop(0) for _ in range(n_saved)]
     if has_next:
@@ -170,7 +178,11 @@
         if bounds[0]:
             refs.pop(0)
         result = refs.pop(0)
-    k_v, once, smooth, own_v, *rest, sems = refs
+    if has_next:
+        k_v, once, smooth, pack = refs
+        own_v, up_s, down_s = own_out, up_out, down_out
+    else:
+        k_v, once, smooth, own_v, turned, sems = refs
     rows, _, cells = forcing.shape
     fields = bounds[1] - bounds[0]
     count, per_row = weights.shape[:2]
@@ -181,7 +193,6 @@
     @pl.when(flags[0] == number)
     def _():
         mine = slice(*bounds)
-        theirs = slice(None) if number else mine
         beside = beside_matrix(cells)
         top = jnp.where(flags[1] == 0, 0.0, 1.0)
         bottom = jnp.where(flags[1] == flags[2] - 1, 0.0, 1.0)
@@ -192,9 +203,9 @@
 
         def entry(i):
             if i < lo:
-                return upper[i, theirs].astype(jnp.float32)
+                return upper[i].astype(jnp.float32)
             if i >= hi:
-                return lower[i - hi, theirs].astype(jnp.float32)
+                return lower[i - hi].astype(jnp.float32)
             value = forcing[i - lo, mine]
             if number:
                 value = value + incoming[i - lo].astype(jnp.float32)
@@ -234,14 +245,16 @@
 
         half = (halo - EDGE) * cells // block
         block_rows = block // cells
-        stores = []
         if has_next:
-            up_s, down_s, pack = rest
-            parts = following[rows].astype(jnp.float32)
-            parts = [parts[p * rows:(p + 1) * rows] for p in range(3)]
-            tail = (up_s.shape[0] - halo, fields, cells)
-            up_s[halo:] = joined([part[:halo] for part in parts], pack).reshape(tail)
-            down_s[halo:] = joined([part[rows - halo:] for part in parts], pack).reshape(tail)
+            if number:
+                up_s[halo:] = ahead[0][halo:]
+                down_s[halo:] = ahead[1][halo:]
+            else:
+                parts = ahead[0][rows].astype(jnp.float32)
+                parts = [parts[p * rows:(p + 1) * rows] for p in range(3)]
+                tail = (up_s.shape[0] - halo, fields, cells)
+                up_s[halo:] = joined([part[:halo] for part in parts], pack).reshape(tail)
+                down_s[halo:] = joined([part[rows - halo:] for part in parts], pack).reshape(tail)
         for j in range(count):
             total = None
             for k in range(per_row):
@@ -256,24 +269,17 @@
                 value = total[:, r * cells:(r + 1) * cells].astype(jnp.bfloat16)
                 own_v[row] = value
                 if has_next:
-                    entry_next = value.astype(jnp.float32) + following[row, mine].astype(jnp.float32)
+                    if number:
+                        ahead_row = ahead[0][row] if row < halo else ahead[1][row - (rows - halo)]
+                    else:
+                        ahead_row = ahead[0][row, mine]
+                    entry_next = value.astype(jnp.float32) + ahead_row.astype(jnp.float32)
                     if row < halo:
                         up_s[row] = entry_next.astype(jnp.bfloat16)
                     if row >= rows - halo:
                         down_s[row - (rows - halo)] = entry_next.astype(jnp.bfloat16)
-                    if row == halo - 1:
-                        stores.append(pltpu.make_async_copy(up_s, up_out, sems.at[0]))
-                        stores[-1].start()
-        if has_next:
-            ends = [
-                pltpu.make_async_copy(down_s, down_out, sems.at[1]),
-                pltpu.make_async_copy(own_v, own_out, sems.at[2]),
-            ]
-            start_all(ends)
-            wait_all(stores + ends)
 
     if not has_next:
-        turned, = rest
         for i, kept in enumerate(saved):
             @pl.when(flags[0] == i)
             def _(kept=kept):
@@ -293,10 +299,12 @@
     rows, total, cells = forcing.shape
     fields = bounds[1] - bounds[0]
     count, per_row, block, _ = weights.shape
-    has_next = following is not None
+    has_next = bool(following)
+    turned_edges = number == 0 and bounds[0] > 0
+    if turned_edges:
+        arrived = arrived[::-1]
     operands = [flags, offsets, kappa, in_vmem(forcing)] + arrived
-    if has_next:
-        operands.append(following)
+    operands += following
     specs = [SMEM] * 2 + [VMEM] * (len(operands) - 2)
     operands.append(in_vmem(weights))
     specs.append(VMEM)
@@ -306,27 +314,28 @@
         pltpu.VMEM((extent, cells), jnp.float32),
         pltpu.VMEM((extent, fields, cells), jnp.float32),
         pltpu.VMEM(((extent - 2 * EDGE) * cells // block, fields, block), jnp.bfloat16),
-        pltpu.VMEM((rows, fields, cells), jnp.bfloat16),
     ]
     aliases = {}
     if has_next:
         outs = [jax.ShapeDtypeStruct((n, fields, cells), jnp.bfloat16) for n in (rows, halo + packed, halo + packed)]
-        out_specs = [ANY] * 3
-        scratch += [pltpu.VMEM((halo + packed, fields, cells), jnp.bfloat16)] * 2
+        out_specs = [VMEM] * 3
         scratch.append(pltpu.VMEM((packed * fields, cells), jnp.float32))
     else:
         outs = [jax.ShapeDtypeStruct((total, rows, cells), jnp.bfloat16)]
         out_specs = [HBM]
-        scratch += [pltpu.VMEM((fields, rows, cells), jnp.bfloat16)]
+        scratch += [
+            pltpu.VMEM((rows, fields, cells), jnp.bfloat16),
+            pltpu.VMEM((fields, rows, cells), jnp.bfloat16),
+            pltpu.SemaphoreType.DMA((2,)),
+        ]
         operands += [in_hbm(value) for value in saved]
         specs += [HBM] * len(saved)
         if result is not None:
             aliases = {len(operands): 0}
             operands.append(result)
             specs.append(HBM)
-    scratch.append(pltpu.SemaphoreType.DMA((3,)))
     return pl.pallas_call(
-        functools.partial(section_kernel, number, bounds, halo, len(saved), has_next),
+        functools.partial(section_kernel, turned_edges, number, bounds, halo, len(saved), has_next),
         in_specs=specs,
         out_shape=outs,
         out_specs=out_specs,
@@ -358,7 +367,7 @@
         pairs = [(place(source, t), place(target, t + shift)) for t in range(n_tile)]
         others = [s for s in range(n_section) if s not in (source, target)]
         if source == target:
-            rest = list(zip(others, others[1:] + others[:1]))
+            rest = list(zip(others[1:] + others[:1], others))
         elif source ^ 1 == target and n_section % 2 == 0:
             rest = [(target, source)] + [(s, s ^ 1) for s in others]
         else:
@@ -366,26 +375,24 @@
         pairs += [(place(s, t), place(to, t)) for s, to in rest for t in range(n_tile)]
         return lax.ppermute(value, AXES, pairs)
 
-    offsets, by_row, narrow, again, first, last = prepare(
-        flags, col_blocks[0].T, forcing.reshape(-1, rows, cells), kappa[0], halo
-    )
-    total = by_row.shape[1]
-    marks = [total * sum(SHARES[:c]) // sum(SHARES) for c in range(len(SHARES) + 1)]
-    chunks = list(zip(marks[:-1], marks[1:]))
-    arrivals = [[send(last, 0, 0, 1), send(first, 0, 0, -1)]] * len(chunks)
-    weights, again = load(flags, weights, again)
-    following = [
-        lax.ppermute(narrow, "comp", [(s, s ^ 1) for s in range(n_section) if s ^ 1 < n_section]),
-        lax.ppermute(again, "comp", [(s + 1, s) for s in range(1, n_section - 1, 2)]),
-    ]
-    owns = [[] for _ in chunks]
+    fields = forcing.reshape(-1, rows, cells)
+    marks = [fields.shape[0] * sum(SHARES[:c]) // sum(SHARES) for c in range(len(SHARES) + 1)]
+    offsets, by_row, narrow, *edges = prepare(flags, col_blocks[0].T, fields, kappa[0], halo, marks)
+    weights, *edges[2:] = load(flags, weights, edges[2:])
+    arrivals = []
+    for c in range(len(SHARES)):
+        sends = [(edges[2 * c + 1], 1), (edges[2 * c], -1)][::1 - c % 2 * 2]
+        arrivals.append([send(edge, 0, 0, shift) for edge, shift in sends][::1 - c % 2 * 2])
+    narrow = lax.ppermute(narrow, "comp", [(s, s ^ 1) for s in range(n_section) if s ^ 1 < n_section])
+    following = [[[narrow]] * len(SHARES)] + [[pair[::-1] for pair in arrivals]] * (n_section - 2) + [[[]] * len(SHARES)]
+    owns = [[] for _ in SHARES]
     result = None
     for s in range(n_section):
         last = s + 1 == n_section
         leaving = []
-        for c, bounds in enumerate(chunks):
+        for c, bounds in enumerate(zip(marks[:-1], marks[1:])):
             parts = section(
-                s, bounds, halo, flags, offsets, kappa[0], by_row, arrivals[c], None if last else following[s % 2],
+                s, bounds, halo, flags, offsets, kappa[0], by_row, arrivals[c], following[s][c],
                 weights, owns[c] if last else [], result,
             )
             if last:

time: 89.6 us -> 84.2 us (0.940)
  starting transfers between devices: 58.2 us -> 48.1 us
  waiting for transfers between devices: 4.15 us -> 8.57 us
    ppermute x20 -> x22, starting transfers between devices: 56.7 us -> 47.3 us  [send(): return lax.ppermute(value, AXES, pairs)]
    ppermute x20 -> x22, waiting for transfers between devices: 4.14 us -> 8.57 us  [send(): return lax.ppermute(value, AXES, pairs)]
  transfers between devices with their start and end apart: 22 -> 23, of which waited for: 2 -> 3; matrix products, arithmetic and copies ran while one was open for 0% -> 0% of each run, Pallas kernels for 21% -> 22%
where the time goes in v3:
time: 84.2 us; the launch traced here: 83.4 us
  starting transfers between devices  48.1 us (57%)
  Pallas kernels  26.2 us (31%)
  waiting for transfers between devices  8.57 us (10%)
    ppermute x22, starting transfers between devices, send(): return lax.ppermute(value, AXES, pairs)  47.3 us
    pallas_call x8, Pallas kernels, section(): pl.pallas_call(functools.partial(section_kernel, turned_edges, number, bo...  13.9 us
    pallas_call x1, Pallas kernels, load(): pl.pallas_call(functools.partial(load_kernel, len(passed)), in_specs=[SME...  9.7 us
    ppermute x22, waiting for transfers between devices, send(): return lax.ppermute(value, AXES, pairs)  8.57 us
    pallas_call x1, Pallas kernels, prepare(): pl.pallas_call(functools.partial(prepare_kernel, halo, marks), in_specs=[...  2.58 us
  transfers between devices with their start and end apart: 23, of which 3 were waited for; matrix products, arithmetic and copies ran while one was open for 0% of the time, Pallas kernels for 22%

profile of v3, /device:TPU:3, one launch (start us, length us, event | category | flops | bytes accessed | tf_op | source)
XLA Modules:
  0.0 83.4 jit_solution(1986653661633610329)
XLA Ops:
  0.0 0.1 pad_add_fusion.flags
  0.1 2.6 %shard_map.46 = (s32[4,16]{1,0:T(4,128)S(1)}, f32[32,128,128]{2,1,0:T(8,128)S(1)}, bf16[33,128,128]{2,1,0:T(8,128)(2,1)S(1)}, bf16[19,64,128]{2,1,0:T(8,128)(2,1...) custom-call(s32[3]{0:T(128)S(1)} %pad_add_fusion.flags, ...), custom_call_target="tpu_custom_call" | custom-call | bytes 6291456 | tf_op jit(solution)/shard_map/pallas_call | solution.py:105
  2.7 0.7 collective-permute-start.2
  3.4 0.1 collective-permute-start.12
  3.5 0.1 collective-permute-start.13
  3.6 9.7 %shard_map.47 = (bf16[16,4,256,256]{3,2,1,0:T(8,128)(2,1)S(1)}, bf16[19,64,128]{2,1,0:T(8,128)(2,1)S(1)}, bf16[19,64,128]{2,1,0:T(8,128)(2,1)S(1)}) custom-call(s32[3]{0:T(128)S(1)} %pad_add_fusion.flags, bf16[16,4,256,256]{3,2,1,0:T(8,128)(2,1)} %bitcast.18, ...), custom_call_target="tpu_custom_call", output_to_operand_aliasing={{1}: (2, {}), {2}: (3, {})} | custom-call | bytes 16777216 | tf_op jit(solution)/shard_map/pallas_call | solution.py:146
  13.3 1.8 %collective-permute-start = (bf16[19,64,128]{2,1,0:T(8,128)(2,1)S(1)}, bf16[19,64,128]{2,1,0:T(8,128)(2,1)S(1)}, u32[]{:S(2)}, u32[]{:S(2)}) collective-permute-start(bf16[19,64,128]{2,1,0:T(8,128)(2,1)S(1)} %get-tuple-element.37), channel_id=1, source_target_pairs={{0,7},{1,0},{2,1},{3,2},{4,3},{5,4},{6,5},{7,6},{16,8},{17,9},{18,... | collective-permute-start | bytes 933896 | tf_op jit(solution)/shard_map/ppermute | solution.py:376
  15.0 0.1 collective-permute-start.1
  15.1 0.0 collective-permute-done.12.refs_0_.refs_4_
  15.1 0.0 collective-permute-done.13.refs_1_.refs_3_
  15.1 0.0 collective-permute-done.2.refs_2_
  15.1 0.0 copy-done
  15.1 0.6 shard_map.51
  15.7 0.0 copy-start.1
  15.7 0.1 collective-permute-start.14
  15.9 0.4 collective-permute-start.15
  16.3 0.1 collective-permute-start.16
  16.4 2.7 %collective-permute-done.refs_0_.refs_3_ = bf16[19,64,128]{2,1,0:T(8,128)(2,1)S(1)} collective-permute-done((bf16[19,64,128]{2,1,0:T(8,128)(2,1)S(1)}, bf16[19,64,128]{2,1,0:T(8,128)(2,1)S(1)}, u32[]{:S(2)}, u32[]{:S(2)}) %collective-permute-start) | collective-permute-done | bytes 311328 | tf_op jit(solution)/shard_map/ppermute | solution.py:376
  19.1 3.3 %collective-permute-done.1.refs_1_.refs_4_ = bf16[19,64,128]{2,1,0:T(8,128)(2,1)S(1)} collective-permute-done((bf16[19,64,128]{2,1,0:T(8,128)(2,1)S(1)}, bf16[19,64,128]{2,1,0:T(8,128)(2,1)S(1)}, u32[]{:S(2)}, u32[]{:S(2)}) %collective-permute-start.1) | collective-permute-done | bytes 311328 | tf_op jit(solution)/shard_map/ppermute | solution.py:376
  22.4 0.6 shard_map.48
  23.0 0.0 copy-done.1
  23.0 0.0 copy-start.2
  23.0 0.5 collective-permute-start.3
  23.5 0.1 collective-permute-start.4
  23.6 0.0 collective-permute-done.15.refs_1_
  23.6 0.4 collective-permute-start.5
  24.1 0.0 collective-permute-done.16.refs_2_
  24.1 0.0 collective-permute-done.14.refs_0_
  24.1 0.6 shard_map.52
  24.6 0.0 copy-done.2
  24.7 0.0 copy-start.3
  24.7 0.7 collective-permute-start.17
  25.4 0.7 collective-permute-start.18
  26.1 0.0 collective-permute-done.4.refs_1_
  26.1 0.7 collective-permute-start.19
  26.8 0.0 collective-permute-done.5.refs_2_
  26.8 0.0 collective-permute-done.3.refs_0_
  26.8 0.8 shard_map.49
  27.5 0.0 copy-done.3
  27.6 0.7 collective-permute-start.6
  28.3 0.7 collective-permute-start.7
  28.9 0.0 collective-permute-done.18.refs_1_
  29.0 0.7 collective-permute-start.8
  29.6 0.0 collective-permute-done.19.refs_2_
  29.7 0.0 collective-permute-done.17.refs_0_
  29.7 0.6 shard_map.53
  30.3 23.1 %collective-permute-start.20 = (bf16[32,64,128]{2,1,0:T(8,128)(2,1)S(1)}, bf16[32,64,128]{2,1,0:T(8,128)(2,1)S(1)}, u32[]{:S(2)}, u32[]{:S(2)}) collective-permute-start(bf16[32,64,128]{2,1,0:T(8,128)(2,1)S(1)} %get-tuple-element.58.refs_6_), channel_id=1, source_target_pairs={{16,24},{17,25},{18,26},{19,27},{20,28},{21,29},{22,30},{23,31},{2... | collective-permute-start | bytes 1572872 | tf_op jit(solution)/shard_map/ppermute | solution.py:376
  53.3 0.1 collective-permute-start.21
  53.4 0.0 collective-permute-done.7.refs_1_
  53.4 3.8 %collective-permute-start.22 = (bf16[19,64,128]{2,1,0:T(8,128)(2,1)S(1)}, bf16[19,64,128]{2,1,0:T(8,128)(2,1)S(1)}, u32[]{:S(2)}, u32[]{:S(2)}) collective-permute-start(bf16[19,64,128]{2,1,0:T(8,128)(2,1)S(1)} %get-tuple-element.60), channel_id=1, source_target_pairs={{16,31},{17,24},{18,25},{19,26},{20,27},{21,28},{22,29},{23,30},{2... | collective-permute-start | bytes 933896 | tf_op jit(solution)/shard_map/ppermute | solution.py:376
  57.2 0.0 collective-permute-done.8.refs_2_
  57.2 0.0 collective-permute-done.6.refs_0_
  57.2 0.6 shard_map.50
  57.8 8.3 %collective-permute-start.9 = (bf16[32,64,128]{2,1,0:T(8,128)(2,1)S(1)}, bf16[32,64,128]{2,1,0:T(8,128)(2,1)S(1)}, u32[]{:S(2)}, u32[]{:S(2)}) collective-permute-start(bf16[32,64,128]{2,1,0:T(8,128)(2,1)S(1)} %get-tuple-element.47.refs_6_), channel_id=1, source_target_pairs={{16,24},{17,25},{18,26},{19,27},{20,28},{21,29},{22,30},{23,31},{2... | collective-permute-start | bytes 1572872 | tf_op jit(solution)/shard_map/ppermute | solution.py:376
  66.1 0.1 collective-permute-start.10
  66.2 0.0 collective-permute-done.21.refs_1_
  66.2 4.3 %collective-permute-start.11 = (bf16[19,64,128]{2,1,0:T(8,128)(2,1)S(1)}, bf16[19,64,128]{2,1,0:T(8,128)(2,1)S(1)}, u32[]{:S(2)}, u32[]{:S(2)}) collective-permute-start(bf16[19,64,128]{2,1,0:T(8,128)(2,1)S(1)} %get-tuple-element.49), channel_id=1, source_target_pairs={{16,31},{17,24},{18,25},{19,26},{20,27},{21,28},{22,29},{23,30},{2... | collective-permute-start | bytes 933896 | tf_op jit(solution)/shard_map/ppermute | solution.py:376
  70.4 0.0 collective-permute-done.22.refs_2_
  70.4 0.0 collective-permute-done.20.refs_0_
  70.4 5.0 %shard_map.54.refs_7_ = bf16[128,32,128]{2,1,0:T(8,128)(2,1)} custom-call(s32[3]{0:T(128)S(1)} %pad_add_fusion.flags, s32[4,16]{1,0:T(4,128)S(1)} %get-tuple-element.33.offsets, f32[32,128]{1,0:T(8,128)S(1)} %bitcast.16, f32[32,128,128]{2,1,0:T(8,128)S(1)} %get-tuple-element.34.forcing, bf16[32,64,128]{2,1,0:T(8,128)(2,1)S(1)} %collective-permute-done.20.refs_0_, ...), custom_call_target="tpu_custom_call" | custom-call | flops 10737418240 | bytes 8388608 | tf_op jit(solution)/shard_map/pallas_call | solution.py:337
  75.5 0.0 collective-permute-done.10.refs_1_
  75.5 2.5 %collective-permute-done.11.refs_2_ = bf16[19,64,128]{2,1,0:T(8,128)(2,1)S(1)} collective-permute-done((bf16[19,64,128]{2,1,0:T(8,128)(2,1)S(1)}, bf16[19,64,128]{2,1,0:T(8,128)(2,1)S(1)}, u32[]{:S(2)}, u32[]{:S(2)}) %collective-permute-start.11) | collective-permute-done | bytes 311328 | tf_op jit(solution)/shard_map/ppermute | solution.py:376
  78.0 0.0 collective-permute-done.9.refs_0_
  78.0 5.2 %shard_map.55 = bf16[128,32,128]{2,1,0:T(8,128)(2,1)} custom-call(s32[3]{0:T(128)S(1)} %pad_add_fusion.flags, s32[4,16]{1,0:T(4,128)S(1)} %get-tuple-element.33.offsets, f32[32,128]{1,0:T(8,128)S(1)} %bitcast.17, f32[32,128,128]{2,1,0:T(8,128)S(1)} %get-tuple-element.34.forcing, ...), custom_call_target="tpu_custom_call", output_to_operand_aliasing={{}: (11, {})} | custom-call | flops 10737418240 | bytes 8388608 | tf_op jit(solution)/shard_map/pallas_call | solution.py:337
  (7 shorter events, 0.0 us)
Async XLA Ops:
  2.7 12.5 %collective-permute-start.2 = (bf16[33,128,128]{2,1,0:T(8,128)(2,1)S(1)}, bf16[33,128,128]{2,1,0:T(8,128)(2,1)S(1)}, u32[]{:S(2)}, u32[]{:S(2)}) collective-permute-start(bf16[33,128,128]{2,1,0:T(8,128)(2,1)S(1)} %get-tuple-element.39), channel_id=1, source_target_pairs={{0,8},{8,0},{16,24},{24,16},{1,9},{9,1},{17,25},{25,17},{2,10},{10... | collective-permute-start | bytes 3244040 | tf_op jit(solution)/shard_map/ppermute | solution.py:386
  3.4 11.7 %collective-permute-start.12 = (bf16[19,64,128]{2,1,0:T(8,128)(2,1)S(1)}, bf16[19,64,128]{2,1,0:T(8,128)(2,1)S(1)}, u32[]{:S(2)}, u32[]{:S(2)}) collective-permute-start(bf16[19,64,128]{2,1,0:T(8,128)(2,1)S(1)} %get-tuple-element.50), channel_id=1, source_target_pairs={{0,1},{1,2},{2,3},{3,4},{4,5},{5,6},{6,7},{7,0},{16,8},{17,9},{18,... | collective-permute-start | bytes 933896 | tf_op jit(solution)/shard_map/ppermute | solution.py:376
  3.5 11.6 %collective-permute-start.13 = (bf16[19,64,128]{2,1,0:T(8,128)(2,1)S(1)}, bf16[19,64,128]{2,1,0:T(8,128)(2,1)S(1)}, u32[]{:S(2)}, u32[]{:S(2)}) collective-permute-start(bf16[19,64,128]{2,1,0:T(8,128)(2,1)S(1)} %get-tuple-element.51), channel_id=1, source_target_pairs={{0,7},{1,0},{2,1},{3,2},{4,3},{5,4},{6,5},{7,6},{16,8},{17,9},{18,... | collective-permute-start | bytes 933896 | tf_op jit(solution)/shard_map/ppermute | solution.py:376
  3.6 11.6 %copy-start = (f32[1,32,128]{2,1,0:T(8,128)S(1)}, f32[1,32,128]{2,1,0:T(8,128)}, u32[]{:S(2)}) copy-start(f32[1,32,128]{2,1,0:T(8,128)} %param.5) | copy-start | bytes 49156
  13.3 5.8 %collective-permute-start = (bf16[19,64,128]{2,1,0:T(8,128)(2,1)S(1)}, bf16[19,64,128]{2,1,0:T(8,128)(2,1)S(1)}, u32[]{:S(2)}, u32[]{:S(2)}) collective-permute-start(bf16[19,64,128]{2,1,0:T(8,128)(2,1)S(1)} %get-tuple-element.37), channel_id=1, source_target_pairs={{0,7},{1,0},{2,1},{3,2},{4,3},{5,4},{6,5},{7,6},{16,8},{17,9},{18,... | collective-permute-start | bytes 933896 | tf_op jit(solution)/shard_map/ppermute | solution.py:376
  15.0 7.4 %collective-permute-start.1 = (bf16[19,64,128]{2,1,0:T(8,128)(2,1)S(1)}, bf16[19,64,128]{2,1,0:T(8,128)(2,1)S(1)}, u32[]{:S(2)}, u32[]{:S(2)}) collective-permute-start(bf16[19,64,128]{2,1,0:T(8,128)(2,1)S(1)} %get-tuple-element.38), channel_id=1, source_target_pairs={{0,1},{1,2},{2,3},{3,4},{4,5},{5,6},{6,7},{7,0},{16,8},{17,9},{18,... | collective-permute-start | bytes 933896 | tf_op jit(solution)/shard_map/ppermute | solution.py:376
  15.7 7.3 %copy-start.1 = (bf16[32,64,128]{2,1,0:T(8,128)(2,1)}, bf16[32,64,128]{2,1,0:T(8,128)(2,1)S(1)}, u32[]{:S(2)}) copy-start(bf16[32,64,128]{2,1,0:T(8,128)(2,1)S(1)} %get-tuple-element.52.refs_4_) | copy-start | bytes 1572868
  15.7 8.3 %collective-permute-start.14 = (bf16[32,64,128]{2,1,0:T(8,128)(2,1)S(1)}, bf16[32,64,128]{2,1,0:T(8,128)(2,1)S(1)}, u32[]{:S(2)}, u32[]{:S(2)}) collective-permute-start(bf16[32,64,128]{2,1,0:T(8,128)(2,1)S(1)} %get-tuple-element.52.refs_4_), channel_id=1, source_target_pairs={{0,8},{1,9},{2,10},{3,11},{4,12},{5,13},{6,14},{7,15},{8,0},{9,1},... | collective-permute-start | bytes 1572872 | tf_op jit(solution)/shard_map/ppermute | solution.py:376
  15.9 7.7 %collective-permute-start.15 = (bf16[19,64,128]{2,1,0:T(8,128)(2,1)S(1)}, bf16[19,64,128]{2,1,0:T(8,128)(2,1)S(1)}, u32[]{:S(2)}, u32[]{:S(2)}) collective-permute-start(bf16[19,64,128]{2,1,0:T(8,128)(2,1)S(1)} %get-tuple-element.53), channel_id=1, source_target_pairs={{0,9},{1,10},{2,11},{3,12},{4,13},{5,14},{6,15},{7,8},{8,0},{9,1},... | collective-permute-start | bytes 933896 | tf_op jit(solution)/shard_map/ppermute | solution.py:376
  16.3 7.7 %collective-permute-start.16 = (bf16[19,64,128]{2,1,0:T(8,128)(2,1)S(1)}, bf16[19,64,128]{2,1,0:T(8,128)(2,1)S(1)}, u32[]{:S(2)}, u32[]{:S(2)}) collective-permute-start(bf16[19,64,128]{2,1,0:T(8,128)(2,1)S(1)} %get-tuple-element.54), channel_id=1, source_target_pairs={{0,15},{1,8},{2,9},{3,10},{4,11},{5,12},{6,13},{7,14},{8,0},{9,1},... | collective-permute-start | bytes 933896 | tf_op jit(solution)/shard_map/ppermute | solution.py:376
  23.0 1.6 %copy-start.2 = (bf16[32,64,128]{2,1,0:T(8,128)(2,1)}, bf16[32,64,128]{2,1,0:T(8,128)(2,1)S(1)}, u32[]{:S(2)}) copy-start(bf16[32,64,128]{2,1,0:T(8,128)(2,1)S(1)} %get-tuple-element.41.refs_4_) | copy-start | bytes 1572868
  23.0 3.7 %collective-permute-start.3 = (bf16[32,64,128]{2,1,0:T(8,128)(2,1)S(1)}, bf16[32,64,128]{2,1,0:T(8,128)(2,1)S(1)}, u32[]{:S(2)}, u32[]{:S(2)}) collective-permute-start(bf16[32,64,128]{2,1,0:T(8,128)(2,1)S(1)} %get-tuple-element.41.refs_4_), channel_id=1, source_target_pairs={{0,8},{1,9},{2,10},{3,11},{4,12},{5,13},{6,14},{7,15},{8,0},{9,1},... | collective-permute-start | bytes 1572872 | tf_op jit(solution)/shard_map/ppermute | solution.py:376
  23.5 2.5 %collective-permute-start.4 = (bf16[19,64,128]{2,1,0:T(8,128)(2,1)S(1)}, bf16[19,64,128]{2,1,0:T(8,128)(2,1)S(1)}, u32[]{:S(2)}, u32[]{:S(2)}) collective-permute-start(bf16[19,64,128]{2,1,0:T(8,128)(2,1)S(1)} %get-tuple-element.42), channel_id=1, source_target_pairs={{0,9},{1,10},{2,11},{3,12},{4,13},{5,14},{6,15},{7,8},{8,0},{9,1},... | collective-permute-start | bytes 933896 | tf_op jit(solution)/shard_map/ppermute | solution.py:376
  23.6 3.1 %collective-permute-start.5 = (bf16[19,64,128]{2,1,0:T(8,128)(2,1)S(1)}, bf16[19,64,128]{2,1,0:T(8,128)(2,1)S(1)}, u32[]{:S(2)}, u32[]{:S(2)}) collective-permute-start(bf16[19,64,128]{2,1,0:T(8,128)(2,1)S(1)} %get-tuple-element.43), channel_id=1, source_target_pairs={{0,15},{1,8},{2,9},{3,10},{4,11},{5,12},{6,13},{7,14},{8,0},{9,1},... | collective-permute-start | bytes 933896 | tf_op jit(solution)/shard_map/ppermute | solution.py:376
  24.7 2.9 %copy-start.3 = (bf16[32,64,128]{2,1,0:T(8,128)(2,1)}, bf16[32,64,128]{2,1,0:T(8,128)(2,1)S(1)}, u32[]{:S(2)}) copy-start(bf16[32,64,128]{2,1,0:T(8,128)(2,1)S(1)} %get-tuple-element.55.refs_5_) | copy-start | bytes 1572868
  24.7 5.0 %collective-permute-start.17 = (bf16[32,64,128]{2,1,0:T(8,128)(2,1)S(1)}, bf16[32,64,128]{2,1,0:T(8,128)(2,1)S(1)}, u32[]{:S(2)}, u32[]{:S(2)}) collective-permute-start(bf16[32,64,128]{2,1,0:T(8,128)(2,1)S(1)} %get-tuple-element.55.refs_5_), channel_id=1, source_target_pairs={{8,16},{9,17},{10,18},{11,19},{12,20},{13,21},{14,22},{15,23}} | collective-permute-start | bytes 1572872 | tf_op jit(solution)/shard_map/ppermute | solution.py:376
  25.4 3.6 %collective-permute-start.18 = (bf16[19,64,128]{2,1,0:T(8,128)(2,1)S(1)}, bf16[19,64,128]{2,1,0:T(8,128)(2,1)S(1)}, u32[]{:S(2)}, u32[]{:S(2)}) collective-permute-start(bf16[19,64,128]{2,1,0:T(8,128)(2,1)S(1)} %get-tuple-element.56), channel_id=1, source_target_pairs={{8,17},{9,18},{10,19},{11,20},{12,21},{13,22},{14,23},{15,16}} | collective-permute-start | bytes 933896 | tf_op jit(solution)/shard_map/ppermute | solution.py:376
  26.1 3.6 %collective-permute-start.19 = (bf16[19,64,128]{2,1,0:T(8,128)(2,1)S(1)}, bf16[19,64,128]{2,1,0:T(8,128)(2,1)S(1)}, u32[]{:S(2)}, u32[]{:S(2)}) collective-permute-start(bf16[19,64,128]{2,1,0:T(8,128)(2,1)S(1)} %get-tuple-element.57), channel_id=1, source_target_pairs={{8,23},{9,16},{10,17},{11,18},{12,19},{13,20},{14,21},{15,22}} | collective-permute-start | bytes 933896 | tf_op jit(solution)/shard_map/ppermute | solution.py:376
  27.5 2.7 %copy-start.4 = (bf16[32,64,128]{2,1,0:T(8,128)(2,1)}, bf16[32,64,128]{2,1,0:T(8,128)(2,1)S(1)}, u32[]{:S(2)}) copy-start(bf16[32,64,128]{2,1,0:T(8,128)(2,1)S(1)} %get-tuple-element.44.refs_5_) | copy-start | bytes 1572868
  27.6 29.6 %collective-permute-start.6 = (bf16[32,64,128]{2,1,0:T(8,128)(2,1)S(1)}, bf16[32,64,128]{2,1,0:T(8,128)(2,1)S(1)}, u32[]{:S(2)}, u32[]{:S(2)}) collective-permute-start(bf16[32,64,128]{2,1,0:T(8,128)(2,1)S(1)} %get-tuple-element.44.refs_5_), channel_id=1, source_target_pairs={{8,16},{9,17},{10,18},{11,19},{12,20},{13,21},{14,22},{15,23}} | collective-permute-start | bytes 1572872 | tf_op jit(solution)/shard_map/ppermute | solution.py:376
  28.3 25.1 %collective-permute-start.7 = (bf16[19,64,128]{2,1,0:T(8,128)(2,1)S(1)}, bf16[19,64,128]{2,1,0:T(8,128)(2,1)S(1)}, u32[]{:S(2)}, u32[]{:S(2)}) collective-permute-start(bf16[19,64,128]{2,1,0:T(8,128)(2,1)S(1)} %get-tuple-element.45), channel_id=1, source_target_pairs={{8,17},{9,18},{10,19},{11,20},{12,21},{13,22},{14,23},{15,16}} | collective-permute-start | bytes 933896 | tf_op jit(solution)/shard_map/ppermute | solution.py:376
  29.0 28.2 %collective-permute-start.8 = (bf16[19,64,128]{2,1,0:T(8,128)(2,1)S(1)}, bf16[19,64,128]{2,1,0:T(8,128)(2,1)S(1)}, u32[]{:S(2)}, u32[]{:S(2)}) collective-permute-start(bf16[19,64,128]{2,1,0:T(8,128)(2,1)S(1)} %get-tuple-element.46), channel_id=1, source_target_pairs={{8,23},{9,16},{10,17},{11,18},{12,19},{13,20},{14,21},{15,22}} | collective-permute-start | bytes 933896 | tf_op jit(solution)/shard_map/ppermute | solution.py:376
  30.3 27.5 %copy-start.5 = (bf16[32,64,128]{2,1,0:T(8,128)(2,1)}, bf16[32,64,128]{2,1,0:T(8,128)(2,1)S(1)}, u32[]{:S(2)}) copy-start(bf16[32,64,128]{2,1,0:T(8,128)(2,1)S(1)} %get-tuple-element.58.refs_6_) | copy-start | bytes 1572868
  30.3 40.2 %collective-permute-start.20 = (bf16[32,64,128]{2,1,0:T(8,128)(2,1)S(1)}, bf16[32,64,128]{2,1,0:T(8,128)(2,1)S(1)}, u32[]{:S(2)}, u32[]{:S(2)}) collective-permute-start(bf16[32,64,128]{2,1,0:T(8,128)(2,1)S(1)} %get-tuple-element.58.refs_6_), channel_id=1, source_target_pairs={{16,24},{17,25},{18,26},{19,27},{20,28},{21,29},{22,30},{23,31},{2... | collective-permute-start | bytes 1572872 | tf_op jit(solution)/shard_map/ppermute | solution.py:376
  53.3 12.8 %collective-permute-start.21 = (bf16[19,64,128]{2,1,0:T(8,128)(2,1)S(1)}, bf16[19,64,128]{2,1,0:T(8,128)(2,1)S(1)}, u32[]{:S(2)}, u32[]{:S(2)}) collective-permute-start(bf16[19,64,128]{2,1,0:T(8,128)(2,1)S(1)} %get-tuple-element.59), channel_id=1, source_target_pairs={{16,25},{17,26},{18,27},{19,28},{20,29},{21,30},{22,31},{23,24},{2... | collective-permute-start | bytes 933896 | tf_op jit(solution)/shard_map/ppermute | solution.py:376
  53.4 17.0 %collective-permute-start.22 = (bf16[19,64,128]{2,1,0:T(8,128)(2,1)S(1)}, bf16[19,64,128]{2,1,0:T(8,128)(2,1)S(1)}, u32[]{:S(2)}, u32[]{:S(2)}) collective-permute-start(bf16[19,64,128]{2,1,0:T(8,128)(2,1)S(1)} %get-tuple-element.60), channel_id=1, source_target_pairs={{16,31},{17,24},{18,25},{19,26},{20,27},{21,28},{22,29},{23,30},{2... | collective-permute-start | bytes 933896 | tf_op jit(solution)/shard_map/ppermute | solution.py:376
  57.8 17.7 %copy-start.6 = (bf16[32,64,128]{2,1,0:T(8,128)(2,1)}, bf16[32,64,128]{2,1,0:T(8,128)(2,1)S(1)}, u32[]{:S(2)}) copy-start(bf16[32,64,128]{2,1,0:T(8,128)(2,1)S(1)} %get-tuple-element.47.refs_6_) | copy-start | bytes 1572868
  57.8 20.2 %collective-permute-start.9 = (bf16[32,64,128]{2,1,0:T(8,128)(2,1)S(1)}, bf16[32,64,128]{2,1,0:T(8,128)(2,1)S(1)}, u32[]{:S(2)}, u32[]{:S(2)}) collective-permute-start(bf16[32,64,128]{2,1,0:T(8,128)(2,1)S(1)} %get-tuple-element.47.refs_6_), channel_id=1, source_target_pairs={{16,24},{17,25},{18,26},{19,27},{20,28},{21,29},{22,30},{23,31},{2... | collective-permute-start | bytes 1572872 | tf_op jit(solution)/shard_map/ppermute | solution.py:376
  66.1 9.4 %collective-permute-start.10 = (bf16[19,64,128]{2,1,0:T(8,128)(2,1)S(1)}, bf16[19,64,128]{2,1,0:T(8,128)(2,1)S(1)}, u32[]{:S(2)}, u32[]{:S(2)}) collective-permute-start(bf16[19,64,128]{2,1,0:T(8,128)(2,1)S(1)} %get-tuple-element.48), channel_id=1, source_target_pairs={{16,25},{17,26},{18,27},{19,28},{20,29},{21,30},{22,31},{23,24},{2... | collective-permute-start | bytes 933896 | tf_op jit(solution)/shard_map/ppermute | solution.py:376
  66.2 11.8 %collective-permute-start.11 = (bf16[19,64,128]{2,1,0:T(8,128)(2,1)S(1)}, bf16[19,64,128]{2,1,0:T(8,128)(2,1)S(1)}, u32[]{:S(2)}, u32[]{:S(2)}) collective-permute-start(bf16[19,64,128]{2,1,0:T(8,128)(2,1)S(1)} %get-tuple-element.49), channel_id=1, source_target_pairs={{16,31},{17,24},{18,25},{19,26},{20,27},{21,28},{22,29},{23,30},{2... | collective-permute-start | bytes 933896 | tf_op jit(solution)/shard_map/ppermute | solution.py:376

commit v4 on v3

--- a/solution.py
+++ b/solution.py
@@ -11,6 +11,7 @@
 SHARES = (1, 1)
 EDGE = 2
 LIMIT = 24 << 20
+ORDERS = (((-2, -1), (-1, -2)), ((-1, -2, 0), (-1, -2, 0)))
 WEIGHT = 20
 HBM = pl.BlockSpec(memory_space=pltpu.HBM)
 VMEM = pl.BlockSpec(memory_space=pltpu.VMEM)
@@ -43,6 +44,10 @@
         parts.append(head)
         value = value - head
     return parts
+
+
+def packed_rows(halo, start, stop):
+    return 0 if start else -(-3 * halo // (stop - start))
 
 
 def joined(parts, room):
@@ -78,9 +83,8 @@
     narrow[rows] = joined(parts, pack)
     for e, start in enumerate((0, rows - halo)):
         row = joined([part[start:start + halo] for part in parts], pack)
-        for edge in edges[e::2]:
-            tail = (edge.shape[0] - halo, *edge.shape[1:])
-            edge[halo:] = row[:tail[0] * tail[1]].reshape(tail)
+        tail = (edges[e].shape[0] - halo, *edges[e].shape[1:])
+        edges[e][halo:] = row[:tail[0] * tail[1]].reshape(tail)
     for i, load in enumerate(loads):
         load.wait()
         turned = jnp.swapaxes(f_v[:, i * step:(i + 1) * step, :], 0, 1)
@@ -98,7 +102,7 @@
 
 def prepare(flags, columns, fields, kappa, halo, marks):
     edges = [
-        jax.ShapeDtypeStruct((halo - (-3 * halo // (stop - start)), stop - start, kappa.shape[1]), jnp.bfloat16)
+        jax.ShapeDtypeStruct((halo + packed_rows(halo, 0, stop - start), stop - start, kappa.shape[1]), jnp.bfloat16)
         for start, stop in zip(marks[:-1], marks[1:]) for _ in range(2)
     ]
     total, rows, cells = fields.shape
@@ -163,12 +167,11 @@
     return jnp.where(same & ((apart == 1) | (apart == cells - 1)), 1.0, 0.0).astype(jnp.bfloat16)
 
 
-def section_kernel(turned_edges, number, bounds, halo, n_saved, has_next, flags, offsets, kappa, forcing, *refs):
+def section_kernel(order, number, bounds, halo, n_saved, has_next, flags, offsets, kappa, forcing, *refs):
     refs = list(refs)
-    incoming = refs.pop(0) if number else None
-    upper, lower = refs.pop(0), refs.pop(0)
-    if turned_edges:
-        upper, lower = lower, upper
+    arrived = dict(zip(order, (refs.pop(0) for _ in order)))
+    upper, lower, incoming = arrived[-2], arrived[-1], arrived.get(0)
+    start_chunk = bounds[0] == 0
     ahead = [refs.pop(0) for _ in range(2 if number else 1)] if has_next else []
     weights = refs.pop(0)
     saved = [refs.pop(0) for _ in range(n_saved)]
@@ -179,10 +182,11 @@
             refs.pop(0)
         result = refs.pop(0)
     if has_next:
-        k_v, once, smooth, pack = refs
         own_v, up_s, down_s = own_out, up_out, down_out
-    else:
-        k_v, once, smooth, own_v, turned, sems = refs
+    k_v = refs.pop(0) if start_chunk else kappa
+    once, smooth, *rest = refs
+    if not has_next:
+        own_v, turned, sems = rest
     rows, _, cells = forcing.shape
     fields = bounds[1] - bounds[0]
     count, per_row = weights.shape[:2]
@@ -190,16 +194,30 @@
     extent = rows + 2 * halo
     lo, hi = halo, halo + rows
 
+    if not has_next:
+        part = rows // 2
+        stores = [
+            pltpu.make_async_copy(
+                turned.at[:, pl.ds(i * part, part)], result.at[pl.ds(bounds[0], fields), pl.ds(i * part, part)], sems.at[i]
+            )
+            for i in range(2)
+        ]
+
+        def store(i):
+            turned[:, i * part:(i + 1) * part, :] = jnp.swapaxes(own_v[i * part:(i + 1) * part], 0, 1)
+            stores[i].start()
+
     @pl.when(flags[0] == number)
     def _():
         mine = slice(*bounds)
         beside = beside_matrix(cells)
         top = jnp.where(flags[1] == 0, 0.0, 1.0)
         bottom = jnp.where(flags[1] == flags[2] - 1, 0.0, 1.0)
-        for edge, start in ((upper, 0), (lower, hi)):
-            parts = edge[halo:].astype(jnp.float32).reshape(-1, cells)
-            k_v[start:start + halo, :] = parts[:halo] + parts[halo:2 * halo] + parts[2 * halo:3 * halo]
-        k_v[lo:hi, :] = kappa[...]
+        if start_chunk:
+            for edge, start in ((upper, 0), (lower, hi)):
+                parts = edge[halo:].astype(jnp.float32).reshape(-1, cells)
+                k_v[start:start + halo, :] = parts[:halo] + parts[halo:2 * halo] + parts[2 * halo:3 * halo]
+            k_v[lo:hi, :] = kappa[...]
 
         def entry(i):
             if i < lo:
@@ -245,7 +263,8 @@
 
         half = (halo - EDGE) * cells // block
         block_rows = block // cells
-        if has_next:
+        if has_next and start_chunk:
+            pack, = rest
             if number:
                 up_s[halo:] = ahead[0][halo:]
                 down_s[halo:] = ahead[1][halo:]
@@ -278,21 +297,23 @@
                         up_s[row] = entry_next.astype(jnp.bfloat16)
                     if row >= rows - halo:
                         down_s[row - (rows - halo)] = entry_next.astype(jnp.bfloat16)
+                elif (row + 1) % part == 0:
+                    store(row // part)
 
     if not has_next:
-        for i, kept in enumerate(saved):
-            @pl.when(flags[0] == i)
-            def _(kept=kept):
-                copy = pltpu.make_async_copy(kept, own_v, sems.at[0])
-                copy.start()
-                copy.wait()
-
-        step_rows = 16
-        for y in range(0, rows, step_rows):
-            turned[:, y:y + step_rows, :] = jnp.swapaxes(own_v[y:y + step_rows], 0, 1)
-        copy = pltpu.make_async_copy(turned, result.at[pl.ds(bounds[0], fields)], sems.at[1])
-        copy.start()
-        copy.wait()
+        @pl.when(flags[0] != number)
+        def _():
+            for i, kept in enumerate(saved):
+                @pl.when(flags[0] == i)
+                def _(kept=kept):
+                    copy = pltpu.make_async_copy(kept, own_v, sems.at[len(stores)])
+                    copy.start()
+                    copy.wait()
+
+            for i in range(len(stores)):
+                store(i)
+
+        wait_all(stores)
 
 
 def section(number, bounds, halo, flags, offsets, kappa, forcing, arrived, following, weights, saved, result):
@@ -300,18 +321,16 @@
     fields = bounds[1] - bounds[0]
     count, per_row, block, _ = weights.shape
     has_next = bool(following)
-    turned_edges = number == 0 and bounds[0] > 0
-    if turned_edges:
-        arrived = arrived[::-1]
+    order = ORDERS[min(number, 1)][bounds[0] > 0]
+    arrived = [arrived[i] for i in order]
     operands = [flags, offsets, kappa, in_vmem(forcing)] + arrived
     operands += following
     specs = [SMEM] * 2 + [VMEM] * (len(operands) - 2)
     operands.append(in_vmem(weights))
     specs.append(VMEM)
     extent = rows + 2 * halo
-    packed = -(-3 * halo // fields)
+    packed = packed_rows(halo, *bounds)
     scratch = [
-        pltpu.VMEM((extent, cells), jnp.float32),
         pltpu.VMEM((extent, fields, cells), jnp.float32),
         pltpu.VMEM(((extent - 2 * EDGE) * cells // block, fields, block), jnp.bfloat16),
     ]
@@ -319,14 +338,15 @@
     if has_next:
         outs = [jax.ShapeDtypeStruct((n, fields, cells), jnp.bfloat16) for n in (rows, halo + packed, halo + packed)]
         out_specs = [VMEM] * 3
-        scratch.append(pltpu.VMEM((packed * fields, cells), jnp.float32))
+        if packed:
+            scratch.append(pltpu.VMEM((packed * fields, cells), jnp.float32))
     else:
         outs = [jax.ShapeDtypeStruct((total, rows, cells), jnp.bfloat16)]
         out_specs = [HBM]
         scratch += [
             pltpu.VMEM((rows, fields, cells), jnp.bfloat16),
             pltpu.VMEM((fields, rows, cells), jnp.bfloat16),
-            pltpu.SemaphoreType.DMA((2,)),
+            pltpu.SemaphoreType.DMA((3,)),
         ]
         operands += [in_hbm(value) for value in saved]
         specs += [HBM] * len(saved)
@@ -334,8 +354,11 @@
             aliases = {len(operands): 0}
             operands.append(result)
             specs.append(HBM)
+    if packed:
+        outs.append(jax.ShapeDtypeStruct((extent, cells), jnp.float32))
+        out_specs.append(VMEM)
     return pl.pallas_call(
-        functools.partial(section_kernel, turned_edges, number, bounds, halo, len(saved), has_next),
+        functools.partial(section_kernel, order, number, bounds, halo, len(saved), has_next),
         in_specs=specs,
         out_shape=outs,
         out_specs=out_specs,
@@ -390,11 +413,14 @@
     for s in range(n_section):
         last = s + 1 == n_section
         leaving = []
+        rates = kappa[0]
         for c, bounds in enumerate(zip(marks[:-1], marks[1:])):
-            parts = section(
-                s, bounds, halo, flags, offsets, kappa[0], by_row, arrivals[c], following[s][c],
+            parts = list(section(
+                s, bounds, halo, flags, offsets, rates, by_row, arrivals[c], following[s][c],
                 weights, owns[c] if last else [], result,
-            )
+            ))
+            if c == 0:
+                rates = parts.pop()
             if last:
                 result = parts[0]
                 continue

time: 84.2 us -> 79.2 us (0.941)
  starting transfers between devices: 48.1 us -> 43.6 us
    ppermute x22, starting transfers between devices: 47.3 us -> 42.9 us  [send(): return lax.ppermute(value, AXES, pairs)]
  transfers between devices with their start and end apart: 23 -> 23, of which waited for: 3 -> 3; matrix products, arithmetic and copies ran while one was open for 0% -> 0% of each run, Pallas kernels for 22% -> 23%
where the time goes in v4:
time: 79.2 us; the launch traced here: 78.9 us
  starting transfers between devices  43.6 us (55%)
  Pallas kernels  25.8 us (33%)
  waiting for transfers between devices  8.96 us (11%)
    ppermute x22, starting transfers between devices, send(): return lax.ppermute(value, AXES, pairs)  42.9 us
    pallas_call x8, Pallas kernels, section(): pl.pallas_call(functools.partial(section_kernel, order, number, bounds, h...  13.5 us
    pallas_call x1, Pallas kernels, load(): pl.pallas_call(functools.partial(load_kernel, len(passed)), in_specs=[SME...  9.7 us
    ppermute x22, waiting for transfers between devices, send(): return lax.ppermute(value, AXES, pairs)  8.96 us
    pallas_call x1, Pallas kernels, prepare(): pl.pallas_call(functools.partial(prepare_kernel, halo, marks), in_specs=[...  2.58 us
  transfers between devices with their start and end apart: 23, of which 3 were waited for; matrix products, arithmetic and copies ran while one was open for 0% of the time, Pallas kernels for 23%

profile of v4, /device:TPU:3, one launch (start us, length us, event | category | flops | bytes accessed | tf_op | source)
XLA Modules:
  0.0 78.9 jit_solution(8866938657813322607)
XLA Ops:
  0.0 0.1 pad_add_fusion.flags
  0.1 2.6 %shard_map.46 = (s32[4,16]{1,0:T(4,128)S(1)}, f32[32,128,128]{2,1,0:T(8,128)S(1)}, bf16[33,128,128]{2,1,0:T(8,128)(2,1)S(1)}, bf16[19,64,128]{2,1,0:T(8,128)(2,1...) custom-call(s32[3]{0:T(128)S(1)} %pad_add_fusion.flags, ...), custom_call_target="tpu_custom_call" | custom-call | bytes 6291456 | tf_op jit(solution)/shard_map/pallas_call | solution.py:109
  2.7 0.7 collective-permute-start.2
  3.4 0.1 collective-permute-start
  3.5 0.1 collective-permute-start.1
  3.6 9.7 %shard_map.47 = (bf16[16,4,256,256]{3,2,1,0:T(8,128)(2,1)S(1)}, bf16[19,64,128]{2,1,0:T(8,128)(2,1)S(1)}, bf16[19,64,128]{2,1,0:T(8,128)(2,1)S(1)}) custom-call(s32[3]{0:T(128)S(1)} %pad_add_fusion.flags, bf16[16,4,256,256]{3,2,1,0:T(8,128)(2,1)} %bitcast.14, ...), custom_call_target="tpu_custom_call", output_to_operand_aliasing={{1}: (2, {}), {2}: (3, {})} | custom-call | bytes 16777216 | tf_op jit(solution)/shard_map/pallas_call | solution.py:150
  13.3 1.8 %collective-permute-start.12 = (bf16[19,64,128]{2,1,0:T(8,128)(2,1)S(1)}, bf16[19,64,128]{2,1,0:T(8,128)(2,1)S(1)}, u32[]{:S(2)}, u32[]{:S(2)}) collective-permute-start(bf16[19,64,128]{2,1,0:T(8,128)(2,1)S(1)} %get-tuple-element.59), channel_id=1, source_target_pairs={{0,7},{1,0},{2,1},{3,2},{4,3},{5,4},{6,5},{7,6},{16,8},{17,9},{18,... | collective-permute-start | bytes 933896 | tf_op jit(solution)/shard_map/ppermute | solution.py:399
  15.0 0.1 collective-permute-start.13
  15.1 0.0 collective-permute-done.refs_0_.refs_4_
  15.1 0.0 collective-permute-done.1.refs_1_.refs_3_
  15.1 0.0 collective-permute-done.2.refs_2_
  15.1 0.0 copy-done
  15.1 0.6 shard_map.48
  15.7 0.0 copy-start.1
  15.7 0.1 collective-permute-start.3
  15.9 0.4 collective-permute-start.4
  16.3 0.1 collective-permute-start.5
  16.4 2.7 %collective-permute-done.12.refs_0_.refs_3_ = bf16[19,64,128]{2,1,0:T(8,128)(2,1)S(1)} collective-permute-done((bf16[19,64,128]{2,1,0:T(8,128)(2,1)S(1)}, bf16[19,64,128]{2,1,0:T(8,128)(2,1)S(1)}, u32[]{:S(2)}, u32[]{:S(2)}) %collective-permute-start.12) | collective-permute-done | bytes 311328 | tf_op jit(solution)/shard_map/ppermute | solution.py:399
  19.1 3.3 %collective-permute-done.13.refs_1_.refs_4_ = bf16[19,64,128]{2,1,0:T(8,128)(2,1)S(1)} collective-permute-done((bf16[19,64,128]{2,1,0:T(8,128)(2,1)S(1)}, bf16[19,64,128]{2,1,0:T(8,128)(2,1)S(1)}, u32[]{:S(2)}, u32[]{:S(2)}) %collective-permute-start.13) | collective-permute-done | bytes 311328 | tf_op jit(solution)/shard_map/ppermute | solution.py:399
  22.4 0.6 shard_map.52
  23.0 0.0 copy-done.1
  23.0 0.0 copy-start.2
  23.0 0.5 collective-permute-start.14
  23.5 0.1 collective-permute-start.15
  23.6 0.0 collective-permute-done.3.refs_0_
  23.6 0.4 collective-permute-start.16
  24.0 0.0 collective-permute-done.4.refs_1_
  24.0 0.0 collective-permute-done.5.refs_2_
  24.0 0.6 shard_map.49
  24.6 0.0 copy-done.2
  24.6 0.0 copy-start.3
  24.6 0.7 collective-permute-start.6
  25.3 0.7 collective-permute-start.7
  26.0 0.0 collective-permute-done.14.refs_0_
  26.0 0.7 collective-permute-start.8
  26.7 0.0 collective-permute-done.15.refs_1_
  26.7 0.0 collective-permute-done.16.refs_2_
  26.8 0.8 shard_map.53
  27.5 0.0 copy-done.3
  27.5 0.7 collective-permute-start.17
  28.2 0.7 collective-permute-start.18
  28.9 0.0 collective-permute-done.6.refs_0_
  28.9 0.7 collective-permute-start.19
  29.6 0.0 collective-permute-done.7.refs_1_
  29.6 0.0 collective-permute-done.8.refs_2_
  29.7 0.6 shard_map.50
  30.3 25.8 %collective-permute-start.9 = (bf16[19,64,128]{2,1,0:T(8,128)(2,1)S(1)}, bf16[19,64,128]{2,1,0:T(8,128)(2,1)S(1)}, u32[]{:S(2)}, u32[]{:S(2)}) collective-permute-start(bf16[19,64,128]{2,1,0:T(8,128)(2,1)S(1)} %get-tuple-element.52), channel_id=1, source_target_pairs={{16,31},{17,24},{18,25},{19,26},{20,27},{21,28},{22,29},{23,30},{2... | collective-permute-start | bytes 933896 | tf_op jit(solution)/shard_map/ppermute | solution.py:399
  56.1 0.1 collective-permute-start.10
  56.1 0.0 collective-permute-done.17.refs_0_
  56.1 0.1 collective-permute-start.11
  56.2 0.0 collective-permute-done.18.refs_1_
  56.2 0.0 collective-permute-done.19.refs_2_
  56.2 0.6 shard_map.54
  56.8 8.0 %collective-permute-start.20 = (bf16[18,64,128]{2,1,0:T(8,128)(2,1)S(1)}, bf16[18,64,128]{2,1,0:T(8,128)(2,1)S(1)}, u32[]{:S(2)}, u32[]{:S(2)}) collective-permute-start(bf16[18,64,128]{2,1,0:T(8,128)(2,1)S(1)} %get-tuple-element.67), channel_id=1, source_target_pairs={{16,31},{17,24},{18,25},{19,26},{20,27},{21,28},{22,29},{23,30},{2... | collective-permute-start | bytes 884744 | tf_op jit(solution)/shard_map/ppermute | solution.py:399
  64.8 0.1 collective-permute-start.21
  64.9 0.0 collective-permute-done.9.refs_0_
  64.9 1.1 %collective-permute-start.22 = (bf16[32,64,128]{2,1,0:T(8,128)(2,1)S(1)}, bf16[32,64,128]{2,1,0:T(8,128)(2,1)S(1)}, u32[]{:S(2)}, u32[]{:S(2)}) collective-permute-start(bf16[32,64,128]{2,1,0:T(8,128)(2,1)S(1)} %get-tuple-element.69.refs_6_), channel_id=1, source_target_pairs={{16,24},{17,25},{18,26},{19,27},{20,28},{21,29},{22,30},{23,31},{2... | collective-permute-start | bytes 1572872 | tf_op jit(solution)/shard_map/ppermute | solution.py:399
  66.0 0.0 collective-permute-done.10.refs_1_
  66.0 0.0 collective-permute-done.11.refs_2_
  66.0 4.8 %shard_map.51 = (bf16[128,32,128]{2,1,0:T(8,128)(2,1)}, f32[68,128]{1,0:T(8,128)S(1)}) custom-call(s32[3]{0:T(128)S(1)} %pad_add_fusion.flags, s32[4,16]{1,0:T(4,128)S(1)} %get-tuple-element.38.offsets, f32[32,128]{1,0:T(8,128)S(1)} %bitcast.13, f32[32,128,128]{2,1,0:T(8,128)S(1)} %get-tuple-element.39.forcing, ...), custom_call_target="tpu_custom_call" | custom-call | flops 10737418240 | bytes 8388608 | tf_op jit(solution)/shard_map/pallas_call | solution.py:360
  70.8 0.0 collective-permute-done.20.refs_0_
  70.8 2.9 %collective-permute-done.21.refs_1_ = bf16[18,64,128]{2,1,0:T(8,128)(2,1)S(1)} collective-permute-done((bf16[18,64,128]{2,1,0:T(8,128)(2,1)S(1)}, bf16[18,64,128]{2,1,0:T(8,128)(2,1)S(1)}, u32[]{:S(2)}, u32[]{:S(2)}) %collective-permute-start.21) | collective-permute-done | bytes 294944 | tf_op jit(solution)/shard_map/ppermute | solution.py:399
  73.7 0.0 collective-permute-done.22.refs_2_
  73.7 5.0 %shard_map.55 = bf16[128,32,128]{2,1,0:T(8,128)(2,1)} custom-call(s32[3]{0:T(128)S(1)} %pad_add_fusion.flags, s32[4,16]{1,0:T(4,128)S(1)} %get-tuple-element.38.offsets, f32[68,128]{1,0:T(8,128)S(1)} %get-tuple-element.55.kappa, f32[32,128,128]{2,1,0:T(8,128)S(1)} %get-tuple-element.39.forcing, ...), custom_call_target="tpu_custom_call", output_to_operand_aliasing={{}: (11, {})} | custom-call | flops 10737418240 | bytes 8388608 | tf_op jit(solution)/shard_map/pallas_call | solution.py:360
  (7 shorter events, 0.0 us)
Async XLA Ops:
  2.7 12.5 %collective-permute-start.2 = (bf16[33,128,128]{2,1,0:T(8,128)(2,1)S(1)}, bf16[33,128,128]{2,1,0:T(8,128)(2,1)S(1)}, u32[]{:S(2)}, u32[]{:S(2)}) collective-permute-start(bf16[33,128,128]{2,1,0:T(8,128)(2,1)S(1)} %get-tuple-element.42), channel_id=1, source_target_pairs={{0,8},{8,0},{16,24},{24,16},{1,9},{9,1},{17,25},{25,17},{2,10},{10... | collective-permute-start | bytes 3244040 | tf_op jit(solution)/shard_map/ppermute | solution.py:409
  3.4 11.7 %collective-permute-start = (bf16[19,64,128]{2,1,0:T(8,128)(2,1)S(1)}, bf16[19,64,128]{2,1,0:T(8,128)(2,1)S(1)}, u32[]{:S(2)}, u32[]{:S(2)}) collective-permute-start(bf16[19,64,128]{2,1,0:T(8,128)(2,1)S(1)} %get-tuple-element.40), channel_id=1, source_target_pairs={{0,1},{1,2},{2,3},{3,4},{4,5},{5,6},{6,7},{7,0},{16,8},{17,9},{18,... | collective-permute-start | bytes 933896 | tf_op jit(solution)/shard_map/ppermute | solution.py:399
  3.5 11.6 %collective-permute-start.1 = (bf16[19,64,128]{2,1,0:T(8,128)(2,1)S(1)}, bf16[19,64,128]{2,1,0:T(8,128)(2,1)S(1)}, u32[]{:S(2)}, u32[]{:S(2)}) collective-permute-start(bf16[19,64,128]{2,1,0:T(8,128)(2,1)S(1)} %get-tuple-element.41), channel_id=1, source_target_pairs={{0,7},{1,0},{2,1},{3,2},{4,3},{5,4},{6,5},{7,6},{16,8},{17,9},{18,... | collective-permute-start | bytes 933896 | tf_op jit(solution)/shard_map/ppermute | solution.py:399
  3.6 11.6 %copy-start = (f32[1,32,128]{2,1,0:T(8,128)S(1)}, f32[1,32,128]{2,1,0:T(8,128)}, u32[]{:S(2)}) copy-start(f32[1,32,128]{2,1,0:T(8,128)} %param.5) | copy-start | bytes 49156
  13.3 5.8 %collective-permute-start.12 = (bf16[19,64,128]{2,1,0:T(8,128)(2,1)S(1)}, bf16[19,64,128]{2,1,0:T(8,128)(2,1)S(1)}, u32[]{:S(2)}, u32[]{:S(2)}) collective-permute-start(bf16[19,64,128]{2,1,0:T(8,128)(2,1)S(1)} %get-tuple-element.59), channel_id=1, source_target_pairs={{0,7},{1,0},{2,1},{3,2},{4,3},{5,4},{6,5},{7,6},{16,8},{17,9},{18,... | collective-permute-start | bytes 933896 | tf_op jit(solution)/shard_map/ppermute | solution.py:399
  15.0 7.4 %collective-permute-start.13 = (bf16[19,64,128]{2,1,0:T(8,128)(2,1)S(1)}, bf16[19,64,128]{2,1,0:T(8,128)(2,1)S(1)}, u32[]{:S(2)}, u32[]{:S(2)}) collective-permute-start(bf16[19,64,128]{2,1,0:T(8,128)(2,1)S(1)} %get-tuple-element.60), channel_id=1, source_target_pairs={{0,1},{1,2},{2,3},{3,4},{4,5},{5,6},{6,7},{7,0},{16,8},{17,9},{18,... | collective-permute-start | bytes 933896 | tf_op jit(solution)/shard_map/ppermute | solution.py:399
  15.7 7.3 %copy-start.1 = (bf16[32,64,128]{2,1,0:T(8,128)(2,1)}, bf16[32,64,128]{2,1,0:T(8,128)(2,1)S(1)}, u32[]{:S(2)}) copy-start(bf16[32,64,128]{2,1,0:T(8,128)(2,1)S(1)} %get-tuple-element.48.refs_4_) | copy-start | bytes 1572868
  15.7 7.9 %collective-permute-start.3 = (bf16[19,64,128]{2,1,0:T(8,128)(2,1)S(1)}, bf16[19,64,128]{2,1,0:T(8,128)(2,1)S(1)}, u32[]{:S(2)}, u32[]{:S(2)}) collective-permute-start(bf16[19,64,128]{2,1,0:T(8,128)(2,1)S(1)} %get-tuple-element.46), channel_id=1, source_target_pairs={{0,15},{1,8},{2,9},{3,10},{4,11},{5,12},{6,13},{7,14},{8,0},{9,1},... | collective-permute-start | bytes 933896 | tf_op jit(solution)/shard_map/ppermute | solution.py:399
  15.9 8.2 %collective-permute-start.4 = (bf16[19,64,128]{2,1,0:T(8,128)(2,1)S(1)}, bf16[19,64,128]{2,1,0:T(8,128)(2,1)S(1)}, u32[]{:S(2)}, u32[]{:S(2)}) collective-permute-start(bf16[19,64,128]{2,1,0:T(8,128)(2,1)S(1)} %get-tuple-element.47), channel_id=1, source_target_pairs={{0,9},{1,10},{2,11},{3,12},{4,13},{5,14},{6,15},{7,8},{8,0},{9,1},... | collective-permute-start | bytes 933896 | tf_op jit(solution)/shard_map/ppermute | solution.py:399
  16.3 7.7 %collective-permute-start.5 = (bf16[32,64,128]{2,1,0:T(8,128)(2,1)S(1)}, bf16[32,64,128]{2,1,0:T(8,128)(2,1)S(1)}, u32[]{:S(2)}, u32[]{:S(2)}) collective-permute-start(bf16[32,64,128]{2,1,0:T(8,128)(2,1)S(1)} %get-tuple-element.48.refs_4_), channel_id=1, source_target_pairs={{0,8},{1,9},{2,10},{3,11},{4,12},{5,13},{6,14},{7,15},{8,0},{9,1},... | collective-permute-start | bytes 1572872 | tf_op jit(solution)/shard_map/ppermute | solution.py:399
  23.0 1.6 %copy-start.2 = (bf16[32,64,128]{2,1,0:T(8,128)(2,1)}, bf16[32,64,128]{2,1,0:T(8,128)(2,1)S(1)}, u32[]{:S(2)}) copy-start(bf16[32,64,128]{2,1,0:T(8,128)(2,1)S(1)} %get-tuple-element.63.refs_4_) | copy-start | bytes 1572868
  23.0 3.0 %collective-permute-start.14 = (bf16[18,64,128]{2,1,0:T(8,128)(2,1)S(1)}, bf16[18,64,128]{2,1,0:T(8,128)(2,1)S(1)}, u32[]{:S(2)}, u32[]{:S(2)}) collective-permute-start(bf16[18,64,128]{2,1,0:T(8,128)(2,1)S(1)} %get-tuple-element.61), channel_id=1, source_target_pairs={{0,15},{1,8},{2,9},{3,10},{4,11},{5,12},{6,13},{7,14},{8,0},{9,1},... | collective-permute-start | bytes 884744 | tf_op jit(solution)/shard_map/ppermute | solution.py:399
  23.5 3.2 %collective-permute-start.15 = (bf16[18,64,128]{2,1,0:T(8,128)(2,1)S(1)}, bf16[18,64,128]{2,1,0:T(8,128)(2,1)S(1)}, u32[]{:S(2)}, u32[]{:S(2)}) collective-permute-start(bf16[18,64,128]{2,1,0:T(8,128)(2,1)S(1)} %get-tuple-element.62), channel_id=1, source_target_pairs={{0,9},{1,10},{2,11},{3,12},{4,13},{5,14},{6,15},{7,8},{8,0},{9,1},... | collective-permute-start | bytes 884744 | tf_op jit(solution)/shard_map/ppermute | solution.py:399
  23.6 3.2 %collective-permute-start.16 = (bf16[32,64,128]{2,1,0:T(8,128)(2,1)S(1)}, bf16[32,64,128]{2,1,0:T(8,128)(2,1)S(1)}, u32[]{:S(2)}, u32[]{:S(2)}) collective-permute-start(bf16[32,64,128]{2,1,0:T(8,128)(2,1)S(1)} %get-tuple-element.63.refs_4_), channel_id=1, source_target_pairs={{0,8},{1,9},{2,10},{3,11},{4,12},{5,13},{6,14},{7,15},{8,0},{9,1},... | collective-permute-start | bytes 1572872 | tf_op jit(solution)/shard_map/ppermute | solution.py:399
  24.6 2.9 %copy-start.3 = (bf16[32,64,128]{2,1,0:T(8,128)(2,1)}, bf16[32,64,128]{2,1,0:T(8,128)(2,1)S(1)}, u32[]{:S(2)}) copy-start(bf16[32,64,128]{2,1,0:T(8,128)(2,1)S(1)} %get-tuple-element.51.refs_5_) | copy-start | bytes 1572868
  24.6 4.3 %collective-permute-start.6 = (bf16[19,64,128]{2,1,0:T(8,128)(2,1)S(1)}, bf16[19,64,128]{2,1,0:T(8,128)(2,1)S(1)}, u32[]{:S(2)}, u32[]{:S(2)}) collective-permute-start(bf16[19,64,128]{2,1,0:T(8,128)(2,1)S(1)} %get-tuple-element.49), channel_id=1, source_target_pairs={{8,23},{9,16},{10,17},{11,18},{12,19},{13,20},{14,21},{15,22}} | collective-permute-start | bytes 933896 | tf_op jit(solution)/shard_map/ppermute | solution.py:399
  25.3 4.3 %collective-permute-start.7 = (bf16[19,64,128]{2,1,0:T(8,128)(2,1)S(1)}, bf16[19,64,128]{2,1,0:T(8,128)(2,1)S(1)}, u32[]{:S(2)}, u32[]{:S(2)}) collective-permute-start(bf16[19,64,128]{2,1,0:T(8,128)(2,1)S(1)} %get-tuple-element.50), channel_id=1, source_target_pairs={{8,17},{9,18},{10,19},{11,20},{12,21},{13,22},{14,23},{15,16}} | collective-permute-start | bytes 933896 | tf_op jit(solution)/shard_map/ppermute | solution.py:399
  26.0 3.6 %collective-permute-start.8 = (bf16[32,64,128]{2,1,0:T(8,128)(2,1)S(1)}, bf16[32,64,128]{2,1,0:T(8,128)(2,1)S(1)}, u32[]{:S(2)}, u32[]{:S(2)}) collective-permute-start(bf16[32,64,128]{2,1,0:T(8,128)(2,1)S(1)} %get-tuple-element.51.refs_5_), channel_id=1, source_target_pairs={{8,16},{9,17},{10,18},{11,19},{12,20},{13,21},{14,22},{15,23}} | collective-permute-start | bytes 1572872 | tf_op jit(solution)/shard_map/ppermute | solution.py:399
  27.5 2.7 %copy-start.4 = (bf16[32,64,128]{2,1,0:T(8,128)(2,1)}, bf16[32,64,128]{2,1,0:T(8,128)(2,1)S(1)}, u32[]{:S(2)}) copy-start(bf16[32,64,128]{2,1,0:T(8,128)(2,1)S(1)} %get-tuple-element.66.refs_5_) | copy-start | bytes 1572868
  27.5 28.6 %collective-permute-start.17 = (bf16[18,64,128]{2,1,0:T(8,128)(2,1)S(1)}, bf16[18,64,128]{2,1,0:T(8,128)(2,1)S(1)}, u32[]{:S(2)}, u32[]{:S(2)}) collective-permute-start(bf16[18,64,128]{2,1,0:T(8,128)(2,1)S(1)} %get-tuple-element.64), channel_id=1, source_target_pairs={{8,23},{9,16},{10,17},{11,18},{12,19},{13,20},{14,21},{15,22}} | collective-permute-start | bytes 884744 | tf_op jit(solution)/shard_map/ppermute | solution.py:399
  28.2 28.0 %collective-permute-start.18 = (bf16[18,64,128]{2,1,0:T(8,128)(2,1)S(1)}, bf16[18,64,128]{2,1,0:T(8,128)(2,1)S(1)}, u32[]{:S(2)}, u32[]{:S(2)}) collective-permute-start(bf16[18,64,128]{2,1,0:T(8,128)(2,1)S(1)} %get-tuple-element.65), channel_id=1, source_target_pairs={{8,17},{9,18},{10,19},{11,20},{12,21},{13,22},{14,23},{15,16}} | collective-permute-start | bytes 884744 | tf_op jit(solution)/shard_map/ppermute | solution.py:399
  28.9 27.3 %collective-permute-start.19 = (bf16[32,64,128]{2,1,0:T(8,128)(2,1)S(1)}, bf16[32,64,128]{2,1,0:T(8,128)(2,1)S(1)}, u32[]{:S(2)}, u32[]{:S(2)}) collective-permute-start(bf16[32,64,128]{2,1,0:T(8,128)(2,1)S(1)} %get-tuple-element.66.refs_5_), channel_id=1, source_target_pairs={{8,16},{9,17},{10,18},{11,19},{12,20},{13,21},{14,22},{15,23}} | collective-permute-start | bytes 1572872 | tf_op jit(solution)/shard_map/ppermute | solution.py:399
  30.3 26.6 %copy-start.5 = (bf16[32,64,128]{2,1,0:T(8,128)(2,1)}, bf16[32,64,128]{2,1,0:T(8,128)(2,1)S(1)}, u32[]{:S(2)}) copy-start(bf16[32,64,128]{2,1,0:T(8,128)(2,1)S(1)} %get-tuple-element.54.refs_6_) | copy-start | bytes 1572868
  30.3 34.6 %collective-permute-start.9 = (bf16[19,64,128]{2,1,0:T(8,128)(2,1)S(1)}, bf16[19,64,128]{2,1,0:T(8,128)(2,1)S(1)}, u32[]{:S(2)}, u32[]{:S(2)}) collective-permute-start(bf16[19,64,128]{2,1,0:T(8,128)(2,1)S(1)} %get-tuple-element.52), channel_id=1, source_target_pairs={{16,31},{17,24},{18,25},{19,26},{20,27},{21,28},{22,29},{23,30},{2... | collective-permute-start | bytes 933896 | tf_op jit(solution)/shard_map/ppermute | solution.py:399
  56.1 9.9 %collective-permute-start.10 = (bf16[19,64,128]{2,1,0:T(8,128)(2,1)S(1)}, bf16[19,64,128]{2,1,0:T(8,128)(2,1)S(1)}, u32[]{:S(2)}, u32[]{:S(2)}) collective-permute-start(bf16[19,64,128]{2,1,0:T(8,128)(2,1)S(1)} %get-tuple-element.53), channel_id=1, source_target_pairs={{16,25},{17,26},{18,27},{19,28},{20,29},{21,30},{22,31},{23,24},{2... | collective-permute-start | bytes 933896 | tf_op jit(solution)/shard_map/ppermute | solution.py:399
  56.1 9.9 %collective-permute-start.11 = (bf16[32,64,128]{2,1,0:T(8,128)(2,1)S(1)}, bf16[32,64,128]{2,1,0:T(8,128)(2,1)S(1)}, u32[]{:S(2)}, u32[]{:S(2)}) collective-permute-start(bf16[32,64,128]{2,1,0:T(8,128)(2,1)S(1)} %get-tuple-element.54.refs_6_), channel_id=1, source_target_pairs={{16,24},{17,25},{18,26},{19,27},{20,28},{21,29},{22,30},{23,31},{2... | collective-permute-start | bytes 1572872 | tf_op jit(solution)/shard_map/ppermute | solution.py:399
  56.8 14.0 %copy-start.6 = (bf16[32,64,128]{2,1,0:T(8,128)(2,1)}, bf16[32,64,128]{2,1,0:T(8,128)(2,1)S(1)}, u32[]{:S(2)}) copy-start(bf16[32,64,128]{2,1,0:T(8,128)(2,1)S(1)} %get-tuple-element.69.refs_6_) | copy-start | bytes 1572868
  56.8 14.0 %collective-permute-start.20 = (bf16[18,64,128]{2,1,0:T(8,128)(2,1)S(1)}, bf16[18,64,128]{2,1,0:T(8,128)(2,1)S(1)}, u32[]{:S(2)}, u32[]{:S(2)}) collective-permute-start(bf16[18,64,128]{2,1,0:T(8,128)(2,1)S(1)} %get-tuple-element.67), channel_id=1, source_target_pairs={{16,31},{17,24},{18,25},{19,26},{20,27},{21,28},{22,29},{23,30},{2... | collective-permute-start | bytes 884744 | tf_op jit(solution)/shard_map/ppermute | solution.py:399
  64.8 8.8 %collective-permute-start.21 = (bf16[18,64,128]{2,1,0:T(8,128)(2,1)S(1)}, bf16[18,64,128]{2,1,0:T(8,128)(2,1)S(1)}, u32[]{:S(2)}, u32[]{:S(2)}) collective-permute-start(bf16[18,64,128]{2,1,0:T(8,128)(2,1)S(1)} %get-tuple-element.68), channel_id=1, source_target_pairs={{16,25},{17,26},{18,27},{19,28},{20,29},{21,30},{22,31},{23,24},{2... | collective-permute-start | bytes 884744 | tf_op jit(solution)/shard_map/ppermute | solution.py:399
  64.9 8.8 %collective-permute-start.22 = (bf16[32,64,128]{2,1,0:T(8,128)(2,1)S(1)}, bf16[32,64,128]{2,1,0:T(8,128)(2,1)S(1)}, u32[]{:S(2)}, u32[]{:S(2)}) collective-permute-start(bf16[32,64,128]{2,1,0:T(8,128)(2,1)S(1)} %get-tuple-element.69.refs_6_), channel_id=1, source_target_pairs={{16,24},{17,25},{18,26},{19,27},{20,28},{21,29},{22,30},{23,31},{2... | collective-permute-start | bytes 1572872 | tf_op jit(solution)/shard_map/ppermute | solution.py:399

commit v5 on v4

--- a/solution.py
+++ b/solution.py
@@ -59,8 +59,8 @@
     return room[...].astype(jnp.bfloat16)
 
 
-def prepare_kernel(halo, marks, flags, columns, forcing, kappa, *refs):
-    offsets, by_row, narrow, *edges, c_v, f_v, k_v, pack, sems, k_sem, c_sem = refs
+def prepare_kernel(halo, marks, _, forcing, kappa, *refs):
+    by_row, narrow, *edges, f_v, k_v, pack, sems, k_sem = refs
     total, rows, cells = f_v.shape
     step = rows // sems.shape[0]
     loads = []
@@ -68,16 +68,8 @@
         part = pl.ds(i * step, step)
         loads.append(pltpu.make_async_copy(forcing.at[:, part], f_v.at[:, part], sems.at[i]))
     fetch = pltpu.make_async_copy(kappa, k_v, k_sem)
-    take = pltpu.make_async_copy(columns, c_v, c_sem)
-    take.start()
     fetch.start()
     start_all(loads)
-    take.wait()
-    count = columns.shape[1]
-    ahead = c_v[...] - (flags[1] * count + lax.broadcasted_iota(jnp.int32, columns.shape, 1)) + count // 2
-    every = flags[2] * count
-    ahead = jnp.where(ahead < 0, ahead + every, jnp.where(ahead >= every, ahead - every, ahead))
-    offsets[...] = ahead - count // 2
     fetch.wait()
     parts = split(k_v[...])
     narrow[rows] = joined(parts, pack)
@@ -100,7 +92,7 @@
                     edge_last[y - (rows - halo)] = value[start:stop]
 
 
-def prepare(flags, columns, fields, kappa, halo, marks):
+def prepare(flags, fields, kappa, halo, marks):
     edges = [
         jax.ShapeDtypeStruct((halo + packed_rows(halo, 0, stop - start), stop - start, kappa.shape[1]), jnp.bfloat16)
         for start, stop in zip(marks[:-1], marks[1:]) for _ in range(2)
@@ -108,32 +100,37 @@
     total, rows, cells = fields.shape
     return pl.pallas_call(
         functools.partial(prepare_kernel, halo, marks),
-        in_specs=[SMEM, HBM, HBM, HBM],
+        in_specs=[ANY, HBM, HBM],
         out_shape=[
-            jax.ShapeDtypeStruct(columns.shape, columns.dtype),
             pltpu.VMEM((rows, total, cells), jnp.float32),
             jax.ShapeDtypeStruct((rows + 1, total, cells), jnp.bfloat16),
         ] + edges,
-        out_specs=[VMEM] * (3 + len(edges)),
+        out_specs=[VMEM] * (2 + len(edges)),
         scratch_shapes=[
-            pltpu.VMEM(columns.shape, columns.dtype),
             pltpu.VMEM((total, rows, cells), jnp.float32),
             pltpu.VMEM(kappa.shape, kappa.dtype),
             pltpu.VMEM((total, cells), jnp.float32),
             pltpu.SemaphoreType.DMA((rows // 8,)),
             pltpu.SemaphoreType.DMA,
-            pltpu.SemaphoreType.DMA,
         ],
         compiler_params=pltpu.CompilerParams(vmem_limit_bytes=LIMIT),
         cost_estimate=pl.CostEstimate(flops=0, bytes_accessed=fields.size * 12, transcendentals=0),
-    )(flags, in_hbm(columns), in_hbm(fields), in_hbm(kappa))
-
-
-def load_kernel(n_passed, flags, weights, *refs):
-    held, sems = refs[n_passed], refs[-1]
+    )(flags, in_hbm(fields), in_hbm(kappa))
+
+
+def load_kernel(n_passed, flags, columns, weights, *refs):
+    held, offsets = refs[n_passed:n_passed + 2]
+    c_v, sems, c_sem = refs[-3:]
     count, per_row = weights.shape[:2]
+    take = pltpu.make_async_copy(columns, c_v, c_sem)
+    take.start()
     loads = [pltpu.make_async_copy(weights.at[j], held.at[j], sems.at[j]) for j in range(count)]
     start_all(loads)
+    take.wait()
+    ahead = c_v[...] - (flags[1] * count + lax.broadcasted_iota(jnp.int32, c_v.shape, 1)) + count // 2
+    every = flags[2] * count
+    ahead = jnp.where(ahead < 0, ahead + every, jnp.where(ahead >= every, ahead - every, ahead))
+    offsets[...] = ahead - count // 2
     wait_all(loads)
 
     @pl.when(flags[0] != 0)
@@ -146,17 +143,23 @@
         lax.fori_loop(0, count * per_row, turn, 0, unroll=4)
 
 
-def load(flags, weights, passed):
+def load(flags, columns, weights, passed):
     return pl.pallas_call(
         functools.partial(load_kernel, len(passed)),
-        in_specs=[SMEM, HBM] + [ANY] * len(passed),
-        out_shape=[pltpu.VMEM(weights.shape, weights.dtype)] + [jax.ShapeDtypeStruct(p.shape, p.dtype) for p in passed],
-        out_specs=[VMEM] + [ANY] * len(passed),
-        input_output_aliases={2 + i: 1 + i for i in range(len(passed))},
-        scratch_shapes=[pltpu.SemaphoreType.DMA((weights.shape[0],))],
+        in_specs=[SMEM, HBM, HBM] + [ANY] * len(passed),
+        out_shape=[
+            pltpu.VMEM(weights.shape, weights.dtype), jax.ShapeDtypeStruct(columns.shape, columns.dtype)
+        ] + [jax.ShapeDtypeStruct(p.shape, p.dtype) for p in passed],
+        out_specs=[VMEM, VMEM] + [ANY] * len(passed),
+        input_output_aliases={3 + i: 2 + i for i in range(len(passed))},
+        scratch_shapes=[
+            pltpu.VMEM(columns.shape, columns.dtype),
+            pltpu.SemaphoreType.DMA((weights.shape[0],)),
+            pltpu.SemaphoreType.DMA,
+        ],
         compiler_params=pltpu.CompilerParams(vmem_limit_bytes=LIMIT),
         cost_estimate=pl.CostEstimate(flops=0, bytes_accessed=weights.size * 4, transcendentals=0),
-    )(flags, in_hbm(weights), *passed)
+    )(flags, in_hbm(columns), in_hbm(weights), *passed)
 
 
 def beside_matrix(cells):
@@ -238,7 +241,8 @@
                 north = north * bottom
             if i == hi - 1:
                 south = south * bottom
-            return here + k_v[i:i + 1, :] * ((north + south) + (east_west - 4.0 * here))
+            rate = k_v[i:i + 1, :]
+            return (1.0 - 4.0 * rate) * here + rate * ((north + south) + east_west)
 
         def pair_beside(a, b):
             both = jnp.concatenate([a.astype(jnp.bfloat16), b.astype(jnp.bfloat16)], axis=1)
@@ -391,6 +395,9 @@
         others = [s for s in range(n_section) if s not in (source, target)]
         if source == target:
             rest = list(zip(others[1:] + others[:1], others))
+        elif n_section % 2 == 0 and source % 2:
+            rest = [(target, target ^ 1), (target ^ 1, source ^ 1), (source ^ 1, source)]
+            rest += [(s, s ^ 1) for s in others if s not in (target ^ 1, source ^ 1)]
         elif source ^ 1 == target and n_section % 2 == 0:
             rest = [(target, source)] + [(s, s ^ 1) for s in others]
         else:
@@ -400,8 +407,8 @@
 
     fields = forcing.reshape(-1, rows, cells)
     marks = [fields.shape[0] * sum(SHARES[:c]) // sum(SHARES) for c in range(len(SHARES) + 1)]
-    offsets, by_row, narrow, *edges = prepare(flags, col_blocks[0].T, fields, kappa[0], halo, marks)
-    weights, *edges[2:] = load(flags, weights, edges[2:])
+    by_row, narrow, *edges = prepare(flags, fields, kappa[0], halo, marks)
+    weights, offsets, *edges[2:] = load(flags, col_blocks[0].T, weights, edges[2:])
     arrivals = []
     for c in range(len(SHARES)):
         sends = [(edges[2 * c + 1], 1), (edges[2 * c], -1)][::1 - c % 2 * 2]

time: 79.2 us -> 77 us (0.972)
  starting transfers between devices: 43.6 us -> 41.2 us
  waiting for transfers between devices: 8.96 us -> 10 us
    ppermute x22, starting transfers between devices: 42.9 us -> 40.5 us  [send(): return lax.ppermute(value, AXES, pairs)]
    ppermute x22, waiting for transfers between devices: 8.96 us -> 10 us  [send(): return lax.ppermute(value, AXES, pairs)]
  transfers between devices with their start and end apart: 23 -> 23, of which waited for: 3 -> 4; matrix products, arithmetic and copies ran while one was open for 0% -> 0% of each run, Pallas kernels for 23% -> 24%
where the time goes in v5:
time: 77 us; the launch traced here: 76.8 us
  starting transfers between devices  41.2 us (54%)
  Pallas kernels  25.1 us (33%)
  waiting for transfers between devices  10 us (13%)
    ppermute x22, starting transfers between devices, send(): return lax.ppermute(value, AXES, pairs)  40.5 us
    pallas_call x8, Pallas kernels, section(): pl.pallas_call(functools.partial(section_kernel, order, number, bounds, h...  13.3 us
    ppermute x22, waiting for transfers between devices, send(): return lax.ppermute(value, AXES, pairs)  10 us
    pallas_call x1, Pallas kernels, load(): pl.pallas_call(functools.partial(load_kernel, len(passed)), in_specs=[SME...  9.72 us
    pallas_call x1, Pallas kernels, prepare(): pl.pallas_call(functools.partial(prepare_kernel, halo, marks), in_specs=[...  2.03 us
  transfers between devices with their start and end apart: 23, of which 4 were waited for; matrix products, arithmetic and copies ran while one was open for 0% of the time, Pallas kernels for 24%

profile of v5, /device:TPU:3, one launch (start us, length us, event | category | flops | bytes accessed | tf_op | source)
XLA Modules:
  0.0 76.8 jit_solution(8666436374476421860)
XLA Ops:
  0.0 0.1 pad_add_fusion._.flags
  0.1 2.0 %shard_map.46 = (f32[32,128,128]{2,1,0:T(8,128)S(1)}, bf16[33,128,128]{2,1,0:T(8,128)(2,1)S(1)}, bf16[19,64,128]{2,1,0:T(8,128)(2,1)S(1)}, bf16[19,64,128]{2,1,0...) custom-call(s32[3]{0:T(128)S(1)} %pad_add_fusion._.flags, ...), custom_call_target="tpu_custom_call" | custom-call | bytes 6291456 | tf_op jit(solution)/shard_map/pallas_call | solution.py:101
  2.1 0.7 collective-permute-start.2
  2.9 0.1 collective-permute-start
  2.9 0.1 collective-permute-start.1
  3.0 9.7 %shard_map.47 = (bf16[16,4,256,256]{3,2,1,0:T(8,128)(2,1)S(1)}, s32[4,16]{1,0:T(4,128)S(1)}, bf16[19,64,128]{2,1,0:T(8,128)(2,1)S(1)}, bf16[19,64,128]{2,1,0:T(8,128)(2,1)S(1)}) custom-call(s32[3]{0:T(128)S(1)} %pad_add_fusion._.flags, s32[4,16]{1,0:T(4,128)} %bitcast.16, ...), custom_call_target="tpu_custom_call", output_to_operand_aliasing={{2}: (3, {}), {3}: (4, {})} | custom-call | bytes 16777216 | tf_op jit(solution)/shard_map/pallas_call | solution.py:147
  12.7 1.8 %collective-permute-start.12 = (bf16[19,64,128]{2,1,0:T(8,128)(2,1)S(1)}, bf16[19,64,128]{2,1,0:T(8,128)(2,1)S(1)}, u32[]{:S(2)}, u32[]{:S(2)}) collective-permute-start(bf16[19,64,128]{2,1,0:T(8,128)(2,1)S(1)} %get-tuple-element.59), channel_id=1, source_target_pairs={{0,7},{1,0},{2,1},{3,2},{4,3},{5,4},{6,5},{7,6},{16,8},{17,9},{18,... | collective-permute-start | bytes 933896 | tf_op jit(solution)/shard_map/ppermute | solution.py:406
  14.5 0.1 collective-permute-start.13
  14.6 0.0 collective-permute-done.refs_0_.refs_4_
  14.6 0.0 collective-permute-done.1.refs_1_.refs_3_
  14.6 0.0 collective-permute-done.2.refs_2_
  14.6 0.0 copy-done
  14.6 0.6 shard_map.48
  15.2 0.0 copy-start.1
  15.2 0.1 collective-permute-start.3
  15.3 0.4 collective-permute-start.4
  15.8 0.1 collective-permute-start.5
  15.8 2.7 %collective-permute-done.12.refs_0_.refs_3_ = bf16[19,64,128]{2,1,0:T(8,128)(2,1)S(1)} collective-permute-done((bf16[19,64,128]{2,1,0:T(8,128)(2,1)S(1)}, bf16[19,64,128]{2,1,0:T(8,128)(2,1)S(1)}, u32[]{:S(2)}, u32[]{:S(2)}) %collective-permute-start.12) | collective-permute-done | bytes 311328 | tf_op jit(solution)/shard_map/ppermute | solution.py:406
  18.5 3.3 %collective-permute-done.13.refs_1_.refs_4_ = bf16[19,64,128]{2,1,0:T(8,128)(2,1)S(1)} collective-permute-done((bf16[19,64,128]{2,1,0:T(8,128)(2,1)S(1)}, bf16[19,64,128]{2,1,0:T(8,128)(2,1)S(1)}, u32[]{:S(2)}, u32[]{:S(2)}) %collective-permute-start.13) | collective-permute-done | bytes 311328 | tf_op jit(solution)/shard_map/ppermute | solution.py:406
  21.9 0.6 shard_map.52
  22.5 0.0 copy-done.1
  22.5 0.5 collective-permute-start.14
  23.0 0.1 collective-permute-start.15
  23.0 0.0 collective-permute-done.3.refs_0_
  23.0 0.4 collective-permute-start.16
  23.5 0.0 collective-permute-done.4.refs_1_
  23.5 0.0 collective-permute-done.5.refs_2_
  23.5 0.6 shard_map.49
  24.1 6.4 %collective-permute-start.6 = (bf16[19,64,128]{2,1,0:T(8,128)(2,1)S(1)}, bf16[19,64,128]{2,1,0:T(8,128)(2,1)S(1)}, u32[]{:S(2)}, u32[]{:S(2)}) collective-permute-start(bf16[19,64,128]{2,1,0:T(8,128)(2,1)S(1)} %get-tuple-element.49), channel_id=1, source_target_pairs={{8,23},{9,16},{10,17},{11,18},{12,19},{13,20},{14,21},{15,22},{16,... | collective-permute-start | bytes 933896 | tf_op jit(solution)/shard_map/ppermute | solution.py:406
  30.5 3.4 %collective-permute-start.7 = (bf16[19,64,128]{2,1,0:T(8,128)(2,1)S(1)}, bf16[19,64,128]{2,1,0:T(8,128)(2,1)S(1)}, u32[]{:S(2)}, u32[]{:S(2)}) collective-permute-start(bf16[19,64,128]{2,1,0:T(8,128)(2,1)S(1)} %get-tuple-element.50), channel_id=1, source_target_pairs={{8,17},{9,18},{10,19},{11,20},{12,21},{13,22},{14,23},{15,16},{16,... | collective-permute-start | bytes 933896 | tf_op jit(solution)/shard_map/ppermute | solution.py:406
  33.9 0.0 collective-permute-done.14.refs_0_
  33.9 0.1 collective-permute-start.8
  34.0 0.0 collective-permute-done.15.refs_1_
  34.0 0.0 collective-permute-done.16.refs_2_
  34.0 0.8 shard_map.53
  34.7 0.0 copy-done.3
  34.8 0.0 copy-start.4
  34.8 0.5 collective-permute-start.17
  35.3 6.9 %collective-permute-start.18 = (bf16[18,64,128]{2,1,0:T(8,128)(2,1)S(1)}, bf16[18,64,128]{2,1,0:T(8,128)(2,1)S(1)}, u32[]{:S(2)}, u32[]{:S(2)}) collective-permute-start(bf16[18,64,128]{2,1,0:T(8,128)(2,1)S(1)} %get-tuple-element.65), channel_id=1, source_target_pairs={{8,17},{9,18},{10,19},{11,20},{12,21},{13,22},{14,23},{15,16},{16,... | collective-permute-start | bytes 884744 | tf_op jit(solution)/shard_map/ppermute | solution.py:406
  42.2 0.0 collective-permute-done.6.refs_0_
  42.2 0.1 collective-permute-start.19
  42.2 0.0 collective-permute-done.7.refs_1_
  42.2 1.1 %collective-permute-done.8.refs_2_ = bf16[32,64,128]{2,1,0:T(8,128)(2,1)S(1)} collective-permute-done((bf16[32,64,128]{2,1,0:T(8,128)(2,1)S(1)}, bf16[32,64,128]{2,1,0:T(8,128)(2,1)S(1)}, u32[]{:S(2)}, u32[]{:S(2)}) %collective-permute-start.8) | collective-permute-done | bytes 524320 | tf_op jit(solution)/shard_map/ppermute | solution.py:406
  43.4 0.6 shard_map.50
  43.9 0.0 copy-done.4
  44.0 0.0 copy-start.5
  44.0 10.1 %collective-permute-start.9 = (bf16[19,64,128]{2,1,0:T(8,128)(2,1)S(1)}, bf16[19,64,128]{2,1,0:T(8,128)(2,1)S(1)}, u32[]{:S(2)}, u32[]{:S(2)}) collective-permute-start(bf16[19,64,128]{2,1,0:T(8,128)(2,1)S(1)} %get-tuple-element.52), channel_id=1, source_target_pairs={{16,31},{17,24},{18,25},{19,26},{20,27},{21,28},{22,29},{23,30},{2... | collective-permute-start | bytes 933896 | tf_op jit(solution)/shard_map/ppermute | solution.py:406
  54.0 0.1 collective-permute-start.10
  54.1 0.0 collective-permute-done.17.refs_0_
  54.1 1.2 %collective-permute-start.11 = (bf16[32,64,128]{2,1,0:T(8,128)(2,1)S(1)}, bf16[32,64,128]{2,1,0:T(8,128)(2,1)S(1)}, u32[]{:S(2)}, u32[]{:S(2)}) collective-permute-start(bf16[32,64,128]{2,1,0:T(8,128)(2,1)S(1)} %get-tuple-element.54.refs_6_), channel_id=1, source_target_pairs={{16,24},{17,25},{18,26},{19,27},{20,28},{21,29},{22,30},{23,31},{2... | collective-permute-start | bytes 1572872 | tf_op jit(solution)/shard_map/ppermute | solution.py:406
  55.3 0.0 collective-permute-done.18.refs_1_
  55.3 0.0 collective-permute-done.19.refs_2_
  55.3 0.6 shard_map.54
  55.9 6.9 %collective-permute-start.20 = (bf16[18,64,128]{2,1,0:T(8,128)(2,1)S(1)}, bf16[18,64,128]{2,1,0:T(8,128)(2,1)S(1)}, u32[]{:S(2)}, u32[]{:S(2)}) collective-permute-start(bf16[18,64,128]{2,1,0:T(8,128)(2,1)S(1)} %get-tuple-element.67), channel_id=1, source_target_pairs={{16,31},{17,24},{18,25},{19,26},{20,27},{21,28},{22,29},{23,30},{2... | collective-permute-start | bytes 884744 | tf_op jit(solution)/shard_map/ppermute | solution.py:406
  62.8 0.1 collective-permute-start.21
  62.9 0.0 collective-permute-done.9.refs_0_
  62.9 1.2 %collective-permute-start.22 = (bf16[32,64,128]{2,1,0:T(8,128)(2,1)S(1)}, bf16[32,64,128]{2,1,0:T(8,128)(2,1)S(1)}, u32[]{:S(2)}, u32[]{:S(2)}) collective-permute-start(bf16[32,64,128]{2,1,0:T(8,128)(2,1)S(1)} %get-tuple-element.69.refs_6_), channel_id=1, source_target_pairs={{16,24},{17,25},{18,26},{19,27},{20,28},{21,29},{22,30},{23,31},{2... | collective-permute-start | bytes 1572872 | tf_op jit(solution)/shard_map/ppermute | solution.py:406
  64.1 0.0 collective-permute-done.10.refs_1_
  64.1 0.0 collective-permute-done.11.refs_2_
  64.1 4.7 %shard_map.51 = (bf16[128,32,128]{2,1,0:T(8,128)(2,1)}, f32[68,128]{1,0:T(8,128)S(1)}) custom-call(s32[3]{0:T(128)S(1)} %pad_add_fusion._.flags, s32[4,16]{1,0:T(4,128)S(1)} %get-tuple-element.40.offsets, f32[32,128]{1,0:T(8,128)S(1)} %bitcast.13, f32[32,128,128]{2,1,0:T(8,128)S(1)} %get-tuple-element.41.forcing, ...), custom_call_target="tpu_custom_call" | custom-call | flops 10737418240 | bytes 8388608 | tf_op jit(solution)/shard_map/pallas_call | solution.py:364
  68.8 0.0 collective-permute-done.20.refs_0_
  68.8 2.8 %collective-permute-done.21.refs_1_ = bf16[18,64,128]{2,1,0:T(8,128)(2,1)S(1)} collective-permute-done((bf16[18,64,128]{2,1,0:T(8,128)(2,1)S(1)}, bf16[18,64,128]{2,1,0:T(8,128)(2,1)S(1)}, u32[]{:S(2)}, u32[]{:S(2)}) %collective-permute-start.21) | collective-permute-done | bytes 294944 | tf_op jit(solution)/shard_map/ppermute | solution.py:406
  71.7 0.0 collective-permute-done.22.refs_2_
  71.7 5.0 %shard_map.55 = bf16[128,32,128]{2,1,0:T(8,128)(2,1)} custom-call(s32[3]{0:T(128)S(1)} %pad_add_fusion._.flags, s32[4,16]{1,0:T(4,128)S(1)} %get-tuple-element.40.offsets, f32[68,128]{1,0:T(8,128)S(1)} %get-tuple-element.55.kappa, f32[32,128,128]{2,1,0:T(8,128)S(1)} %get-tuple-element.41.forcing, ...), custom_call_target="tpu_custom_call", output_to_operand_aliasing={{}: (11, {})} | custom-call | flops 10737418240 | bytes 8388608 | tf_op jit(solution)/shard_map/pallas_call | solution.py:364
  (7 shorter events, 0.0 us)
Async XLA Ops:
  2.1 12.5 %collective-permute-start.2 = (bf16[33,128,128]{2,1,0:T(8,128)(2,1)S(1)}, bf16[33,128,128]{2,1,0:T(8,128)(2,1)S(1)}, u32[]{:S(2)}, u32[]{:S(2)}) collective-permute-start(bf16[33,128,128]{2,1,0:T(8,128)(2,1)S(1)} %get-tuple-element.44), channel_id=1, source_target_pairs={{0,8},{8,0},{16,24},{24,16},{1,9},{9,1},{17,25},{25,17},{2,10},{10... | collective-permute-start | bytes 3244040 | tf_op jit(solution)/shard_map/ppermute | solution.py:416
  2.9 11.7 %collective-permute-start = (bf16[19,64,128]{2,1,0:T(8,128)(2,1)S(1)}, bf16[19,64,128]{2,1,0:T(8,128)(2,1)S(1)}, u32[]{:S(2)}, u32[]{:S(2)}) collective-permute-start(bf16[19,64,128]{2,1,0:T(8,128)(2,1)S(1)} %get-tuple-element.42), channel_id=1, source_target_pairs={{0,1},{1,2},{2,3},{3,4},{4,5},{5,6},{6,7},{7,0},{16,8},{17,9},{18,... | collective-permute-start | bytes 933896 | tf_op jit(solution)/shard_map/ppermute | solution.py:406
  2.9 11.7 %collective-permute-start.1 = (bf16[19,64,128]{2,1,0:T(8,128)(2,1)S(1)}, bf16[19,64,128]{2,1,0:T(8,128)(2,1)S(1)}, u32[]{:S(2)}, u32[]{:S(2)}) collective-permute-start(bf16[19,64,128]{2,1,0:T(8,128)(2,1)S(1)} %get-tuple-element.43), channel_id=1, source_target_pairs={{0,7},{1,0},{2,1},{3,2},{4,3},{5,4},{6,5},{7,6},{16,8},{17,9},{18,... | collective-permute-start | bytes 933896 | tf_op jit(solution)/shard_map/ppermute | solution.py:406
  3.0 11.6 %copy-start = (f32[1,32,128]{2,1,0:T(8,128)S(1)}, f32[1,32,128]{2,1,0:T(8,128)}, u32[]{:S(2)}) copy-start(f32[1,32,128]{2,1,0:T(8,128)} %param.5) | copy-start | bytes 49156
  12.7 5.8 %collective-permute-start.12 = (bf16[19,64,128]{2,1,0:T(8,128)(2,1)S(1)}, bf16[19,64,128]{2,1,0:T(8,128)(2,1)S(1)}, u32[]{:S(2)}, u32[]{:S(2)}) collective-permute-start(bf16[19,64,128]{2,1,0:T(8,128)(2,1)S(1)} %get-tuple-element.59), channel_id=1, source_target_pairs={{0,7},{1,0},{2,1},{3,2},{4,3},{5,4},{6,5},{7,6},{16,8},{17,9},{18,... | collective-permute-start | bytes 933896 | tf_op jit(solution)/shard_map/ppermute | solution.py:406
  14.5 7.4 %collective-permute-start.13 = (bf16[19,64,128]{2,1,0:T(8,128)(2,1)S(1)}, bf16[19,64,128]{2,1,0:T(8,128)(2,1)S(1)}, u32[]{:S(2)}, u32[]{:S(2)}) collective-permute-start(bf16[19,64,128]{2,1,0:T(8,128)(2,1)S(1)} %get-tuple-element.60), channel_id=1, source_target_pairs={{0,1},{1,2},{2,3},{3,4},{4,5},{5,6},{6,7},{7,0},{16,8},{17,9},{18,... | collective-permute-start | bytes 933896 | tf_op jit(solution)/shard_map/ppermute | solution.py:406
  15.2 7.3 %copy-start.1 = (bf16[32,64,128]{2,1,0:T(8,128)(2,1)}, bf16[32,64,128]{2,1,0:T(8,128)(2,1)S(1)}, u32[]{:S(2)}) copy-start(bf16[32,64,128]{2,1,0:T(8,128)(2,1)S(1)} %get-tuple-element.48.refs_4_) | copy-start | bytes 1572868
  15.2 7.9 %collective-permute-start.3 = (bf16[19,64,128]{2,1,0:T(8,128)(2,1)S(1)}, bf16[19,64,128]{2,1,0:T(8,128)(2,1)S(1)}, u32[]{:S(2)}, u32[]{:S(2)}) collective-permute-start(bf16[19,64,128]{2,1,0:T(8,128)(2,1)S(1)} %get-tuple-element.46), channel_id=1, source_target_pairs={{0,15},{1,8},{2,9},{3,10},{4,11},{5,12},{6,13},{7,14},{8,0},{9,1},... | collective-permute-start | bytes 933896 | tf_op jit(solution)/shard_map/ppermute | solution.py:406
  15.3 8.2 %collective-permute-start.4 = (bf16[19,64,128]{2,1,0:T(8,128)(2,1)S(1)}, bf16[19,64,128]{2,1,0:T(8,128)(2,1)S(1)}, u32[]{:S(2)}, u32[]{:S(2)}) collective-permute-start(bf16[19,64,128]{2,1,0:T(8,128)(2,1)S(1)} %get-tuple-element.47), channel_id=1, source_target_pairs={{0,9},{1,10},{2,11},{3,12},{4,13},{5,14},{6,15},{7,8},{8,0},{9,1},... | collective-permute-start | bytes 933896 | tf_op jit(solution)/shard_map/ppermute | solution.py:406
  15.8 7.7 %collective-permute-start.5 = (bf16[32,64,128]{2,1,0:T(8,128)(2,1)S(1)}, bf16[32,64,128]{2,1,0:T(8,128)(2,1)S(1)}, u32[]{:S(2)}, u32[]{:S(2)}) collective-permute-start(bf16[32,64,128]{2,1,0:T(8,128)(2,1)S(1)} %get-tuple-element.48.refs_4_), channel_id=1, source_target_pairs={{0,8},{1,9},{2,10},{3,11},{4,12},{5,13},{6,14},{7,15},{8,0},{9,1},... | collective-permute-start | bytes 1572872 | tf_op jit(solution)/shard_map/ppermute | solution.py:406
  22.5 1.6 %copy-start.2 = (bf16[32,64,128]{2,1,0:T(8,128)(2,1)}, bf16[32,64,128]{2,1,0:T(8,128)(2,1)S(1)}, u32[]{:S(2)}) copy-start(bf16[32,64,128]{2,1,0:T(8,128)(2,1)S(1)} %get-tuple-element.63.refs_4_) | copy-start | bytes 1572868
  22.5 11.4 %collective-permute-start.14 = (bf16[18,64,128]{2,1,0:T(8,128)(2,1)S(1)}, bf16[18,64,128]{2,1,0:T(8,128)(2,1)S(1)}, u32[]{:S(2)}, u32[]{:S(2)}) collective-permute-start(bf16[18,64,128]{2,1,0:T(8,128)(2,1)S(1)} %get-tuple-element.61), channel_id=1, source_target_pairs={{0,15},{1,8},{2,9},{3,10},{4,11},{5,12},{6,13},{7,14},{8,0},{9,1},... | collective-permute-start | bytes 884744 | tf_op jit(solution)/shard_map/ppermute | solution.py:406
  23.0 11.0 %collective-permute-start.15 = (bf16[18,64,128]{2,1,0:T(8,128)(2,1)S(1)}, bf16[18,64,128]{2,1,0:T(8,128)(2,1)S(1)}, u32[]{:S(2)}, u32[]{:S(2)}) collective-permute-start(bf16[18,64,128]{2,1,0:T(8,128)(2,1)S(1)} %get-tuple-element.62), channel_id=1, source_target_pairs={{0,9},{1,10},{2,11},{3,12},{4,13},{5,14},{6,15},{7,8},{8,0},{9,1},... | collective-permute-start | bytes 884744 | tf_op jit(solution)/shard_map/ppermute | solution.py:406
  23.0 10.9 %collective-permute-start.16 = (bf16[32,64,128]{2,1,0:T(8,128)(2,1)S(1)}, bf16[32,64,128]{2,1,0:T(8,128)(2,1)S(1)}, u32[]{:S(2)}, u32[]{:S(2)}) collective-permute-start(bf16[32,64,128]{2,1,0:T(8,128)(2,1)S(1)} %get-tuple-element.63.refs_4_), channel_id=1, source_target_pairs={{0,8},{1,9},{2,10},{3,11},{4,12},{5,13},{6,14},{7,15},{8,0},{9,1},... | collective-permute-start | bytes 1572872 | tf_op jit(solution)/shard_map/ppermute | solution.py:406
  24.1 10.7 %copy-start.3 = (bf16[32,64,128]{2,1,0:T(8,128)(2,1)}, bf16[32,64,128]{2,1,0:T(8,128)(2,1)S(1)}, u32[]{:S(2)}) copy-start(bf16[32,64,128]{2,1,0:T(8,128)(2,1)S(1)} %get-tuple-element.51.refs_5_) | copy-start | bytes 1572868
  24.1 18.1 %collective-permute-start.6 = (bf16[19,64,128]{2,1,0:T(8,128)(2,1)S(1)}, bf16[19,64,128]{2,1,0:T(8,128)(2,1)S(1)}, u32[]{:S(2)}, u32[]{:S(2)}) collective-permute-start(bf16[19,64,128]{2,1,0:T(8,128)(2,1)S(1)} %get-tuple-element.49), channel_id=1, source_target_pairs={{8,23},{9,16},{10,17},{11,18},{12,19},{13,20},{14,21},{15,22},{16,... | collective-permute-start | bytes 933896 | tf_op jit(solution)/shard_map/ppermute | solution.py:406
  30.5 11.7 %collective-permute-start.7 = (bf16[19,64,128]{2,1,0:T(8,128)(2,1)S(1)}, bf16[19,64,128]{2,1,0:T(8,128)(2,1)S(1)}, u32[]{:S(2)}, u32[]{:S(2)}) collective-permute-start(bf16[19,64,128]{2,1,0:T(8,128)(2,1)S(1)} %get-tuple-element.50), channel_id=1, source_target_pairs={{8,17},{9,18},{10,19},{11,20},{12,21},{13,22},{14,23},{15,16},{16,... | collective-permute-start | bytes 933896 | tf_op jit(solution)/shard_map/ppermute | solution.py:406
  33.9 9.5 %collective-permute-start.8 = (bf16[32,64,128]{2,1,0:T(8,128)(2,1)S(1)}, bf16[32,64,128]{2,1,0:T(8,128)(2,1)S(1)}, u32[]{:S(2)}, u32[]{:S(2)}) collective-permute-start(bf16[32,64,128]{2,1,0:T(8,128)(2,1)S(1)} %get-tuple-element.51.refs_5_), channel_id=1, source_target_pairs={{8,16},{9,17},{10,18},{11,19},{12,20},{13,21},{14,22},{15,23},{16,... | collective-permute-start | bytes 1572872 | tf_op jit(solution)/shard_map/ppermute | solution.py:406
  34.8 9.2 %copy-start.4 = (bf16[32,64,128]{2,1,0:T(8,128)(2,1)}, bf16[32,64,128]{2,1,0:T(8,128)(2,1)S(1)}, u32[]{:S(2)}) copy-start(bf16[32,64,128]{2,1,0:T(8,128)(2,1)S(1)} %get-tuple-element.66.refs_5_) | copy-start | bytes 1572868
  34.8 19.4 %collective-permute-start.17 = (bf16[18,64,128]{2,1,0:T(8,128)(2,1)S(1)}, bf16[18,64,128]{2,1,0:T(8,128)(2,1)S(1)}, u32[]{:S(2)}, u32[]{:S(2)}) collective-permute-start(bf16[18,64,128]{2,1,0:T(8,128)(2,1)S(1)} %get-tuple-element.64), channel_id=1, source_target_pairs={{8,23},{9,16},{10,17},{11,18},{12,19},{13,20},{14,21},{15,22},{16,... | collective-permute-start | bytes 884744 | tf_op jit(solution)/shard_map/ppermute | solution.py:406
  35.3 20.0 %collective-permute-start.18 = (bf16[18,64,128]{2,1,0:T(8,128)(2,1)S(1)}, bf16[18,64,128]{2,1,0:T(8,128)(2,1)S(1)}, u32[]{:S(2)}, u32[]{:S(2)}) collective-permute-start(bf16[18,64,128]{2,1,0:T(8,128)(2,1)S(1)} %get-tuple-element.65), channel_id=1, source_target_pairs={{8,17},{9,18},{10,19},{11,20},{12,21},{13,22},{14,23},{15,16},{16,... | collective-permute-start | bytes 884744 | tf_op jit(solution)/shard_map/ppermute | solution.py:406
  42.2 13.1 %collective-permute-start.19 = (bf16[32,64,128]{2,1,0:T(8,128)(2,1)S(1)}, bf16[32,64,128]{2,1,0:T(8,128)(2,1)S(1)}, u32[]{:S(2)}, u32[]{:S(2)}) collective-permute-start(bf16[32,64,128]{2,1,0:T(8,128)(2,1)S(1)} %get-tuple-element.66.refs_5_), channel_id=1, source_target_pairs={{8,16},{9,17},{10,18},{11,19},{12,20},{13,21},{14,22},{15,23},{16,... | collective-permute-start | bytes 1572872 | tf_op jit(solution)/shard_map/ppermute | solution.py:406
  44.0 11.9 %copy-start.5 = (bf16[32,64,128]{2,1,0:T(8,128)(2,1)}, bf16[32,64,128]{2,1,0:T(8,128)(2,1)S(1)}, u32[]{:S(2)}) copy-start(bf16[32,64,128]{2,1,0:T(8,128)(2,1)S(1)} %get-tuple-element.54.refs_6_) | copy-start | bytes 1572868
  44.0 18.9 %collective-permute-start.9 = (bf16[19,64,128]{2,1,0:T(8,128)(2,1)S(1)}, bf16[19,64,128]{2,1,0:T(8,128)(2,1)S(1)}, u32[]{:S(2)}, u32[]{:S(2)}) collective-permute-start(bf16[19,64,128]{2,1,0:T(8,128)(2,1)S(1)} %get-tuple-element.52), channel_id=1, source_target_pairs={{16,31},{17,24},{18,25},{19,26},{20,27},{21,28},{22,29},{23,30},{2... | collective-permute-start | bytes 933896 | tf_op jit(solution)/shard_map/ppermute | solution.py:406
  54.0 10.0 %collective-permute-start.10 = (bf16[19,64,128]{2,1,0:T(8,128)(2,1)S(1)}, bf16[19,64,128]{2,1,0:T(8,128)(2,1)S(1)}, u32[]{:S(2)}, u32[]{:S(2)}) collective-permute-start(bf16[19,64,128]{2,1,0:T(8,128)(2,1)S(1)} %get-tuple-element.53), channel_id=1, source_target_pairs={{16,25},{17,26},{18,27},{19,28},{20,29},{21,30},{22,31},{23,24},{2... | collective-permute-start | bytes 933896 | tf_op jit(solution)/shard_map/ppermute | solution.py:406
  54.1 10.0 %collective-permute-start.11 = (bf16[32,64,128]{2,1,0:T(8,128)(2,1)S(1)}, bf16[32,64,128]{2,1,0:T(8,128)(2,1)S(1)}, u32[]{:S(2)}, u32[]{:S(2)}) collective-permute-start(bf16[32,64,128]{2,1,0:T(8,128)(2,1)S(1)} %get-tuple-element.54.refs_6_), channel_id=1, source_target_pairs={{16,24},{17,25},{18,26},{19,27},{20,28},{21,29},{22,30},{23,31},{2... | collective-permute-start | bytes 1572872 | tf_op jit(solution)/shard_map/ppermute | solution.py:406
  55.9 12.9 %copy-start.6 = (bf16[32,64,128]{2,1,0:T(8,128)(2,1)}, bf16[32,64,128]{2,1,0:T(8,128)(2,1)S(1)}, u32[]{:S(2)}) copy-start(bf16[32,64,128]{2,1,0:T(8,128)(2,1)S(1)} %get-tuple-element.69.refs_6_) | copy-start | bytes 1572868
  55.9 12.9 %collective-permute-start.20 = (bf16[18,64,128]{2,1,0:T(8,128)(2,1)S(1)}, bf16[18,64,128]{2,1,0:T(8,128)(2,1)S(1)}, u32[]{:S(2)}, u32[]{:S(2)}) collective-permute-start(bf16[18,64,128]{2,1,0:T(8,128)(2,1)S(1)} %get-tuple-element.67), channel_id=1, source_target_pairs={{16,31},{17,24},{18,25},{19,26},{20,27},{21,28},{22,29},{23,30},{2... | collective-permute-start | bytes 884744 | tf_op jit(solution)/shard_map/ppermute | solution.py:406
  62.8 8.8 %collective-permute-start.21 = (bf16[18,64,128]{2,1,0:T(8,128)(2,1)S(1)}, bf16[18,64,128]{2,1,0:T(8,128)(2,1)S(1)}, u32[]{:S(2)}, u32[]{:S(2)}) collective-permute-start(bf16[18,64,128]{2,1,0:T(8,128)(2,1)S(1)} %get-tuple-element.68), channel_id=1, source_target_pairs={{16,25},{17,26},{18,27},{19,28},{20,29},{21,30},{22,31},{23,24},{2... | collective-permute-start | bytes 884744 | tf_op jit(solution)/shard_map/ppermute | solution.py:406
  62.9 8.8 %collective-permute-start.22 = (bf16[32,64,128]{2,1,0:T(8,128)(2,1)S(1)}, bf16[32,64,128]{2,1,0:T(8,128)(2,1)S(1)}, u32[]{:S(2)}, u32[]{:S(2)}) collective-permute-start(bf16[32,64,128]{2,1,0:T(8,128)(2,1)S(1)} %get-tuple-element.69.refs_6_), channel_id=1, source_target_pairs={{16,24},{17,25},{18,26},{19,27},{20,28},{21,29},{22,30},{23,31},{2... | collective-permute-start | bytes 1572872 | tf_op jit(solution)/shard_map/ppermute | solution.py:406

commit v6 on v5

--- a/solution.py
+++ b/solution.py
@@ -11,7 +11,7 @@
 SHARES = (1, 1)
 EDGE = 2
 LIMIT = 24 << 20
-ORDERS = (((-2, -1), (-1, -2)), ((-1, -2, 0), (-1, -2, 0)))
+ORDERS = (((0, 1), (0, 1)), ((-2, -1, 0), (-1, -2, 0)))
 WEIGHT = 20
 HBM = pl.BlockSpec(memory_space=pltpu.HBM)
 VMEM = pl.BlockSpec(memory_space=pltpu.VMEM)
@@ -71,25 +71,37 @@
     fetch.start()
     start_all(loads)
     fetch.wait()
-    parts = split(k_v[...])
-    narrow[rows] = joined(parts, pack)
-    for e, start in enumerate((0, rows - halo)):
-        row = joined([part[start:start + halo] for part in parts], pack)
-        tail = (edges[e].shape[0] - halo, *edges[e].shape[1:])
-        edges[e][halo:] = row[:tail[0] * tail[1]].reshape(tail)
-    for i, load in enumerate(loads):
-        load.wait()
-        turned = jnp.swapaxes(f_v[:, i * step:(i + 1) * step, :], 0, 1)
-        by_row[i * step:(i + 1) * step] = turned
-        for r in range(step):
-            y = i * step + r
-            value = turned[r].astype(jnp.bfloat16)
-            narrow[y] = value
-            for edge_first, edge_last, start, stop in zip(edges[0::2], edges[1::2], marks[:-1], marks[1:]):
-                if y < halo:
-                    edge_first[y] = value[start:stop]
-                if y >= rows - halo:
-                    edge_last[y - (rows - halo)] = value[start:stop]
+    odd = lax.rem(lax.axis_index("tile"), 2) == 1
+    swapped = odd & (lax.axis_index("comp") == 0)
+
+    def write(edges):
+        parts = split(k_v[...])
+        narrow[rows] = joined(parts, pack)
+        for e, start in enumerate((0, rows - halo)):
+            row = joined([part[start:start + halo] for part in parts], pack)
+            tail = (edges[e].shape[0] - halo, *edges[e].shape[1:])
+            edges[e][halo:] = row[:tail[0] * tail[1]].reshape(tail)
+        for i, load in enumerate(loads):
+            load.wait()
+            turned = jnp.swapaxes(f_v[:, i * step:(i + 1) * step, :], 0, 1)
+            by_row[i * step:(i + 1) * step] = turned
+            for r in range(step):
+                y = i * step + r
+                value = turned[r].astype(jnp.bfloat16)
+                narrow[y] = value
+                for edge_first, edge_last, start, stop in zip(edges[0::2], edges[1::2], marks[:-1], marks[1:]):
+                    if y < halo:
+                        edge_first[y] = value[start:stop]
+                    if y >= rows - halo:
+                        edge_last[y - (rows - halo)] = value[start:stop]
+
+    @pl.when(swapped)
+    def _():
+        write([edge for pair in zip(edges[1::2], edges[0::2]) for edge in pair])
+
+    @pl.when(jnp.logical_not(swapped))
+    def _():
+        write(edges)
 
 
 def prepare(flags, fields, kappa, halo, marks):
@@ -172,8 +184,7 @@
 
 def section_kernel(order, number, bounds, halo, n_saved, has_next, flags, offsets, kappa, forcing, *refs):
     refs = list(refs)
-    arrived = dict(zip(order, (refs.pop(0) for _ in order)))
-    upper, lower, incoming = arrived[-2], arrived[-1], arrived.get(0)
+    arrived = [refs.pop(0) for _ in order]
     start_chunk = bounds[0] == 0
     ahead = [refs.pop(0) for _ in range(2 if number else 1)] if has_next else []
     weights = refs.pop(0)
@@ -210,8 +221,7 @@
             turned[:, i * part:(i + 1) * part, :] = jnp.swapaxes(own_v[i * part:(i + 1) * part], 0, 1)
             stores[i].start()
 
-    @pl.when(flags[0] == number)
-    def _():
+    def active(upper, lower, incoming=None):
         mine = slice(*bounds)
         beside = beside_matrix(cells)
         top = jnp.where(flags[1] == 0, 0.0, 1.0)
@@ -303,6 +313,17 @@
                         down_s[row - (rows - halo)] = entry_next.astype(jnp.bfloat16)
                 elif (row + 1) % part == 0:
                     store(row // part)
+
+    if number:
+        @pl.when(flags[0] == number)
+        def _():
+            by_name = dict(zip(order, arrived))
+            active(by_name[-2], by_name[-1], by_name[0])
+    else:
+        for odd in range(2):
+            @pl.when((flags[0] == number) & (lax.rem(flags[1], 2) == odd))
+            def _(odd=odd):
+                active(arrived[1 - odd], arrived[odd])
 
     if not has_next:
         @pl.when(flags[0] != number)
@@ -393,9 +414,7 @@
     def send(value, source, target, shift):
         pairs = [(place(source, t), place(target, t + shift)) for t in range(n_tile)]
         others = [s for s in range(n_section) if s not in (source, target)]
-        if source == target:
-            rest = list(zip(others[1:] + others[:1], others))
-        elif n_section % 2 == 0 and source % 2:
+        if n_section % 2 == 0 and source % 2:
             rest = [(target, target ^ 1), (target ^ 1, source ^ 1), (source ^ 1, source)]
             rest += [(s, s ^ 1) for s in others if s not in (target ^ 1, source ^ 1)]
         elif source ^ 1 == target and n_section % 2 == 0:
@@ -405,14 +424,18 @@
         pairs += [(place(s, t), place(to, t)) for s, to in rest for t in range(n_tile)]
         return lax.ppermute(value, AXES, pairs)
 
+    def exchange(value, first):
+        pairs = [(place(0, t), place(0, t + 1 if t % 2 == first else t - 1)) for t in range(n_tile)]
+        pairs += [(place(s, t), place((s - 2) % (n_section - 1) + 1, t)) for s in range(1, n_section) for t in range(n_tile)]
+        return lax.ppermute(value, AXES, pairs)
+
     fields = forcing.reshape(-1, rows, cells)
     marks = [fields.shape[0] * sum(SHARES[:c]) // sum(SHARES) for c in range(len(SHARES) + 1)]
     by_row, narrow, *edges = prepare(flags, fields, kappa[0], halo, marks)
     weights, offsets, *edges[2:] = load(flags, col_blocks[0].T, weights, edges[2:])
     arrivals = []
     for c in range(len(SHARES)):
-        sends = [(edges[2 * c + 1], 1), (edges[2 * c], -1)][::1 - c % 2 * 2]
-        arrivals.append([send(edge, 0, 0, shift) for edge, shift in sends][::1 - c % 2 * 2])
+        arrivals.append([exchange(edges[2 * c + 1], 0), exchange(edges[2 * c], 1)])
     narrow = lax.ppermute(narrow, "comp", [(s, s ^ 1) for s in range(n_section) if s ^ 1 < n_section])
     following = [[[narrow]] * len(SHARES)] + [[pair[::-1] for pair in arrivals]] * (n_section - 2) + [[[]] * len(SHARES)]
     owns = [[] for _ in SHARES]

time: 77 us -> 76.6 us (level)
  starting transfers between devices: 41.2 us -> 39.6 us
  waiting for transfers between devices: 10 us -> 11.1 us
    ppermute x0 -> x4, waiting for transfers between devices: none -> 6.03 us  [exchange(): return lax.ppermute(value, AXES, pairs)]
    ppermute x22 -> x18, waiting for transfers between devices: 10 us -> 5.11 us  [send(): return lax.ppermute(value, AXES, pairs)]
    ppermute x22 -> x18, starting transfers between devices: 40.5 us -> 36.9 us  [send(): return lax.ppermute(value, AXES, pairs)]
    ppermute x0 -> x4, starting transfers between devices: none -> 1.99 us  [exchange(): return lax.ppermute(value, AXES, pairs)]
  transfers between devices with their start and end apart: 23 -> 23, of which waited for: 4 -> 5; matrix products, arithmetic and copies ran while one was open for 0% -> 0% of each run, Pallas kernels for 24% -> 24%
where the time goes in v6:
time: 76.6 us; the launch traced here: 76.4 us
  starting transfers between devices  39.6 us (52%)
  Pallas kernels  25.1 us (33%)
  waiting for transfers between devices  11.1 us (14%)
    ppermute x18, starting transfers between devices, send(): return lax.ppermute(value, AXES, pairs)  36.9 us
    pallas_call x8, Pallas kernels, section(): pl.pallas_call(functools.partial(section_kernel, order, number, bounds, h...  13.4 us
    pallas_call x1, Pallas kernels, load(): pl.pallas_call(functools.partial(load_kernel, len(passed)), in_specs=[SME...  9.72 us
    ppermute x4, waiting for transfers between devices, exchange(): return lax.ppermute(value, AXES, pairs)  6.03 us
    ppermute x18, waiting for transfers between devices, send(): return lax.ppermute(value, AXES, pairs)  5.11 us
    pallas_call x1, Pallas kernels, prepare(): pl.pallas_call(functools.partial(prepare_kernel, halo, marks), in_specs=[...  2.03 us
    ppermute x4, starting transfers between devices, exchange(): return lax.ppermute(value, AXES, pairs)  1.99 us
  transfers between devices with their start and end apart: 23, of which 5 were waited for; matrix products, arithmetic and copies ran while one was open for 0% of the time, Pallas kernels for 24%

profile of v6, /device:TPU:3, one launch (start us, length us, event | category | flops | bytes accessed | tf_op | source)
XLA Modules:
  0.0 76.4 jit_solution(13111701562469550397)
XLA Ops:
  0.0 0.1 pad_add_fusion._.flags
  0.1 2.0 %shard_map.46 = (f32[32,128,128]{2,1,0:T(8,128)S(1)}, bf16[33,128,128]{2,1,0:T(8,128)(2,1)S(1)}, bf16[19,64,128]{2,1,0:T(8,128)(2,1)S(1)}, bf16[19,64,128]{2,1,0...) custom-call(s32[3]{0:T(128)S(1)} %pad_add_fusion._.flags, ...), custom_call_target="tpu_custom_call" | custom-call | bytes 6291456 | tf_op jit(solution)/shard_map/pallas_call | solution.py:113
  2.1 0.7 collective-permute-start.2
  2.9 0.1 collective-permute-start
  2.9 0.1 collective-permute-start.1
  3.0 9.7 %shard_map.47 = (bf16[16,4,256,256]{3,2,1,0:T(8,128)(2,1)S(1)}, s32[4,16]{1,0:T(4,128)S(1)}, bf16[19,64,128]{2,1,0:T(8,128)(2,1)S(1)}, bf16[19,64,128]{2,1,0:T(8,128)(2,1)S(1)}) custom-call(s32[3]{0:T(128)S(1)} %pad_add_fusion._.flags, s32[4,16]{1,0:T(4,128)} %bitcast.16, ...), custom_call_target="tpu_custom_call", output_to_operand_aliasing={{2}: (3, {}), {3}: (4, {})} | custom-call | bytes 16777216 | tf_op jit(solution)/shard_map/pallas_call | solution.py:159
  12.7 1.8 %collective-permute-start.12 = (bf16[19,64,128]{2,1,0:T(8,128)(2,1)S(1)}, bf16[19,64,128]{2,1,0:T(8,128)(2,1)S(1)}, u32[]{:S(2)}, u32[]{:S(2)}) collective-permute-start(bf16[19,64,128]{2,1,0:T(8,128)(2,1)S(1)} %get-tuple-element.59), channel_id=1, source_target_pairs={{0,1},{1,0},{2,3},{3,2},{4,5},{5,4},{6,7},{7,6},{8,24},{9,25},{10,... | collective-permute-start | bytes 933896 | tf_op jit(solution)/shard_map/ppermute | solution.py:430
  14.5 0.1 collective-permute-start.13
  14.6 0.0 collective-permute-done.refs_0_.refs_4_
  14.6 0.0 collective-permute-done.1.refs_1_.refs_3_
  14.6 0.0 collective-permute-done.2.refs_2_
  14.6 0.0 copy-done
  14.6 0.6 shard_map.48
  15.2 0.0 copy-start.1
  15.2 0.1 collective-permute-start.3
  15.3 0.4 collective-permute-start.4
  15.8 0.1 collective-permute-start.5
  15.8 2.7 %collective-permute-done.12.refs_0_.refs_4_ = bf16[19,64,128]{2,1,0:T(8,128)(2,1)S(1)} collective-permute-done((bf16[19,64,128]{2,1,0:T(8,128)(2,1)S(1)}, bf16[19,64,128]{2,1,0:T(8,128)(2,1)S(1)}, u32[]{:S(2)}, u32[]{:S(2)}) %collective-permute-start.12) | collective-permute-done | bytes 311328 | tf_op jit(solution)/shard_map/ppermute | solution.py:430
  18.5 3.3 %collective-permute-done.13.refs_1_.refs_3_ = bf16[19,64,128]{2,1,0:T(8,128)(2,1)S(1)} collective-permute-done((bf16[19,64,128]{2,1,0:T(8,128)(2,1)S(1)}, bf16[19,64,128]{2,1,0:T(8,128)(2,1)S(1)}, u32[]{:S(2)}, u32[]{:S(2)}) %collective-permute-start.13) | collective-permute-done | bytes 311328 | tf_op jit(solution)/shard_map/ppermute | solution.py:430
  21.9 0.8 %shard_map.52 = (bf16[32,64,128]{2,1,0:T(8,128)(2,1)S(1)}, bf16[18,64,128]{2,1,0:T(8,128)(2,1)S(1)}, bf16[18,64,128]{2,1,0:T(8,128)(2,1)S(1)}) custom-call(s32[3]{0:T(128)S(1)} %pad_add_fusion._.flags, s32[4,16]{1,0:T(4,128)S(1)} %get-tuple-element.40.offsets, f32[68,128]{1,0:T(8,128)S(1)} %get-tuple-element.58.kappa, ...), custom_call_target="tpu_custom_call" | custom-call | flops 10737418240 | bytes 8388608 | tf_op jit(solution)/shard_map/pallas_call | solution.py:385
  22.6 0.0 copy-done.1
  22.6 0.0 copy-start.2
  22.7 0.5 collective-permute-start.14
  23.2 0.1 collective-permute-start.15
  23.2 0.0 collective-permute-done.3.refs_0_
  23.2 0.4 collective-permute-start.16
  23.7 0.0 collective-permute-done.4.refs_1_
  23.7 0.0 collective-permute-done.5.refs_2_
  23.7 0.6 shard_map.49
  24.3 0.0 copy-done.2
  24.3 0.0 copy-start.3
  24.3 6.1 %collective-permute-start.6 = (bf16[19,64,128]{2,1,0:T(8,128)(2,1)S(1)}, bf16[19,64,128]{2,1,0:T(8,128)(2,1)S(1)}, u32[]{:S(2)}, u32[]{:S(2)}) collective-permute-start(bf16[19,64,128]{2,1,0:T(8,128)(2,1)S(1)} %get-tuple-element.49), channel_id=1, source_target_pairs={{8,17},{9,18},{10,19},{11,20},{12,21},{13,22},{14,23},{15,16},{16,... | collective-permute-start | bytes 933896 | tf_op jit(solution)/shard_map/ppermute | solution.py:425
  30.4 3.4 %collective-permute-start.7 = (bf16[19,64,128]{2,1,0:T(8,128)(2,1)S(1)}, bf16[19,64,128]{2,1,0:T(8,128)(2,1)S(1)}, u32[]{:S(2)}, u32[]{:S(2)}) collective-permute-start(bf16[19,64,128]{2,1,0:T(8,128)(2,1)S(1)} %get-tuple-element.50), channel_id=1, source_target_pairs={{8,23},{9,16},{10,17},{11,18},{12,19},{13,20},{14,21},{15,22},{16,... | collective-permute-start | bytes 933896 | tf_op jit(solution)/shard_map/ppermute | solution.py:425
  33.8 0.0 collective-permute-done.14.refs_0_
  33.8 0.1 collective-permute-start.8
  33.9 0.0 collective-permute-done.15.refs_1_
  33.9 0.0 collective-permute-done.16.refs_2_
  33.9 0.6 shard_map.53
  34.4 0.0 copy-done.3
  34.5 0.7 collective-permute-start.17
  35.2 6.4 %collective-permute-start.18 = (bf16[18,64,128]{2,1,0:T(8,128)(2,1)S(1)}, bf16[18,64,128]{2,1,0:T(8,128)(2,1)S(1)}, u32[]{:S(2)}, u32[]{:S(2)}) collective-permute-start(bf16[18,64,128]{2,1,0:T(8,128)(2,1)S(1)} %get-tuple-element.65), channel_id=1, source_target_pairs={{8,17},{9,18},{10,19},{11,20},{12,21},{13,22},{14,23},{15,16},{16,... | collective-permute-start | bytes 884744 | tf_op jit(solution)/shard_map/ppermute | solution.py:425
  41.6 0.0 collective-permute-done.6.refs_0_
  41.6 0.1 collective-permute-start.19
  41.7 0.0 collective-permute-done.7.refs_1_
  41.7 1.6 %collective-permute-done.8.refs_2_ = bf16[32,64,128]{2,1,0:T(8,128)(2,1)S(1)} collective-permute-done((bf16[32,64,128]{2,1,0:T(8,128)(2,1)S(1)}, bf16[32,64,128]{2,1,0:T(8,128)(2,1)S(1)}, u32[]{:S(2)}, u32[]{:S(2)}) %collective-permute-start.8) | collective-permute-done | bytes 524320 | tf_op jit(solution)/shard_map/ppermute | solution.py:425
  43.2 0.6 shard_map.50
  43.9 9.8 %collective-permute-start.9 = (bf16[19,64,128]{2,1,0:T(8,128)(2,1)S(1)}, bf16[19,64,128]{2,1,0:T(8,128)(2,1)S(1)}, u32[]{:S(2)}, u32[]{:S(2)}) collective-permute-start(bf16[19,64,128]{2,1,0:T(8,128)(2,1)S(1)} %get-tuple-element.52), channel_id=1, source_target_pairs={{16,25},{17,26},{18,27},{19,28},{20,29},{21,30},{22,31},{23,24},{2... | collective-permute-start | bytes 933896 | tf_op jit(solution)/shard_map/ppermute | solution.py:425
  53.6 0.1 collective-permute-start.10
  53.7 0.0 collective-permute-done.17.refs_0_
  53.7 2.9 %collective-permute-start.11 = (bf16[32,64,128]{2,1,0:T(8,128)(2,1)S(1)}, bf16[32,64,128]{2,1,0:T(8,128)(2,1)S(1)}, u32[]{:S(2)}, u32[]{:S(2)}) collective-permute-start(bf16[32,64,128]{2,1,0:T(8,128)(2,1)S(1)} %get-tuple-element.54.refs_6_), channel_id=1, source_target_pairs={{16,24},{17,25},{18,26},{19,27},{20,28},{21,29},{22,30},{23,31},{2... | collective-permute-start | bytes 1572872 | tf_op jit(solution)/shard_map/ppermute | solution.py:425
  56.6 0.0 collective-permute-done.18.refs_1_
  56.6 0.0 collective-permute-done.19.refs_2_
  56.6 0.8 %shard_map.54 = (bf16[32,64,128]{2,1,0:T(8,128)(2,1)S(1)}, bf16[18,64,128]{2,1,0:T(8,128)(2,1)S(1)}, bf16[18,64,128]{2,1,0:T(8,128)(2,1)S(1)}) custom-call(s32[3]{0:T(128)S(1)} %pad_add_fusion._.flags, s32[4,16]{1,0:T(4,128)S(1)} %get-tuple-element.40.offsets, f32[68,128]{1,0:T(8,128)S(1)} %get-tuple-element.56.kappa, ...), custom_call_target="tpu_custom_call" | custom-call | flops 10737418240 | bytes 8388608 | tf_op jit(solution)/shard_map/pallas_call | solution.py:385
  57.4 5.2 %collective-permute-start.20 = (bf16[18,64,128]{2,1,0:T(8,128)(2,1)S(1)}, bf16[18,64,128]{2,1,0:T(8,128)(2,1)S(1)}, u32[]{:S(2)}, u32[]{:S(2)}) collective-permute-start(bf16[18,64,128]{2,1,0:T(8,128)(2,1)S(1)} %get-tuple-element.67), channel_id=1, source_target_pairs={{16,31},{17,24},{18,25},{19,26},{20,27},{21,28},{22,29},{23,30},{2... | collective-permute-start | bytes 884744 | tf_op jit(solution)/shard_map/ppermute | solution.py:425
  62.6 0.1 collective-permute-start.21
  62.7 0.0 collective-permute-done.9.refs_0_
  62.7 0.5 collective-permute-start.22
  63.2 0.1 collective-permute-done.10.refs_1_
  63.3 0.0 collective-permute-done.11.refs_2_
  63.3 4.7 %shard_map.51 = (bf16[128,32,128]{2,1,0:T(8,128)(2,1)}, f32[68,128]{1,0:T(8,128)S(1)}) custom-call(s32[3]{0:T(128)S(1)} %pad_add_fusion._.flags, s32[4,16]{1,0:T(4,128)S(1)} %get-tuple-element.40.offsets, f32[32,128]{1,0:T(8,128)S(1)} %bitcast.13, f32[32,128,128]{2,1,0:T(8,128)S(1)} %get-tuple-element.41.forcing, ...), custom_call_target="tpu_custom_call" | custom-call | flops 10737418240 | bytes 8388608 | tf_op jit(solution)/shard_map/pallas_call | solution.py:385
  68.0 0.0 collective-permute-done.20.refs_0_
  68.1 3.4 %collective-permute-done.21.refs_1_ = bf16[18,64,128]{2,1,0:T(8,128)(2,1)S(1)} collective-permute-done((bf16[18,64,128]{2,1,0:T(8,128)(2,1)S(1)}, bf16[18,64,128]{2,1,0:T(8,128)(2,1)S(1)}, u32[]{:S(2)}, u32[]{:S(2)}) %collective-permute-start.21) | collective-permute-done | bytes 294944 | tf_op jit(solution)/shard_map/ppermute | solution.py:425
  71.5 0.0 collective-permute-done.22.refs_2_
  71.5 4.7 %shard_map.55 = bf16[128,32,128]{2,1,0:T(8,128)(2,1)} custom-call(s32[3]{0:T(128)S(1)} %pad_add_fusion._.flags, s32[4,16]{1,0:T(4,128)S(1)} %get-tuple-element.40.offsets, f32[68,128]{1,0:T(8,128)S(1)} %get-tuple-element.55.kappa, f32[32,128,128]{2,1,0:T(8,128)S(1)} %get-tuple-element.41.forcing, ...), custom_call_target="tpu_custom_call", output_to_operand_aliasing={{}: (11, {})} | custom-call | flops 10737418240 | bytes 8388608 | tf_op jit(solution)/shard_map/pallas_call | solution.py:385
  (7 shorter events, 0.0 us)
Async XLA Ops:
  2.1 12.5 %collective-permute-start.2 = (bf16[33,128,128]{2,1,0:T(8,128)(2,1)S(1)}, bf16[33,128,128]{2,1,0:T(8,128)(2,1)S(1)}, u32[]{:S(2)}, u32[]{:S(2)}) collective-permute-start(bf16[33,128,128]{2,1,0:T(8,128)(2,1)S(1)} %get-tuple-element.44), channel_id=1, source_target_pairs={{0,8},{8,0},{16,24},{24,16},{1,9},{9,1},{17,25},{25,17},{2,10},{10... | collective-permute-start | bytes 3244040 | tf_op jit(solution)/shard_map/ppermute | solution.py:439
  2.9 11.7 %collective-permute-start = (bf16[19,64,128]{2,1,0:T(8,128)(2,1)S(1)}, bf16[19,64,128]{2,1,0:T(8,128)(2,1)S(1)}, u32[]{:S(2)}, u32[]{:S(2)}) collective-permute-start(bf16[19,64,128]{2,1,0:T(8,128)(2,1)S(1)} %get-tuple-element.42), channel_id=1, source_target_pairs={{0,1},{1,0},{2,3},{3,2},{4,5},{5,4},{6,7},{7,6},{8,24},{9,25},{10,... | collective-permute-start | bytes 933896 | tf_op jit(solution)/shard_map/ppermute | solution.py:430
  2.9 11.6 %collective-permute-start.1 = (bf16[19,64,128]{2,1,0:T(8,128)(2,1)S(1)}, bf16[19,64,128]{2,1,0:T(8,128)(2,1)S(1)}, u32[]{:S(2)}, u32[]{:S(2)}) collective-permute-start(bf16[19,64,128]{2,1,0:T(8,128)(2,1)S(1)} %get-tuple-element.43), channel_id=1, source_target_pairs={{0,7},{1,2},{2,1},{3,4},{4,3},{5,6},{6,5},{7,0},{8,24},{9,25},{10,... | collective-permute-start | bytes 933896 | tf_op jit(solution)/shard_map/ppermute | solution.py:430
  3.0 11.6 %copy-start = (f32[1,32,128]{2,1,0:T(8,128)S(1)}, f32[1,32,128]{2,1,0:T(8,128)}, u32[]{:S(2)}) copy-start(f32[1,32,128]{2,1,0:T(8,128)} %param.5) | copy-start | bytes 49156
  12.7 5.8 %collective-permute-start.12 = (bf16[19,64,128]{2,1,0:T(8,128)(2,1)S(1)}, bf16[19,64,128]{2,1,0:T(8,128)(2,1)S(1)}, u32[]{:S(2)}, u32[]{:S(2)}) collective-permute-start(bf16[19,64,128]{2,1,0:T(8,128)(2,1)S(1)} %get-tuple-element.59), channel_id=1, source_target_pairs={{0,1},{1,0},{2,3},{3,2},{4,5},{5,4},{6,7},{7,6},{8,24},{9,25},{10,... | collective-permute-start | bytes 933896 | tf_op jit(solution)/shard_map/ppermute | solution.py:430
  14.5 7.4 %collective-permute-start.13 = (bf16[19,64,128]{2,1,0:T(8,128)(2,1)S(1)}, bf16[19,64,128]{2,1,0:T(8,128)(2,1)S(1)}, u32[]{:S(2)}, u32[]{:S(2)}) collective-permute-start(bf16[19,64,128]{2,1,0:T(8,128)(2,1)S(1)} %get-tuple-element.60), channel_id=1, source_target_pairs={{0,7},{1,2},{2,1},{3,4},{4,3},{5,6},{6,5},{7,0},{8,24},{9,25},{10,... | collective-permute-start | bytes 933896 | tf_op jit(solution)/shard_map/ppermute | solution.py:430
  15.2 7.4 %copy-start.1 = (bf16[32,64,128]{2,1,0:T(8,128)(2,1)}, bf16[32,64,128]{2,1,0:T(8,128)(2,1)S(1)}, u32[]{:S(2)}) copy-start(bf16[32,64,128]{2,1,0:T(8,128)(2,1)S(1)} %get-tuple-element.48.refs_4_) | copy-start | bytes 1572868
  15.2 8.0 %collective-permute-start.3 = (bf16[19,64,128]{2,1,0:T(8,128)(2,1)S(1)}, bf16[19,64,128]{2,1,0:T(8,128)(2,1)S(1)}, u32[]{:S(2)}, u32[]{:S(2)}) collective-permute-start(bf16[19,64,128]{2,1,0:T(8,128)(2,1)S(1)} %get-tuple-element.46), channel_id=1, source_target_pairs={{0,9},{1,10},{2,11},{3,12},{4,13},{5,14},{6,15},{7,8},{8,0},{9,1},... | collective-permute-start | bytes 933896 | tf_op jit(solution)/shard_map/ppermute | solution.py:425
  15.3 8.4 %collective-permute-start.4 = (bf16[19,64,128]{2,1,0:T(8,128)(2,1)S(1)}, bf16[19,64,128]{2,1,0:T(8,128)(2,1)S(1)}, u32[]{:S(2)}, u32[]{:S(2)}) collective-permute-start(bf16[19,64,128]{2,1,0:T(8,128)(2,1)S(1)} %get-tuple-element.47), channel_id=1, source_target_pairs={{0,15},{1,8},{2,9},{3,10},{4,11},{5,12},{6,13},{7,14},{8,0},{9,1},... | collective-permute-start | bytes 933896 | tf_op jit(solution)/shard_map/ppermute | solution.py:425
  15.8 7.9 %collective-permute-start.5 = (bf16[32,64,128]{2,1,0:T(8,128)(2,1)S(1)}, bf16[32,64,128]{2,1,0:T(8,128)(2,1)S(1)}, u32[]{:S(2)}, u32[]{:S(2)}) collective-permute-start(bf16[32,64,128]{2,1,0:T(8,128)(2,1)S(1)} %get-tuple-element.48.refs_4_), channel_id=1, source_target_pairs={{0,8},{1,9},{2,10},{3,11},{4,12},{5,13},{6,14},{7,15},{8,0},{9,1},... | collective-permute-start | bytes 1572872 | tf_op jit(solution)/shard_map/ppermute | solution.py:425
  22.6 1.6 %copy-start.2 = (bf16[32,64,128]{2,1,0:T(8,128)(2,1)}, bf16[32,64,128]{2,1,0:T(8,128)(2,1)S(1)}, u32[]{:S(2)}) copy-start(bf16[32,64,128]{2,1,0:T(8,128)(2,1)S(1)} %get-tuple-element.63.refs_4_) | copy-start | bytes 1572868
  22.7 11.1 %collective-permute-start.14 = (bf16[18,64,128]{2,1,0:T(8,128)(2,1)S(1)}, bf16[18,64,128]{2,1,0:T(8,128)(2,1)S(1)}, u32[]{:S(2)}, u32[]{:S(2)}) collective-permute-start(bf16[18,64,128]{2,1,0:T(8,128)(2,1)S(1)} %get-tuple-element.61), channel_id=1, source_target_pairs={{0,15},{1,8},{2,9},{3,10},{4,11},{5,12},{6,13},{7,14},{8,0},{9,1},... | collective-permute-start | bytes 884744 | tf_op jit(solution)/shard_map/ppermute | solution.py:425
  23.2 10.7 %collective-permute-start.15 = (bf16[18,64,128]{2,1,0:T(8,128)(2,1)S(1)}, bf16[18,64,128]{2,1,0:T(8,128)(2,1)S(1)}, u32[]{:S(2)}, u32[]{:S(2)}) collective-permute-start(bf16[18,64,128]{2,1,0:T(8,128)(2,1)S(1)} %get-tuple-element.62), channel_id=1, source_target_pairs={{0,9},{1,10},{2,11},{3,12},{4,13},{5,14},{6,15},{7,8},{8,0},{9,1},... | collective-permute-start | bytes 884744 | tf_op jit(solution)/shard_map/ppermute | solution.py:425
  23.2 10.6 %collective-permute-start.16 = (bf16[32,64,128]{2,1,0:T(8,128)(2,1)S(1)}, bf16[32,64,128]{2,1,0:T(8,128)(2,1)S(1)}, u32[]{:S(2)}, u32[]{:S(2)}) collective-permute-start(bf16[32,64,128]{2,1,0:T(8,128)(2,1)S(1)} %get-tuple-element.63.refs_4_), channel_id=1, source_target_pairs={{0,8},{1,9},{2,10},{3,11},{4,12},{5,13},{6,14},{7,15},{8,0},{9,1},... | collective-permute-start | bytes 1572872 | tf_op jit(solution)/shard_map/ppermute | solution.py:425
  24.3 10.2 %copy-start.3 = (bf16[32,64,128]{2,1,0:T(8,128)(2,1)}, bf16[32,64,128]{2,1,0:T(8,128)(2,1)S(1)}, u32[]{:S(2)}) copy-start(bf16[32,64,128]{2,1,0:T(8,128)(2,1)S(1)} %get-tuple-element.51.refs_5_) | copy-start | bytes 1572868
  24.3 17.3 %collective-permute-start.6 = (bf16[19,64,128]{2,1,0:T(8,128)(2,1)S(1)}, bf16[19,64,128]{2,1,0:T(8,128)(2,1)S(1)}, u32[]{:S(2)}, u32[]{:S(2)}) collective-permute-start(bf16[19,64,128]{2,1,0:T(8,128)(2,1)S(1)} %get-tuple-element.49), channel_id=1, source_target_pairs={{8,17},{9,18},{10,19},{11,20},{12,21},{13,22},{14,23},{15,16},{16,... | collective-permute-start | bytes 933896 | tf_op jit(solution)/shard_map/ppermute | solution.py:425
  30.4 11.3 %collective-permute-start.7 = (bf16[19,64,128]{2,1,0:T(8,128)(2,1)S(1)}, bf16[19,64,128]{2,1,0:T(8,128)(2,1)S(1)}, u32[]{:S(2)}, u32[]{:S(2)}) collective-permute-start(bf16[19,64,128]{2,1,0:T(8,128)(2,1)S(1)} %get-tuple-element.50), channel_id=1, source_target_pairs={{8,23},{9,16},{10,17},{11,18},{12,19},{13,20},{14,21},{15,22},{16,... | collective-permute-start | bytes 933896 | tf_op jit(solution)/shard_map/ppermute | solution.py:425
  33.8 9.5 %collective-permute-start.8 = (bf16[32,64,128]{2,1,0:T(8,128)(2,1)S(1)}, bf16[32,64,128]{2,1,0:T(8,128)(2,1)S(1)}, u32[]{:S(2)}, u32[]{:S(2)}) collective-permute-start(bf16[32,64,128]{2,1,0:T(8,128)(2,1)S(1)} %get-tuple-element.51.refs_5_), channel_id=1, source_target_pairs={{8,16},{9,17},{10,18},{11,19},{12,20},{13,21},{14,22},{15,23},{16,... | collective-permute-start | bytes 1572872 | tf_op jit(solution)/shard_map/ppermute | solution.py:425
  34.5 9.4 %copy-start.4 = (bf16[32,64,128]{2,1,0:T(8,128)(2,1)}, bf16[32,64,128]{2,1,0:T(8,128)(2,1)S(1)}, u32[]{:S(2)}) copy-start(bf16[32,64,128]{2,1,0:T(8,128)(2,1)S(1)} %get-tuple-element.66.refs_5_) | copy-start | bytes 1572868
  34.5 19.2 %collective-permute-start.17 = (bf16[18,64,128]{2,1,0:T(8,128)(2,1)S(1)}, bf16[18,64,128]{2,1,0:T(8,128)(2,1)S(1)}, u32[]{:S(2)}, u32[]{:S(2)}) collective-permute-start(bf16[18,64,128]{2,1,0:T(8,128)(2,1)S(1)} %get-tuple-element.64), channel_id=1, source_target_pairs={{8,23},{9,16},{10,17},{11,18},{12,19},{13,20},{14,21},{15,22},{16,... | collective-permute-start | bytes 884744 | tf_op jit(solution)/shard_map/ppermute | solution.py:425
  35.2 21.5 %collective-permute-start.18 = (bf16[18,64,128]{2,1,0:T(8,128)(2,1)S(1)}, bf16[18,64,128]{2,1,0:T(8,128)(2,1)S(1)}, u32[]{:S(2)}, u32[]{:S(2)}) collective-permute-start(bf16[18,64,128]{2,1,0:T(8,128)(2,1)S(1)} %get-tuple-element.65), channel_id=1, source_target_pairs={{8,17},{9,18},{10,19},{11,20},{12,21},{13,22},{14,23},{15,16},{16,... | collective-permute-start | bytes 884744 | tf_op jit(solution)/shard_map/ppermute | solution.py:425
  41.6 15.0 %collective-permute-start.19 = (bf16[32,64,128]{2,1,0:T(8,128)(2,1)S(1)}, bf16[32,64,128]{2,1,0:T(8,128)(2,1)S(1)}, u32[]{:S(2)}, u32[]{:S(2)}) collective-permute-start(bf16[32,64,128]{2,1,0:T(8,128)(2,1)S(1)} %get-tuple-element.66.refs_5_), channel_id=1, source_target_pairs={{8,16},{9,17},{10,18},{11,19},{12,20},{13,21},{14,22},{15,23},{16,... | collective-permute-start | bytes 1572872 | tf_op jit(solution)/shard_map/ppermute | solution.py:425
  43.8 13.6 %copy-start.5 = (bf16[32,64,128]{2,1,0:T(8,128)(2,1)}, bf16[32,64,128]{2,1,0:T(8,128)(2,1)S(1)}, u32[]{:S(2)}) copy-start(bf16[32,64,128]{2,1,0:T(8,128)(2,1)S(1)} %get-tuple-element.54.refs_6_) | copy-start | bytes 1572868
  43.9 18.8 %collective-permute-start.9 = (bf16[19,64,128]{2,1,0:T(8,128)(2,1)S(1)}, bf16[19,64,128]{2,1,0:T(8,128)(2,1)S(1)}, u32[]{:S(2)}, u32[]{:S(2)}) collective-permute-start(bf16[19,64,128]{2,1,0:T(8,128)(2,1)S(1)} %get-tuple-element.52), channel_id=1, source_target_pairs={{16,25},{17,26},{18,27},{19,28},{20,29},{21,30},{22,31},{23,24},{2... | collective-permute-start | bytes 933896 | tf_op jit(solution)/shard_map/ppermute | solution.py:425
  53.6 9.7 %collective-permute-start.10 = (bf16[19,64,128]{2,1,0:T(8,128)(2,1)S(1)}, bf16[19,64,128]{2,1,0:T(8,128)(2,1)S(1)}, u32[]{:S(2)}, u32[]{:S(2)}) collective-permute-start(bf16[19,64,128]{2,1,0:T(8,128)(2,1)S(1)} %get-tuple-element.53), channel_id=1, source_target_pairs={{16,31},{17,24},{18,25},{19,26},{20,27},{21,28},{22,29},{23,30},{2... | collective-permute-start | bytes 933896 | tf_op jit(solution)/shard_map/ppermute | solution.py:425
  53.7 9.6 %collective-permute-start.11 = (bf16[32,64,128]{2,1,0:T(8,128)(2,1)S(1)}, bf16[32,64,128]{2,1,0:T(8,128)(2,1)S(1)}, u32[]{:S(2)}, u32[]{:S(2)}) collective-permute-start(bf16[32,64,128]{2,1,0:T(8,128)(2,1)S(1)} %get-tuple-element.54.refs_6_), channel_id=1, source_target_pairs={{16,24},{17,25},{18,26},{19,27},{20,28},{21,29},{22,30},{23,31},{2... | collective-permute-start | bytes 1572872 | tf_op jit(solution)/shard_map/ppermute | solution.py:425
  57.4 10.6 %copy-start.6 = (bf16[32,64,128]{2,1,0:T(8,128)(2,1)}, bf16[32,64,128]{2,1,0:T(8,128)(2,1)S(1)}, u32[]{:S(2)}) copy-start(bf16[32,64,128]{2,1,0:T(8,128)(2,1)S(1)} %get-tuple-element.69.refs_6_) | copy-start | bytes 1572868
  57.4 10.6 %collective-permute-start.20 = (bf16[18,64,128]{2,1,0:T(8,128)(2,1)S(1)}, bf16[18,64,128]{2,1,0:T(8,128)(2,1)S(1)}, u32[]{:S(2)}, u32[]{:S(2)}) collective-permute-start(bf16[18,64,128]{2,1,0:T(8,128)(2,1)S(1)} %get-tuple-element.67), channel_id=1, source_target_pairs={{16,31},{17,24},{18,25},{19,26},{20,27},{21,28},{22,29},{23,30},{2... | collective-permute-start | bytes 884744 | tf_op jit(solution)/shard_map/ppermute | solution.py:425
  62.6 8.8 %collective-permute-start.21 = (bf16[18,64,128]{2,1,0:T(8,128)(2,1)S(1)}, bf16[18,64,128]{2,1,0:T(8,128)(2,1)S(1)}, u32[]{:S(2)}, u32[]{:S(2)}) collective-permute-start(bf16[18,64,128]{2,1,0:T(8,128)(2,1)S(1)} %get-tuple-element.68), channel_id=1, source_target_pairs={{16,25},{17,26},{18,27},{19,28},{20,29},{21,30},{22,31},{23,24},{2... | collective-permute-start | bytes 884744 | tf_op jit(solution)/shard_map/ppermute | solution.py:425
  62.7 8.8 %collective-permute-start.22 = (bf16[32,64,128]{2,1,0:T(8,128)(2,1)S(1)}, bf16[32,64,128]{2,1,0:T(8,128)(2,1)S(1)}, u32[]{:S(2)}, u32[]{:S(2)}) collective-permute-start(bf16[32,64,128]{2,1,0:T(8,128)(2,1)S(1)} %get-tuple-element.69.refs_6_), channel_id=1, source_target_pairs={{16,24},{17,25},{18,26},{19,27},{20,28},{21,29},{22,30},{23,31},{2... | collective-permute-start | bytes 1572872 | tf_op jit(solution)/shard_map/ppermute | solution.py:425

commit v7 on v6

--- a/solution.py
+++ b/solution.py
@@ -9,6 +9,7 @@
 
 AXES = ("comp", "tile")
 SHARES = (1, 1)
+PAIRS = 4
 EDGE = 2
 LIMIT = 24 << 20
 ORDERS = (((0, 1), (0, 1)), ((-2, -1, 0), (-1, -2, 0)))
@@ -254,26 +255,37 @@
             rate = k_v[i:i + 1, :]
             return (1.0 - 4.0 * rate) * here + rate * ((north + south) + east_west)
 
-        def pair_beside(a, b):
-            both = jnp.concatenate([a.astype(jnp.bfloat16), b.astype(jnp.bfloat16)], axis=1)
-            total = jnp.dot(both, beside, preferred_element_type=jnp.float32)
-            return total[:, :cells], total[:, cells:]
-
-        there, after = None, entry(0)
-        for i in range(0, extent, 2):
-            before, here, there = there, after, entry(i + 1)
-            after = entry(i + 2) if i + 2 < extent else None
-            ew_here, ew_there = pair_beside(here, there)
-            if i > 0:
-                once[i] = step(i, here, before, there, ew_here)
-            if i + 2 < extent:
-                once[i + 1] = step(i + 1, there, here, after, ew_there)
-        for i in range(2, extent - 2, 2):
-            here, there = once[i], once[i + 1]
-            ew_here, ew_there = pair_beside(here, there)
-            out = i // 2 - 1
-            smooth[out, :, :cells] = step(i, here, once[i - 1], there, ew_here).astype(jnp.bfloat16)
-            smooth[out, :, cells:] = step(i + 1, there, here, once[i + 2], ew_there).astype(jnp.bfloat16)
+        def sums_beside(values):
+            pairs = [
+                jnp.concatenate([a.astype(jnp.bfloat16), b.astype(jnp.bfloat16)], axis=1)
+                for a, b in zip(values[0::2], values[1::2])
+            ]
+            total = jnp.dot(jnp.concatenate(pairs, axis=0), beside, preferred_element_type=jnp.float32)
+            sums = []
+            for p in range(len(pairs)):
+                both = total[p * fields:(p + 1) * fields]
+                sums += [both[:, :cells], both[:, cells:]]
+            return sums
+
+        def sweep(fetch, start, stop, put):
+            for i in range(start, stop, 2 * PAIRS):
+                group = range(i, min(i + 2 * PAIRS, stop))
+                values = [fetch(r) for r in group]
+                sums = sums_beside(values)
+                around = [fetch(i - 1)] + values + [fetch(group[-1] + 1)]
+                for g, r in enumerate(group):
+                    put(r, around[g], around[g + 1], around[g + 2], sums[g])
+
+        def put_once(r, north, here, south, east_west):
+            if 0 < r < extent - 1:
+                once[r] = step(r, here, north, south, east_west)
+
+        def put_smooth(r, north, here, south, east_west):
+            side = slice(0, cells) if r % 2 == 0 else slice(cells, 2 * cells)
+            smooth[r // 2 - 1, :, side] = step(r, here, north, south, east_west).astype(jnp.bfloat16)
+
+        sweep(lambda r: entry(r) if 0 <= r < extent else None, 0, extent, put_once)
+        sweep(lambda r: once[r], 2, extent - 2, put_smooth)
 
         half = (halo - EDGE) * cells // block
         block_rows = block // cells

time: 76.6 us -> 75.1 us (0.980)
  starting transfers between devices: 39.6 us -> 37.4 us
  waiting for transfers between devices: 11.1 us -> 12.8 us
  Pallas kernels: 25.1 us -> 24.3 us
    ppermute x18, starting transfers between devices: 36.9 us -> 34.7 us  [send(): return lax.ppermute(value, AXES, pairs)]
    ppermute x18, waiting for transfers between devices: 5.11 us -> 6.75 us  [send(): return lax.ppermute(value, AXES, pairs)]
    pallas_call x8, Pallas kernels: 13.4 us -> 12.5 us  [section(): pl.pallas_call(functools.partial(section_kernel, order, number, bounds, h...]
where the time goes in v7:
time: 75.1 us; the launch traced here: 74.9 us
  starting transfers between devices  37.4 us (50%)
  Pallas kernels  24.3 us (32%)
  waiting for transfers between devices  12.8 us (17%)
    ppermute x18, starting transfers between devices, send(): return lax.ppermute(value, AXES, pairs)  34.7 us
    pallas_call x8, Pallas kernels, section(): pl.pallas_call(functools.partial(section_kernel, order, number, bounds, h...  12.5 us
    pallas_call x1, Pallas kernels, load(): pl.pallas_call(functools.partial(load_kernel, len(passed)), in_specs=[SME...  9.72 us
    ppermute x18, waiting for transfers between devices, send(): return lax.ppermute(value, AXES, pairs)  6.75 us
    ppermute x4, waiting for transfers between devices, exchange(): return lax.ppermute(value, AXES, pairs)  6.03 us
    pallas_call x1, Pallas kernels, prepare(): pl.pallas_call(functools.partial(prepare_kernel, halo, marks), in_specs=[...  2.03 us
    ppermute x4, starting transfers between devices, exchange(): return lax.ppermute(value, AXES, pairs)  1.99 us
  transfers between devices with their start and end apart: 23, of which 5 were waited for; matrix products, arithmetic and copies ran while one was open for 0% of the time, Pallas kernels for 24%

profile of v7, /device:TPU:3, one launch (start us, length us, event | category | flops | bytes accessed | tf_op | source)
XLA Modules:
  0.0 74.9 jit_solution(12293836393824701068)
XLA Ops:
  0.0 0.1 pad_add_fusion._.flags
  0.1 2.0 %shard_map.46 = (f32[32,128,128]{2,1,0:T(8,128)S(1)}, bf16[33,128,128]{2,1,0:T(8,128)(2,1)S(1)}, bf16[19,64,128]{2,1,0:T(8,128)(2,1)S(1)}, bf16[19,64,128]{2,1,0...) custom-call(s32[3]{0:T(128)S(1)} %pad_add_fusion._.flags, ...), custom_call_target="tpu_custom_call" | custom-call | bytes 6291456 | tf_op jit(solution)/shard_map/pallas_call | solution.py:114
  2.1 0.7 collective-permute-start.2
  2.9 0.1 collective-permute-start
  2.9 0.1 collective-permute-start.1
  3.0 9.7 %shard_map.47 = (bf16[16,4,256,256]{3,2,1,0:T(8,128)(2,1)S(1)}, s32[4,16]{1,0:T(4,128)S(1)}, bf16[19,64,128]{2,1,0:T(8,128)(2,1)S(1)}, bf16[19,64,128]{2,1,0:T(8,128)(2,1)S(1)}) custom-call(s32[3]{0:T(128)S(1)} %pad_add_fusion._.flags, s32[4,16]{1,0:T(4,128)} %bitcast.16, ...), custom_call_target="tpu_custom_call", output_to_operand_aliasing={{2}: (3, {}), {3}: (4, {})} | custom-call | bytes 16777216 | tf_op jit(solution)/shard_map/pallas_call | solution.py:160
  12.7 1.8 %collective-permute-start.12 = (bf16[19,64,128]{2,1,0:T(8,128)(2,1)S(1)}, bf16[19,64,128]{2,1,0:T(8,128)(2,1)S(1)}, u32[]{:S(2)}, u32[]{:S(2)}) collective-permute-start(bf16[19,64,128]{2,1,0:T(8,128)(2,1)S(1)} %get-tuple-element.59), channel_id=1, source_target_pairs={{0,1},{1,0},{2,3},{3,2},{4,5},{5,4},{6,7},{7,6},{8,24},{9,25},{10,... | collective-permute-start | bytes 933896 | tf_op jit(solution)/shard_map/ppermute | solution.py:442
  14.5 0.1 collective-permute-start.13
  14.6 0.0 collective-permute-done.refs_0_.refs_4_
  14.6 0.0 collective-permute-done.1.refs_1_.refs_3_
  14.6 0.0 collective-permute-done.2.refs_2_
  14.6 0.0 copy-done
  14.6 0.6 shard_map.48
  15.2 0.0 copy-start.1
  15.2 0.1 collective-permute-start.3
  15.3 0.4 collective-permute-start.4
  15.8 0.1 collective-permute-start.5
  15.8 2.7 %collective-permute-done.12.refs_0_.refs_4_ = bf16[19,64,128]{2,1,0:T(8,128)(2,1)S(1)} collective-permute-done((bf16[19,64,128]{2,1,0:T(8,128)(2,1)S(1)}, bf16[19,64,128]{2,1,0:T(8,128)(2,1)S(1)}, u32[]{:S(2)}, u32[]{:S(2)}) %collective-permute-start.12) | collective-permute-done | bytes 311328 | tf_op jit(solution)/shard_map/ppermute | solution.py:442
  18.5 3.3 %collective-permute-done.13.refs_1_.refs_3_ = bf16[19,64,128]{2,1,0:T(8,128)(2,1)S(1)} collective-permute-done((bf16[19,64,128]{2,1,0:T(8,128)(2,1)S(1)}, bf16[19,64,128]{2,1,0:T(8,128)(2,1)S(1)}, u32[]{:S(2)}, u32[]{:S(2)}) %collective-permute-start.13) | collective-permute-done | bytes 311328 | tf_op jit(solution)/shard_map/ppermute | solution.py:442
  21.9 0.8 %shard_map.52 = (bf16[32,64,128]{2,1,0:T(8,128)(2,1)S(1)}, bf16[18,64,128]{2,1,0:T(8,128)(2,1)S(1)}, bf16[18,64,128]{2,1,0:T(8,128)(2,1)S(1)}) custom-call(s32[3]{0:T(128)S(1)} %pad_add_fusion._.flags, s32[4,16]{1,0:T(4,128)S(1)} %get-tuple-element.40.offsets, f32[68,128]{1,0:T(8,128)S(1)} %get-tuple-element.58.kappa, ...), custom_call_target="tpu_custom_call" | custom-call | flops 10737418240 | bytes 8388608 | tf_op jit(solution)/shard_map/pallas_call | solution.py:397
  22.7 0.5 collective-permute-start.14
  23.2 0.1 collective-permute-start.15
  23.2 0.0 collective-permute-done.3.refs_0_
  23.2 0.4 collective-permute-start.16
  23.7 0.0 collective-permute-done.4.refs_1_
  23.7 0.0 collective-permute-done.5.refs_2_
  23.7 0.6 shard_map.49
  24.3 0.0 copy-done.2
  24.3 0.0 copy-start.3
  24.3 6.1 %collective-permute-start.6 = (bf16[19,64,128]{2,1,0:T(8,128)(2,1)S(1)}, bf16[19,64,128]{2,1,0:T(8,128)(2,1)S(1)}, u32[]{:S(2)}, u32[]{:S(2)}) collective-permute-start(bf16[19,64,128]{2,1,0:T(8,128)(2,1)S(1)} %get-tuple-element.49), channel_id=1, source_target_pairs={{8,17},{9,18},{10,19},{11,20},{12,21},{13,22},{14,23},{15,16},{16,... | collective-permute-start | bytes 933896 | tf_op jit(solution)/shard_map/ppermute | solution.py:437
  30.4 3.0 %collective-permute-start.7 = (bf16[19,64,128]{2,1,0:T(8,128)(2,1)S(1)}, bf16[19,64,128]{2,1,0:T(8,128)(2,1)S(1)}, u32[]{:S(2)}, u32[]{:S(2)}) collective-permute-start(bf16[19,64,128]{2,1,0:T(8,128)(2,1)S(1)} %get-tuple-element.50), channel_id=1, source_target_pairs={{8,23},{9,16},{10,17},{11,18},{12,19},{13,20},{14,21},{15,22},{16,... | collective-permute-start | bytes 933896 | tf_op jit(solution)/shard_map/ppermute | solution.py:437
  33.4 0.0 collective-permute-done.14.refs_0_
  33.4 0.1 collective-permute-start.8
  33.5 0.0 collective-permute-done.15.refs_1_
  33.5 0.0 collective-permute-done.16.refs_2_
  33.5 0.6 shard_map.53
  34.1 0.0 copy-done.3
  34.1 0.0 copy-start.4
  34.1 1.1 %collective-permute-start.17 = (bf16[18,64,128]{2,1,0:T(8,128)(2,1)S(1)}, bf16[18,64,128]{2,1,0:T(8,128)(2,1)S(1)}, u32[]{:S(2)}, u32[]{:S(2)}) collective-permute-start(bf16[18,64,128]{2,1,0:T(8,128)(2,1)S(1)} %get-tuple-element.64), channel_id=1, source_target_pairs={{8,23},{9,16},{10,17},{11,18},{12,19},{13,20},{14,21},{15,22},{16,... | collective-permute-start | bytes 884744 | tf_op jit(solution)/shard_map/ppermute | solution.py:437
  35.2 5.3 %collective-permute-start.18 = (bf16[18,64,128]{2,1,0:T(8,128)(2,1)S(1)}, bf16[18,64,128]{2,1,0:T(8,128)(2,1)S(1)}, u32[]{:S(2)}, u32[]{:S(2)}) collective-permute-start(bf16[18,64,128]{2,1,0:T(8,128)(2,1)S(1)} %get-tuple-element.65), channel_id=1, source_target_pairs={{8,17},{9,18},{10,19},{11,20},{12,21},{13,22},{14,23},{15,16},{16,... | collective-permute-start | bytes 884744 | tf_op jit(solution)/shard_map/ppermute | solution.py:437
  40.4 0.0 collective-permute-done.6.refs_0_
  40.4 0.1 collective-permute-start.19
  40.5 0.0 collective-permute-done.7.refs_1_
  40.5 2.7 %collective-permute-done.8.refs_2_ = bf16[32,64,128]{2,1,0:T(8,128)(2,1)S(1)} collective-permute-done((bf16[32,64,128]{2,1,0:T(8,128)(2,1)S(1)}, bf16[32,64,128]{2,1,0:T(8,128)(2,1)S(1)}, u32[]{:S(2)}, u32[]{:S(2)}) %collective-permute-start.8) | collective-permute-done | bytes 524320 | tf_op jit(solution)/shard_map/ppermute | solution.py:437
  43.2 0.6 shard_map.50
  43.8 8.8 %collective-permute-start.9 = (bf16[19,64,128]{2,1,0:T(8,128)(2,1)S(1)}, bf16[19,64,128]{2,1,0:T(8,128)(2,1)S(1)}, u32[]{:S(2)}, u32[]{:S(2)}) collective-permute-start(bf16[19,64,128]{2,1,0:T(8,128)(2,1)S(1)} %get-tuple-element.52), channel_id=1, source_target_pairs={{16,25},{17,26},{18,27},{19,28},{20,29},{21,30},{22,31},{23,24},{2... | collective-permute-start | bytes 933896 | tf_op jit(solution)/shard_map/ppermute | solution.py:437
  52.6 0.1 collective-permute-start.10
  52.7 0.0 collective-permute-done.17.refs_0_
  52.7 2.8 %collective-permute-start.11 = (bf16[32,64,128]{2,1,0:T(8,128)(2,1)S(1)}, bf16[32,64,128]{2,1,0:T(8,128)(2,1)S(1)}, u32[]{:S(2)}, u32[]{:S(2)}) collective-permute-start(bf16[32,64,128]{2,1,0:T(8,128)(2,1)S(1)} %get-tuple-element.54.refs_6_), channel_id=1, source_target_pairs={{16,24},{17,25},{18,26},{19,27},{20,28},{21,29},{22,30},{23,31},{2... | collective-permute-start | bytes 1572872 | tf_op jit(solution)/shard_map/ppermute | solution.py:437
  55.5 0.0 collective-permute-done.18.refs_1_
  55.5 0.0 collective-permute-done.19.refs_2_
  55.5 0.8 %shard_map.54 = (bf16[32,64,128]{2,1,0:T(8,128)(2,1)S(1)}, bf16[18,64,128]{2,1,0:T(8,128)(2,1)S(1)}, bf16[18,64,128]{2,1,0:T(8,128)(2,1)S(1)}) custom-call(s32[3]{0:T(128)S(1)} %pad_add_fusion._.flags, s32[4,16]{1,0:T(4,128)S(1)} %get-tuple-element.40.offsets, f32[68,128]{1,0:T(8,128)S(1)} %get-tuple-element.56.kappa, ...), custom_call_target="tpu_custom_call" | custom-call | flops 10737418240 | bytes 8388608 | tf_op jit(solution)/shard_map/pallas_call | solution.py:397
  56.3 5.3 %collective-permute-start.20 = (bf16[18,64,128]{2,1,0:T(8,128)(2,1)S(1)}, bf16[18,64,128]{2,1,0:T(8,128)(2,1)S(1)}, u32[]{:S(2)}, u32[]{:S(2)}) collective-permute-start(bf16[18,64,128]{2,1,0:T(8,128)(2,1)S(1)} %get-tuple-element.67), channel_id=1, source_target_pairs={{16,31},{17,24},{18,25},{19,26},{20,27},{21,28},{22,29},{23,30},{2... | collective-permute-start | bytes 884744 | tf_op jit(solution)/shard_map/ppermute | solution.py:437
  61.6 0.1 collective-permute-start.21
  61.6 0.0 collective-permute-done.9.refs_0_
  61.6 0.5 collective-permute-start.22
  62.1 0.2 collective-permute-done.10.refs_1_
  62.3 0.0 collective-permute-done.11.refs_2_
  62.3 4.3 %shard_map.51 = (bf16[128,32,128]{2,1,0:T(8,128)(2,1)}, f32[68,128]{1,0:T(8,128)S(1)}) custom-call(s32[3]{0:T(128)S(1)} %pad_add_fusion._.flags, s32[4,16]{1,0:T(4,128)S(1)} %get-tuple-element.40.offsets, f32[32,128]{1,0:T(8,128)S(1)} %bitcast.13, f32[32,128,128]{2,1,0:T(8,128)S(1)} %get-tuple-element.41.forcing, ...), custom_call_target="tpu_custom_call" | custom-call | flops 10737418240 | bytes 8388608 | tf_op jit(solution)/shard_map/pallas_call | solution.py:397
  66.6 0.0 copy-done.6
  66.6 0.0 collective-permute-done.20.refs_0_
  66.6 3.8 %collective-permute-done.21.refs_1_ = bf16[18,64,128]{2,1,0:T(8,128)(2,1)S(1)} collective-permute-done((bf16[18,64,128]{2,1,0:T(8,128)(2,1)S(1)}, bf16[18,64,128]{2,1,0:T(8,128)(2,1)S(1)}, u32[]{:S(2)}, u32[]{:S(2)}) %collective-permute-start.21) | collective-permute-done | bytes 294944 | tf_op jit(solution)/shard_map/ppermute | solution.py:437
  70.4 0.0 collective-permute-done.22.refs_2_
  70.4 4.3 %shard_map.55 = bf16[128,32,128]{2,1,0:T(8,128)(2,1)} custom-call(s32[3]{0:T(128)S(1)} %pad_add_fusion._.flags, s32[4,16]{1,0:T(4,128)S(1)} %get-tuple-element.40.offsets, f32[68,128]{1,0:T(8,128)S(1)} %get-tuple-element.55.kappa, f32[32,128,128]{2,1,0:T(8,128)S(1)} %get-tuple-element.41.forcing, ...), custom_call_target="tpu_custom_call", output_to_operand_aliasing={{}: (11, {})} | custom-call | flops 10737418240 | bytes 8388608 | tf_op jit(solution)/shard_map/pallas_call | solution.py:397
  (7 shorter events, 0.0 us)
Async XLA Ops:
  2.1 12.5 %collective-permute-start.2 = (bf16[33,128,128]{2,1,0:T(8,128)(2,1)S(1)}, bf16[33,128,128]{2,1,0:T(8,128)(2,1)S(1)}, u32[]{:S(2)}, u32[]{:S(2)}) collective-permute-start(bf16[33,128,128]{2,1,0:T(8,128)(2,1)S(1)} %get-tuple-element.44), channel_id=1, source_target_pairs={{0,8},{8,0},{16,24},{24,16},{1,9},{9,1},{17,25},{25,17},{2,10},{10... | collective-permute-start | bytes 3244040 | tf_op jit(solution)/shard_map/ppermute | solution.py:451
  2.9 11.7 %collective-permute-start = (bf16[19,64,128]{2,1,0:T(8,128)(2,1)S(1)}, bf16[19,64,128]{2,1,0:T(8,128)(2,1)S(1)}, u32[]{:S(2)}, u32[]{:S(2)}) collective-permute-start(bf16[19,64,128]{2,1,0:T(8,128)(2,1)S(1)} %get-tuple-element.42), channel_id=1, source_target_pairs={{0,1},{1,0},{2,3},{3,2},{4,5},{5,4},{6,7},{7,6},{8,24},{9,25},{10,... | collective-permute-start | bytes 933896 | tf_op jit(solution)/shard_map/ppermute | solution.py:442
  2.9 11.6 %collective-permute-start.1 = (bf16[19,64,128]{2,1,0:T(8,128)(2,1)S(1)}, bf16[19,64,128]{2,1,0:T(8,128)(2,1)S(1)}, u32[]{:S(2)}, u32[]{:S(2)}) collective-permute-start(bf16[19,64,128]{2,1,0:T(8,128)(2,1)S(1)} %get-tuple-element.43), channel_id=1, source_target_pairs={{0,7},{1,2},{2,1},{3,4},{4,3},{5,6},{6,5},{7,0},{8,24},{9,25},{10,... | collective-permute-start | bytes 933896 | tf_op jit(solution)/shard_map/ppermute | solution.py:442
  3.0 11.6 %copy-start = (f32[1,32,128]{2,1,0:T(8,128)S(1)}, f32[1,32,128]{2,1,0:T(8,128)}, u32[]{:S(2)}) copy-start(f32[1,32,128]{2,1,0:T(8,128)} %param.5) | copy-start | bytes 49156
  12.7 5.8 %collective-permute-start.12 = (bf16[19,64,128]{2,1,0:T(8,128)(2,1)S(1)}, bf16[19,64,128]{2,1,0:T(8,128)(2,1)S(1)}, u32[]{:S(2)}, u32[]{:S(2)}) collective-permute-start(bf16[19,64,128]{2,1,0:T(8,128)(2,1)S(1)} %get-tuple-element.59), channel_id=1, source_target_pairs={{0,1},{1,0},{2,3},{3,2},{4,5},{5,4},{6,7},{7,6},{8,24},{9,25},{10,... | collective-permute-start | bytes 933896 | tf_op jit(solution)/shard_map/ppermute | solution.py:442
  14.5 7.4 %collective-permute-start.13 = (bf16[19,64,128]{2,1,0:T(8,128)(2,1)S(1)}, bf16[19,64,128]{2,1,0:T(8,128)(2,1)S(1)}, u32[]{:S(2)}, u32[]{:S(2)}) collective-permute-start(bf16[19,64,128]{2,1,0:T(8,128)(2,1)S(1)} %get-tuple-element.60), channel_id=1, source_target_pairs={{0,7},{1,2},{2,1},{3,4},{4,3},{5,6},{6,5},{7,0},{8,24},{9,25},{10,... | collective-permute-start | bytes 933896 | tf_op jit(solution)/shard_map/ppermute | solution.py:442
  15.2 7.4 %copy-start.1 = (bf16[32,64,128]{2,1,0:T(8,128)(2,1)}, bf16[32,64,128]{2,1,0:T(8,128)(2,1)S(1)}, u32[]{:S(2)}) copy-start(bf16[32,64,128]{2,1,0:T(8,128)(2,1)S(1)} %get-tuple-element.48.refs_4_) | copy-start | bytes 1572868
  15.2 8.0 %collective-permute-start.3 = (bf16[19,64,128]{2,1,0:T(8,128)(2,1)S(1)}, bf16[19,64,128]{2,1,0:T(8,128)(2,1)S(1)}, u32[]{:S(2)}, u32[]{:S(2)}) collective-permute-start(bf16[19,64,128]{2,1,0:T(8,128)(2,1)S(1)} %get-tuple-element.46), channel_id=1, source_target_pairs={{0,9},{1,10},{2,11},{3,12},{4,13},{5,14},{6,15},{7,8},{8,0},{9,1},... | collective-permute-start | bytes 933896 | tf_op jit(solution)/shard_map/ppermute | solution.py:437
  15.3 8.4 %collective-permute-start.4 = (bf16[19,64,128]{2,1,0:T(8,128)(2,1)S(1)}, bf16[19,64,128]{2,1,0:T(8,128)(2,1)S(1)}, u32[]{:S(2)}, u32[]{:S(2)}) collective-permute-start(bf16[19,64,128]{2,1,0:T(8,128)(2,1)S(1)} %get-tuple-element.47), channel_id=1, source_target_pairs={{0,15},{1,8},{2,9},{3,10},{4,11},{5,12},{6,13},{7,14},{8,0},{9,1},... | collective-permute-start | bytes 933896 | tf_op jit(solution)/shard_map/ppermute | solution.py:437
  15.8 7.9 %collective-permute-start.5 = (bf16[32,64,128]{2,1,0:T(8,128)(2,1)S(1)}, bf16[32,64,128]{2,1,0:T(8,128)(2,1)S(1)}, u32[]{:S(2)}, u32[]{:S(2)}) collective-permute-start(bf16[32,64,128]{2,1,0:T(8,128)(2,1)S(1)} %get-tuple-element.48.refs_4_), channel_id=1, source_target_pairs={{0,8},{1,9},{2,10},{3,11},{4,12},{5,13},{6,14},{7,15},{8,0},{9,1},... | collective-permute-start | bytes 1572872 | tf_op jit(solution)/shard_map/ppermute | solution.py:437
  22.6 1.6 %copy-start.2 = (bf16[32,64,128]{2,1,0:T(8,128)(2,1)}, bf16[32,64,128]{2,1,0:T(8,128)(2,1)S(1)}, u32[]{:S(2)}) copy-start(bf16[32,64,128]{2,1,0:T(8,128)(2,1)S(1)} %get-tuple-element.63.refs_4_) | copy-start | bytes 1572868
  22.7 10.7 %collective-permute-start.14 = (bf16[18,64,128]{2,1,0:T(8,128)(2,1)S(1)}, bf16[18,64,128]{2,1,0:T(8,128)(2,1)S(1)}, u32[]{:S(2)}, u32[]{:S(2)}) collective-permute-start(bf16[18,64,128]{2,1,0:T(8,128)(2,1)S(1)} %get-tuple-element.61), channel_id=1, source_target_pairs={{0,15},{1,8},{2,9},{3,10},{4,11},{5,12},{6,13},{7,14},{8,0},{9,1},... | collective-permute-start | bytes 884744 | tf_op jit(solution)/shard_map/ppermute | solution.py:437
  23.2 10.3 %collective-permute-start.15 = (bf16[18,64,128]{2,1,0:T(8,128)(2,1)S(1)}, bf16[18,64,128]{2,1,0:T(8,128)(2,1)S(1)}, u32[]{:S(2)}, u32[]{:S(2)}) collective-permute-start(bf16[18,64,128]{2,1,0:T(8,128)(2,1)S(1)} %get-tuple-element.62), channel_id=1, source_target_pairs={{0,9},{1,10},{2,11},{3,12},{4,13},{5,14},{6,15},{7,8},{8,0},{9,1},... | collective-permute-start | bytes 884744 | tf_op jit(solution)/shard_map/ppermute | solution.py:437
  23.2 10.3 %collective-permute-start.16 = (bf16[32,64,128]{2,1,0:T(8,128)(2,1)S(1)}, bf16[32,64,128]{2,1,0:T(8,128)(2,1)S(1)}, u32[]{:S(2)}, u32[]{:S(2)}) collective-permute-start(bf16[32,64,128]{2,1,0:T(8,128)(2,1)S(1)} %get-tuple-element.63.refs_4_), channel_id=1, source_target_pairs={{0,8},{1,9},{2,10},{3,11},{4,12},{5,13},{6,14},{7,15},{8,0},{9,1},... | collective-permute-start | bytes 1572872 | tf_op jit(solution)/shard_map/ppermute | solution.py:437
  24.3 9.8 %copy-start.3 = (bf16[32,64,128]{2,1,0:T(8,128)(2,1)}, bf16[32,64,128]{2,1,0:T(8,128)(2,1)S(1)}, u32[]{:S(2)}) copy-start(bf16[32,64,128]{2,1,0:T(8,128)(2,1)S(1)} %get-tuple-element.51.refs_5_) | copy-start | bytes 1572868
  24.3 16.1 %collective-permute-start.6 = (bf16[19,64,128]{2,1,0:T(8,128)(2,1)S(1)}, bf16[19,64,128]{2,1,0:T(8,128)(2,1)S(1)}, u32[]{:S(2)}, u32[]{:S(2)}) collective-permute-start(bf16[19,64,128]{2,1,0:T(8,128)(2,1)S(1)} %get-tuple-element.49), channel_id=1, source_target_pairs={{8,17},{9,18},{10,19},{11,20},{12,21},{13,22},{14,23},{15,16},{16,... | collective-permute-start | bytes 933896 | tf_op jit(solution)/shard_map/ppermute | solution.py:437
  30.4 10.1 %collective-permute-start.7 = (bf16[19,64,128]{2,1,0:T(8,128)(2,1)S(1)}, bf16[19,64,128]{2,1,0:T(8,128)(2,1)S(1)}, u32[]{:S(2)}, u32[]{:S(2)}) collective-permute-start(bf16[19,64,128]{2,1,0:T(8,128)(2,1)S(1)} %get-tuple-element.50), channel_id=1, source_target_pairs={{8,23},{9,16},{10,17},{11,18},{12,19},{13,20},{14,21},{15,22},{16,... | collective-permute-start | bytes 933896 | tf_op jit(solution)/shard_map/ppermute | solution.py:437
  33.4 9.8 %collective-permute-start.8 = (bf16[32,64,128]{2,1,0:T(8,128)(2,1)S(1)}, bf16[32,64,128]{2,1,0:T(8,128)(2,1)S(1)}, u32[]{:S(2)}, u32[]{:S(2)}) collective-permute-start(bf16[32,64,128]{2,1,0:T(8,128)(2,1)S(1)} %get-tuple-element.51.refs_5_), channel_id=1, source_target_pairs={{8,16},{9,17},{10,18},{11,19},{12,20},{13,21},{14,22},{15,23},{16,... | collective-permute-start | bytes 1572872 | tf_op jit(solution)/shard_map/ppermute | solution.py:437
  34.1 9.7 %copy-start.4 = (bf16[32,64,128]{2,1,0:T(8,128)(2,1)}, bf16[32,64,128]{2,1,0:T(8,128)(2,1)S(1)}, u32[]{:S(2)}) copy-start(bf16[32,64,128]{2,1,0:T(8,128)(2,1)S(1)} %get-tuple-element.66.refs_5_) | copy-start | bytes 1572868
  34.1 18.6 %collective-permute-start.17 = (bf16[18,64,128]{2,1,0:T(8,128)(2,1)S(1)}, bf16[18,64,128]{2,1,0:T(8,128)(2,1)S(1)}, u32[]{:S(2)}, u32[]{:S(2)}) collective-permute-start(bf16[18,64,128]{2,1,0:T(8,128)(2,1)S(1)} %get-tuple-element.64), channel_id=1, source_target_pairs={{8,23},{9,16},{10,17},{11,18},{12,19},{13,20},{14,21},{15,22},{16,... | collective-permute-start | bytes 884744 | tf_op jit(solution)/shard_map/ppermute | solution.py:437
  35.2 20.3 %collective-permute-start.18 = (bf16[18,64,128]{2,1,0:T(8,128)(2,1)S(1)}, bf16[18,64,128]{2,1,0:T(8,128)(2,1)S(1)}, u32[]{:S(2)}, u32[]{:S(2)}) collective-permute-start(bf16[18,64,128]{2,1,0:T(8,128)(2,1)S(1)} %get-tuple-element.65), channel_id=1, source_target_pairs={{8,17},{9,18},{10,19},{11,20},{12,21},{13,22},{14,23},{15,16},{16,... | collective-permute-start | bytes 884744 | tf_op jit(solution)/shard_map/ppermute | solution.py:437
  40.4 15.1 %collective-permute-start.19 = (bf16[32,64,128]{2,1,0:T(8,128)(2,1)S(1)}, bf16[32,64,128]{2,1,0:T(8,128)(2,1)S(1)}, u32[]{:S(2)}, u32[]{:S(2)}) collective-permute-start(bf16[32,64,128]{2,1,0:T(8,128)(2,1)S(1)} %get-tuple-element.66.refs_5_), channel_id=1, source_target_pairs={{8,16},{9,17},{10,18},{11,19},{12,20},{13,21},{14,22},{15,23},{16,... | collective-permute-start | bytes 1572872 | tf_op jit(solution)/shard_map/ppermute | solution.py:437
  43.8 12.5 %copy-start.5 = (bf16[32,64,128]{2,1,0:T(8,128)(2,1)}, bf16[32,64,128]{2,1,0:T(8,128)(2,1)S(1)}, u32[]{:S(2)}) copy-start(bf16[32,64,128]{2,1,0:T(8,128)(2,1)S(1)} %get-tuple-element.54.refs_6_) | copy-start | bytes 1572868
  43.8 17.8 %collective-permute-start.9 = (bf16[19,64,128]{2,1,0:T(8,128)(2,1)S(1)}, bf16[19,64,128]{2,1,0:T(8,128)(2,1)S(1)}, u32[]{:S(2)}, u32[]{:S(2)}) collective-permute-start(bf16[19,64,128]{2,1,0:T(8,128)(2,1)S(1)} %get-tuple-element.52), channel_id=1, source_target_pairs={{16,25},{17,26},{18,27},{19,28},{20,29},{21,30},{22,31},{23,24},{2... | collective-permute-start | bytes 933896 | tf_op jit(solution)/shard_map/ppermute | solution.py:437
  52.6 9.7 %collective-permute-start.10 = (bf16[19,64,128]{2,1,0:T(8,128)(2,1)S(1)}, bf16[19,64,128]{2,1,0:T(8,128)(2,1)S(1)}, u32[]{:S(2)}, u32[]{:S(2)}) collective-permute-start(bf16[19,64,128]{2,1,0:T(8,128)(2,1)S(1)} %get-tuple-element.53), channel_id=1, source_target_pairs={{16,31},{17,24},{18,25},{19,26},{20,27},{21,28},{22,29},{23,30},{2... | collective-permute-start | bytes 933896 | tf_op jit(solution)/shard_map/ppermute | solution.py:437
  52.7 9.6 %collective-permute-start.11 = (bf16[32,64,128]{2,1,0:T(8,128)(2,1)S(1)}, bf16[32,64,128]{2,1,0:T(8,128)(2,1)S(1)}, u32[]{:S(2)}, u32[]{:S(2)}) collective-permute-start(bf16[32,64,128]{2,1,0:T(8,128)(2,1)S(1)} %get-tuple-element.54.refs_6_), channel_id=1, source_target_pairs={{16,24},{17,25},{18,26},{19,27},{20,28},{21,29},{22,30},{23,31},{2... | collective-permute-start | bytes 1572872 | tf_op jit(solution)/shard_map/ppermute | solution.py:437
  56.3 10.3 %copy-start.6 = (bf16[32,64,128]{2,1,0:T(8,128)(2,1)}, bf16[32,64,128]{2,1,0:T(8,128)(2,1)S(1)}, u32[]{:S(2)}) copy-start(bf16[32,64,128]{2,1,0:T(8,128)(2,1)S(1)} %get-tuple-element.69.refs_6_) | copy-start | bytes 1572868
  56.3 10.3 %collective-permute-start.20 = (bf16[18,64,128]{2,1,0:T(8,128)(2,1)S(1)}, bf16[18,64,128]{2,1,0:T(8,128)(2,1)S(1)}, u32[]{:S(2)}, u32[]{:S(2)}) collective-permute-start(bf16[18,64,128]{2,1,0:T(8,128)(2,1)S(1)} %get-tuple-element.67), channel_id=1, source_target_pairs={{16,31},{17,24},{18,25},{19,26},{20,27},{21,28},{22,29},{23,30},{2... | collective-permute-start | bytes 884744 | tf_op jit(solution)/shard_map/ppermute | solution.py:437
  61.6 8.8 %collective-permute-start.21 = (bf16[18,64,128]{2,1,0:T(8,128)(2,1)S(1)}, bf16[18,64,128]{2,1,0:T(8,128)(2,1)S(1)}, u32[]{:S(2)}, u32[]{:S(2)}) collective-permute-start(bf16[18,64,128]{2,1,0:T(8,128)(2,1)S(1)} %get-tuple-element.68), channel_id=1, source_target_pairs={{16,25},{17,26},{18,27},{19,28},{20,29},{21,30},{22,31},{23,24},{2... | collective-permute-start | bytes 884744 | tf_op jit(solution)/shard_map/ppermute | solution.py:437
  61.6 8.8 %collective-permute-start.22 = (bf16[32,64,128]{2,1,0:T(8,128)(2,1)S(1)}, bf16[32,64,128]{2,1,0:T(8,128)(2,1)S(1)}, u32[]{:S(2)}, u32[]{:S(2)}) collective-permute-start(bf16[32,64,128]{2,1,0:T(8,128)(2,1)S(1)} %get-tuple-element.69.refs_6_), channel_id=1, source_target_pairs={{16,24},{17,25},{18,26},{19,27},{20,28},{21,29},{22,30},{23,31},{2... | collective-permute-start | bytes 1572872 | tf_op jit(solution)/shard_map/ppermute | solution.py:437

commit v8 on v7

--- a/solution.py
+++ b/solution.py
@@ -9,7 +9,7 @@
 
 AXES = ("comp", "tile")
 SHARES = (1, 1)
-PAIRS = 4
+PAIRS = 8
 EDGE = 2
 LIMIT = 24 << 20
 ORDERS = (((0, 1), (0, 1)), ((-2, -1, 0), (-1, -2, 0)))
@@ -301,14 +301,19 @@
                 up_s[halo:] = joined([part[:halo] for part in parts], pack).reshape(tail)
                 down_s[halo:] = joined([part[rows - halo:] for part in parts], pack).reshape(tail)
         for j in range(count):
-            total = None
-            for k in range(per_row):
-                source = smooth[offsets[k, j] + (j + half)]
-                term = lax.dot_general(
-                    source, weights[j, k], (((1,), (0 if number else 1,)), ((), ())),
+            sources = [smooth[offsets[k, j] + (j + half)] for k in range(per_row)]
+            if number:
+                total = jnp.dot(
+                    jnp.concatenate(sources, axis=1), weights[j].reshape(per_row * block, block),
                     preferred_element_type=jnp.float32,
                 )
-                total = term if total is None else total + term
+            else:
+                total = None
+                for k in range(per_row):
+                    term = lax.dot_general(
+                        sources[k], weights[j, k], (((1,), (1,)), ((), ())), preferred_element_type=jnp.float32
+                    )
+                    total = term if total is None else total + term
             for r in range(block_rows):
                 row = j * block_rows + r
                 value = total[:, r * cells:(r + 1) * cells].astype(jnp.bfloat16)

time: 75.1 us -> 75 us (level)
  no operation moved by 1% of the time
where the time goes in v8:
time: 75 us; the launch traced here: 74.8 us
  starting transfers between devices  37.2 us (50%)
  Pallas kernels  24.2 us (32%)
  waiting for transfers between devices  12.9 us (17%)
    ppermute x18, starting transfers between devices, send(): return lax.ppermute(value, AXES, pairs)  34.5 us
    pallas_call x8, Pallas kernels, section(): pl.pallas_call(functools.partial(section_kernel, order, number, bounds, h...  12.4 us
    pallas_call x1, Pallas kernels, load(): pl.pallas_call(functools.partial(load_kernel, len(passed)), in_specs=[SME...  9.72 us
    ppermute x18, waiting for transfers between devices, send(): return lax.ppermute(value, AXES, pairs)  6.89 us
    ppermute x4, waiting for transfers between devices, exchange(): return lax.ppermute(value, AXES, pairs)  6.03 us
    pallas_call x1, Pallas kernels, prepare(): pl.pallas_call(functools.partial(prepare_kernel, halo, marks), in_specs=[...  2.03 us
    ppermute x4, starting transfers between devices, exchange(): return lax.ppermute(value, AXES, pairs)  1.99 us
  transfers between devices with their start and end apart: 23, of which 5 were waited for; matrix products, arithmetic and copies ran while one was open for 0% of the time, Pallas kernels for 24%

profile of v8, /device:TPU:3, one launch (start us, length us, event | category | flops | bytes accessed | tf_op | source)
XLA Modules:
  0.0 74.8 jit_solution(16994217206126465624)
XLA Ops:
  0.0 0.1 pad_add_fusion._.flags
  0.1 2.0 %shard_map.46 = (f32[32,128,128]{2,1,0:T(8,128)S(1)}, bf16[33,128,128]{2,1,0:T(8,128)(2,1)S(1)}, bf16[19,64,128]{2,1,0:T(8,128)(2,1)S(1)}, bf16[19,64,128]{2,1,0...) custom-call(s32[3]{0:T(128)S(1)} %pad_add_fusion._.flags, ...), custom_call_target="tpu_custom_call" | custom-call | bytes 6291456 | tf_op jit(solution)/shard_map/pallas_call | solution.py:114
  2.1 0.7 collective-permute-start.2
  2.9 0.1 collective-permute-start
  2.9 0.1 collective-permute-start.1
  3.0 9.7 %shard_map.47 = (bf16[16,4,256,256]{3,2,1,0:T(8,128)(2,1)S(1)}, s32[4,16]{1,0:T(4,128)S(1)}, bf16[19,64,128]{2,1,0:T(8,128)(2,1)S(1)}, bf16[19,64,128]{2,1,0:T(8,128)(2,1)S(1)}) custom-call(s32[3]{0:T(128)S(1)} %pad_add_fusion._.flags, s32[4,16]{1,0:T(4,128)} %bitcast.16, ...), custom_call_target="tpu_custom_call", output_to_operand_aliasing={{2}: (3, {}), {3}: (4, {})} | custom-call | bytes 16777216 | tf_op jit(solution)/shard_map/pallas_call | solution.py:160
  12.7 1.8 %collective-permute-start.12 = (bf16[19,64,128]{2,1,0:T(8,128)(2,1)S(1)}, bf16[19,64,128]{2,1,0:T(8,128)(2,1)S(1)}, u32[]{:S(2)}, u32[]{:S(2)}) collective-permute-start(bf16[19,64,128]{2,1,0:T(8,128)(2,1)S(1)} %get-tuple-element.59), channel_id=1, source_target_pairs={{0,1},{1,0},{2,3},{3,2},{4,5},{5,4},{6,7},{7,6},{8,24},{9,25},{10,... | collective-permute-start | bytes 933896 | tf_op jit(solution)/shard_map/ppermute | solution.py:447
  14.5 0.1 collective-permute-start.13
  14.6 0.0 collective-permute-done.refs_0_.refs_4_
  14.6 0.0 collective-permute-done.1.refs_1_.refs_3_
  14.6 0.0 collective-permute-done.2.refs_2_
  14.6 0.0 copy-done
  14.6 0.6 shard_map.48
  15.2 0.0 copy-start.1
  15.2 0.1 collective-permute-start.3
  15.3 0.4 collective-permute-start.4
  15.8 0.1 collective-permute-start.5
  15.8 2.7 %collective-permute-done.12.refs_0_.refs_4_ = bf16[19,64,128]{2,1,0:T(8,128)(2,1)S(1)} collective-permute-done((bf16[19,64,128]{2,1,0:T(8,128)(2,1)S(1)}, bf16[19,64,128]{2,1,0:T(8,128)(2,1)S(1)}, u32[]{:S(2)}, u32[]{:S(2)}) %collective-permute-start.12) | collective-permute-done | bytes 311328 | tf_op jit(solution)/shard_map/ppermute | solution.py:447
  18.5 3.3 %collective-permute-done.13.refs_1_.refs_3_ = bf16[19,64,128]{2,1,0:T(8,128)(2,1)S(1)} collective-permute-done((bf16[19,64,128]{2,1,0:T(8,128)(2,1)S(1)}, bf16[19,64,128]{2,1,0:T(8,128)(2,1)S(1)}, u32[]{:S(2)}, u32[]{:S(2)}) %collective-permute-start.13) | collective-permute-done | bytes 311328 | tf_op jit(solution)/shard_map/ppermute | solution.py:447
  21.9 0.8 %shard_map.52 = (bf16[32,64,128]{2,1,0:T(8,128)(2,1)S(1)}, bf16[18,64,128]{2,1,0:T(8,128)(2,1)S(1)}, bf16[18,64,128]{2,1,0:T(8,128)(2,1)S(1)}) custom-call(s32[3]{0:T(128)S(1)} %pad_add_fusion._.flags, s32[4,16]{1,0:T(4,128)S(1)} %get-tuple-element.40.offsets, f32[68,128]{1,0:T(8,128)S(1)} %get-tuple-element.58.kappa, ...), custom_call_target="tpu_custom_call" | custom-call | flops 10737418240 | bytes 8388608 | tf_op jit(solution)/shard_map/pallas_call | solution.py:402
  22.7 0.5 collective-permute-start.14
  23.2 0.1 collective-permute-start.15
  23.2 0.0 collective-permute-done.3.refs_0_
  23.2 0.4 collective-permute-start.16
  23.7 0.0 collective-permute-done.4.refs_1_
  23.7 0.0 collective-permute-done.5.refs_2_
  23.7 0.6 shard_map.49
  24.3 0.0 copy-done.2
  24.3 0.0 copy-start.3
  24.3 6.1 %collective-permute-start.6 = (bf16[19,64,128]{2,1,0:T(8,128)(2,1)S(1)}, bf16[19,64,128]{2,1,0:T(8,128)(2,1)S(1)}, u32[]{:S(2)}, u32[]{:S(2)}) collective-permute-start(bf16[19,64,128]{2,1,0:T(8,128)(2,1)S(1)} %get-tuple-element.49), channel_id=1, source_target_pairs={{8,17},{9,18},{10,19},{11,20},{12,21},{13,22},{14,23},{15,16},{16,... | collective-permute-start | bytes 933896 | tf_op jit(solution)/shard_map/ppermute | solution.py:442
  30.4 2.9 %collective-permute-start.7 = (bf16[19,64,128]{2,1,0:T(8,128)(2,1)S(1)}, bf16[19,64,128]{2,1,0:T(8,128)(2,1)S(1)}, u32[]{:S(2)}, u32[]{:S(2)}) collective-permute-start(bf16[19,64,128]{2,1,0:T(8,128)(2,1)S(1)} %get-tuple-element.50), channel_id=1, source_target_pairs={{8,23},{9,16},{10,17},{11,18},{12,19},{13,20},{14,21},{15,22},{16,... | collective-permute-start | bytes 933896 | tf_op jit(solution)/shard_map/ppermute | solution.py:442
  33.3 0.0 collective-permute-done.14.refs_0_
  33.4 0.1 collective-permute-start.8
  33.5 0.0 collective-permute-done.15.refs_1_
  33.5 0.0 collective-permute-done.16.refs_2_
  33.5 0.6 shard_map.53
  34.1 0.0 copy-done.3
  34.1 0.0 copy-start.4
  34.1 1.1 %collective-permute-start.17 = (bf16[18,64,128]{2,1,0:T(8,128)(2,1)S(1)}, bf16[18,64,128]{2,1,0:T(8,128)(2,1)S(1)}, u32[]{:S(2)}, u32[]{:S(2)}) collective-permute-start(bf16[18,64,128]{2,1,0:T(8,128)(2,1)S(1)} %get-tuple-element.64), channel_id=1, source_target_pairs={{8,23},{9,16},{10,17},{11,18},{12,19},{13,20},{14,21},{15,22},{16,... | collective-permute-start | bytes 884744 | tf_op jit(solution)/shard_map/ppermute | solution.py:442
  35.2 5.2 %collective-permute-start.18 = (bf16[18,64,128]{2,1,0:T(8,128)(2,1)S(1)}, bf16[18,64,128]{2,1,0:T(8,128)(2,1)S(1)}, u32[]{:S(2)}, u32[]{:S(2)}) collective-permute-start(bf16[18,64,128]{2,1,0:T(8,128)(2,1)S(1)} %get-tuple-element.65), channel_id=1, source_target_pairs={{8,17},{9,18},{10,19},{11,20},{12,21},{13,22},{14,23},{15,16},{16,... | collective-permute-start | bytes 884744 | tf_op jit(solution)/shard_map/ppermute | solution.py:442
  40.3 0.0 collective-permute-done.6.refs_0_
  40.3 0.1 collective-permute-start.19
  40.4 0.0 collective-permute-done.7.refs_1_
  40.4 2.8 %collective-permute-done.8.refs_2_ = bf16[32,64,128]{2,1,0:T(8,128)(2,1)S(1)} collective-permute-done((bf16[32,64,128]{2,1,0:T(8,128)(2,1)S(1)}, bf16[32,64,128]{2,1,0:T(8,128)(2,1)S(1)}, u32[]{:S(2)}, u32[]{:S(2)}) %collective-permute-start.8) | collective-permute-done | bytes 524320 | tf_op jit(solution)/shard_map/ppermute | solution.py:442
  43.2 0.6 shard_map.50
  43.8 8.7 %collective-permute-start.9 = (bf16[19,64,128]{2,1,0:T(8,128)(2,1)S(1)}, bf16[19,64,128]{2,1,0:T(8,128)(2,1)S(1)}, u32[]{:S(2)}, u32[]{:S(2)}) collective-permute-start(bf16[19,64,128]{2,1,0:T(8,128)(2,1)S(1)} %get-tuple-element.52), channel_id=1, source_target_pairs={{16,25},{17,26},{18,27},{19,28},{20,29},{21,30},{22,31},{23,24},{2... | collective-permute-start | bytes 933896 | tf_op jit(solution)/shard_map/ppermute | solution.py:442
  52.5 0.1 collective-permute-start.10
  52.6 0.0 collective-permute-done.17.refs_0_
  52.6 2.8 %collective-permute-start.11 = (bf16[32,64,128]{2,1,0:T(8,128)(2,1)S(1)}, bf16[32,64,128]{2,1,0:T(8,128)(2,1)S(1)}, u32[]{:S(2)}, u32[]{:S(2)}) collective-permute-start(bf16[32,64,128]{2,1,0:T(8,128)(2,1)S(1)} %get-tuple-element.54.refs_6_), channel_id=1, source_target_pairs={{16,24},{17,25},{18,26},{19,27},{20,28},{21,29},{22,30},{23,31},{2... | collective-permute-start | bytes 1572872 | tf_op jit(solution)/shard_map/ppermute | solution.py:442
  55.4 0.0 collective-permute-done.18.refs_1_
  55.4 0.0 collective-permute-done.19.refs_2_
  55.4 0.8 %shard_map.54 = (bf16[32,64,128]{2,1,0:T(8,128)(2,1)S(1)}, bf16[18,64,128]{2,1,0:T(8,128)(2,1)S(1)}, bf16[18,64,128]{2,1,0:T(8,128)(2,1)S(1)}) custom-call(s32[3]{0:T(128)S(1)} %pad_add_fusion._.flags, s32[4,16]{1,0:T(4,128)S(1)} %get-tuple-element.40.offsets, f32[68,128]{1,0:T(8,128)S(1)} %get-tuple-element.56.kappa, ...), custom_call_target="tpu_custom_call" | custom-call | flops 10737418240 | bytes 8388608 | tf_op jit(solution)/shard_map/pallas_call | solution.py:402
  56.2 5.3 %collective-permute-start.20 = (bf16[18,64,128]{2,1,0:T(8,128)(2,1)S(1)}, bf16[18,64,128]{2,1,0:T(8,128)(2,1)S(1)}, u32[]{:S(2)}, u32[]{:S(2)}) collective-permute-start(bf16[18,64,128]{2,1,0:T(8,128)(2,1)S(1)} %get-tuple-element.67), channel_id=1, source_target_pairs={{16,31},{17,24},{18,25},{19,26},{20,27},{21,28},{22,29},{23,30},{2... | collective-permute-start | bytes 884744 | tf_op jit(solution)/shard_map/ppermute | solution.py:442
  61.5 0.1 collective-permute-start.21
  61.6 0.0 collective-permute-done.9.refs_0_
  61.6 0.4 collective-permute-start.22
  62.0 0.2 collective-permute-done.10.refs_1_
  62.2 0.0 collective-permute-done.11.refs_2_
  62.2 4.3 %shard_map.51 = (bf16[128,32,128]{2,1,0:T(8,128)(2,1)}, f32[68,128]{1,0:T(8,128)S(1)}) custom-call(s32[3]{0:T(128)S(1)} %pad_add_fusion._.flags, s32[4,16]{1,0:T(4,128)S(1)} %get-tuple-element.40.offsets, f32[32,128]{1,0:T(8,128)S(1)} %bitcast.13, f32[32,128,128]{2,1,0:T(8,128)S(1)} %get-tuple-element.41.forcing, ...), custom_call_target="tpu_custom_call" | custom-call | flops 10737418240 | bytes 8388608 | tf_op jit(solution)/shard_map/pallas_call | solution.py:402
  66.5 0.0 copy-done.6
  66.5 0.0 collective-permute-done.20.refs_0_
  66.5 3.9 %collective-permute-done.21.refs_1_ = bf16[18,64,128]{2,1,0:T(8,128)(2,1)S(1)} collective-permute-done((bf16[18,64,128]{2,1,0:T(8,128)(2,1)S(1)}, bf16[18,64,128]{2,1,0:T(8,128)(2,1)S(1)}, u32[]{:S(2)}, u32[]{:S(2)}) %collective-permute-start.21) | collective-permute-done | bytes 294944 | tf_op jit(solution)/shard_map/ppermute | solution.py:442
  70.3 0.0 collective-permute-done.22.refs_2_
  70.4 4.3 %shard_map.55 = bf16[128,32,128]{2,1,0:T(8,128)(2,1)} custom-call(s32[3]{0:T(128)S(1)} %pad_add_fusion._.flags, s32[4,16]{1,0:T(4,128)S(1)} %get-tuple-element.40.offsets, f32[68,128]{1,0:T(8,128)S(1)} %get-tuple-element.55.kappa, f32[32,128,128]{2,1,0:T(8,128)S(1)} %get-tuple-element.41.forcing, ...), custom_call_target="tpu_custom_call", output_to_operand_aliasing={{}: (11, {})} | custom-call | flops 10737418240 | bytes 8388608 | tf_op jit(solution)/shard_map/pallas_call | solution.py:402
  (7 shorter events, 0.0 us)
Async XLA Ops:
  2.1 12.5 %collective-permute-start.2 = (bf16[33,128,128]{2,1,0:T(8,128)(2,1)S(1)}, bf16[33,128,128]{2,1,0:T(8,128)(2,1)S(1)}, u32[]{:S(2)}, u32[]{:S(2)}) collective-permute-start(bf16[33,128,128]{2,1,0:T(8,128)(2,1)S(1)} %get-tuple-element.44), channel_id=1, source_target_pairs={{0,8},{8,0},{16,24},{24,16},{1,9},{9,1},{17,25},{25,17},{2,10},{10... | collective-permute-start | bytes 3244040 | tf_op jit(solution)/shard_map/ppermute | solution.py:456
  2.9 11.7 %collective-permute-start = (bf16[19,64,128]{2,1,0:T(8,128)(2,1)S(1)}, bf16[19,64,128]{2,1,0:T(8,128)(2,1)S(1)}, u32[]{:S(2)}, u32[]{:S(2)}) collective-permute-start(bf16[19,64,128]{2,1,0:T(8,128)(2,1)S(1)} %get-tuple-element.42), channel_id=1, source_target_pairs={{0,1},{1,0},{2,3},{3,2},{4,5},{5,4},{6,7},{7,6},{8,24},{9,25},{10,... | collective-permute-start | bytes 933896 | tf_op jit(solution)/shard_map/ppermute | solution.py:447
  2.9 11.6 %collective-permute-start.1 = (bf16[19,64,128]{2,1,0:T(8,128)(2,1)S(1)}, bf16[19,64,128]{2,1,0:T(8,128)(2,1)S(1)}, u32[]{:S(2)}, u32[]{:S(2)}) collective-permute-start(bf16[19,64,128]{2,1,0:T(8,128)(2,1)S(1)} %get-tuple-element.43), channel_id=1, source_target_pairs={{0,7},{1,2},{2,1},{3,4},{4,3},{5,6},{6,5},{7,0},{8,24},{9,25},{10,... | collective-permute-start | bytes 933896 | tf_op jit(solution)/shard_map/ppermute | solution.py:447
  3.0 11.6 %copy-start = (f32[1,32,128]{2,1,0:T(8,128)S(1)}, f32[1,32,128]{2,1,0:T(8,128)}, u32[]{:S(2)}) copy-start(f32[1,32,128]{2,1,0:T(8,128)} %param.5) | copy-start | bytes 49156
  12.7 5.8 %collective-permute-start.12 = (bf16[19,64,128]{2,1,0:T(8,128)(2,1)S(1)}, bf16[19,64,128]{2,1,0:T(8,128)(2,1)S(1)}, u32[]{:S(2)}, u32[]{:S(2)}) collective-permute-start(bf16[19,64,128]{2,1,0:T(8,128)(2,1)S(1)} %get-tuple-element.59), channel_id=1, source_target_pairs={{0,1},{1,0},{2,3},{3,2},{4,5},{5,4},{6,7},{7,6},{8,24},{9,25},{10,... | collective-permute-start | bytes 933896 | tf_op jit(solution)/shard_map/ppermute | solution.py:447
  14.5 7.4 %collective-permute-start.13 = (bf16[19,64,128]{2,1,0:T(8,128)(2,1)S(1)}, bf16[19,64,128]{2,1,0:T(8,128)(2,1)S(1)}, u32[]{:S(2)}, u32[]{:S(2)}) collective-permute-start(bf16[19,64,128]{2,1,0:T(8,128)(2,1)S(1)} %get-tuple-element.60), channel_id=1, source_target_pairs={{0,7},{1,2},{2,1},{3,4},{4,3},{5,6},{6,5},{7,0},{8,24},{9,25},{10,... | collective-permute-start | bytes 933896 | tf_op jit(solution)/shard_map/ppermute | solution.py:447
  15.2 7.4 %copy-start.1 = (bf16[32,64,128]{2,1,0:T(8,128)(2,1)}, bf16[32,64,128]{2,1,0:T(8,128)(2,1)S(1)}, u32[]{:S(2)}) copy-start(bf16[32,64,128]{2,1,0:T(8,128)(2,1)S(1)} %get-tuple-element.48.refs_4_) | copy-start | bytes 1572868
  15.2 8.0 %collective-permute-start.3 = (bf16[19,64,128]{2,1,0:T(8,128)(2,1)S(1)}, bf16[19,64,128]{2,1,0:T(8,128)(2,1)S(1)}, u32[]{:S(2)}, u32[]{:S(2)}) collective-permute-start(bf16[19,64,128]{2,1,0:T(8,128)(2,1)S(1)} %get-tuple-element.46), channel_id=1, source_target_pairs={{0,9},{1,10},{2,11},{3,12},{4,13},{5,14},{6,15},{7,8},{8,0},{9,1},... | collective-permute-start | bytes 933896 | tf_op jit(solution)/shard_map/ppermute | solution.py:442
  15.3 8.4 %collective-permute-start.4 = (bf16[19,64,128]{2,1,0:T(8,128)(2,1)S(1)}, bf16[19,64,128]{2,1,0:T(8,128)(2,1)S(1)}, u32[]{:S(2)}, u32[]{:S(2)}) collective-permute-start(bf16[19,64,128]{2,1,0:T(8,128)(2,1)S(1)} %get-tuple-element.47), channel_id=1, source_target_pairs={{0,15},{1,8},{2,9},{3,10},{4,11},{5,12},{6,13},{7,14},{8,0},{9,1},... | collective-permute-start | bytes 933896 | tf_op jit(solution)/shard_map/ppermute | solution.py:442
  15.8 7.9 %collective-permute-start.5 = (bf16[32,64,128]{2,1,0:T(8,128)(2,1)S(1)}, bf16[32,64,128]{2,1,0:T(8,128)(2,1)S(1)}, u32[]{:S(2)}, u32[]{:S(2)}) collective-permute-start(bf16[32,64,128]{2,1,0:T(8,128)(2,1)S(1)} %get-tuple-element.48.refs_4_), channel_id=1, source_target_pairs={{0,8},{1,9},{2,10},{3,11},{4,12},{5,13},{6,14},{7,15},{8,0},{9,1},... | collective-permute-start | bytes 1572872 | tf_op jit(solution)/shard_map/ppermute | solution.py:442
  22.6 1.6 %copy-start.2 = (bf16[32,64,128]{2,1,0:T(8,128)(2,1)}, bf16[32,64,128]{2,1,0:T(8,128)(2,1)S(1)}, u32[]{:S(2)}) copy-start(bf16[32,64,128]{2,1,0:T(8,128)(2,1)S(1)} %get-tuple-element.63.refs_4_) | copy-start | bytes 1572868
  22.7 10.7 %collective-permute-start.14 = (bf16[18,64,128]{2,1,0:T(8,128)(2,1)S(1)}, bf16[18,64,128]{2,1,0:T(8,128)(2,1)S(1)}, u32[]{:S(2)}, u32[]{:S(2)}) collective-permute-start(bf16[18,64,128]{2,1,0:T(8,128)(2,1)S(1)} %get-tuple-element.61), channel_id=1, source_target_pairs={{0,15},{1,8},{2,9},{3,10},{4,11},{5,12},{6,13},{7,14},{8,0},{9,1},... | collective-permute-start | bytes 884744 | tf_op jit(solution)/shard_map/ppermute | solution.py:442
  23.2 10.3 %collective-permute-start.15 = (bf16[18,64,128]{2,1,0:T(8,128)(2,1)S(1)}, bf16[18,64,128]{2,1,0:T(8,128)(2,1)S(1)}, u32[]{:S(2)}, u32[]{:S(2)}) collective-permute-start(bf16[18,64,128]{2,1,0:T(8,128)(2,1)S(1)} %get-tuple-element.62), channel_id=1, source_target_pairs={{0,9},{1,10},{2,11},{3,12},{4,13},{5,14},{6,15},{7,8},{8,0},{9,1},... | collective-permute-start | bytes 884744 | tf_op jit(solution)/shard_map/ppermute | solution.py:442
  23.2 10.3 %collective-permute-start.16 = (bf16[32,64,128]{2,1,0:T(8,128)(2,1)S(1)}, bf16[32,64,128]{2,1,0:T(8,128)(2,1)S(1)}, u32[]{:S(2)}, u32[]{:S(2)}) collective-permute-start(bf16[32,64,128]{2,1,0:T(8,128)(2,1)S(1)} %get-tuple-element.63.refs_4_), channel_id=1, source_target_pairs={{0,8},{1,9},{2,10},{3,11},{4,12},{5,13},{6,14},{7,15},{8,0},{9,1},... | collective-permute-start | bytes 1572872 | tf_op jit(solution)/shard_map/ppermute | solution.py:442
  24.3 9.8 %copy-start.3 = (bf16[32,64,128]{2,1,0:T(8,128)(2,1)}, bf16[32,64,128]{2,1,0:T(8,128)(2,1)S(1)}, u32[]{:S(2)}) copy-start(bf16[32,64,128]{2,1,0:T(8,128)(2,1)S(1)} %get-tuple-element.51.refs_5_) | copy-start | bytes 1572868
  24.3 16.0 %collective-permute-start.6 = (bf16[19,64,128]{2,1,0:T(8,128)(2,1)S(1)}, bf16[19,64,128]{2,1,0:T(8,128)(2,1)S(1)}, u32[]{:S(2)}, u32[]{:S(2)}) collective-permute-start(bf16[19,64,128]{2,1,0:T(8,128)(2,1)S(1)} %get-tuple-element.49), channel_id=1, source_target_pairs={{8,17},{9,18},{10,19},{11,20},{12,21},{13,22},{14,23},{15,16},{16,... | collective-permute-start | bytes 933896 | tf_op jit(solution)/shard_map/ppermute | solution.py:442
  30.4 10.0 %collective-permute-start.7 = (bf16[19,64,128]{2,1,0:T(8,128)(2,1)S(1)}, bf16[19,64,128]{2,1,0:T(8,128)(2,1)S(1)}, u32[]{:S(2)}, u32[]{:S(2)}) collective-permute-start(bf16[19,64,128]{2,1,0:T(8,128)(2,1)S(1)} %get-tuple-element.50), channel_id=1, source_target_pairs={{8,23},{9,16},{10,17},{11,18},{12,19},{13,20},{14,21},{15,22},{16,... | collective-permute-start | bytes 933896 | tf_op jit(solution)/shard_map/ppermute | solution.py:442
  33.4 9.9 %collective-permute-start.8 = (bf16[32,64,128]{2,1,0:T(8,128)(2,1)S(1)}, bf16[32,64,128]{2,1,0:T(8,128)(2,1)S(1)}, u32[]{:S(2)}, u32[]{:S(2)}) collective-permute-start(bf16[32,64,128]{2,1,0:T(8,128)(2,1)S(1)} %get-tuple-element.51.refs_5_), channel_id=1, source_target_pairs={{8,16},{9,17},{10,18},{11,19},{12,20},{13,21},{14,22},{15,23},{16,... | collective-permute-start | bytes 1572872 | tf_op jit(solution)/shard_map/ppermute | solution.py:442
  34.1 9.7 %copy-start.4 = (bf16[32,64,128]{2,1,0:T(8,128)(2,1)}, bf16[32,64,128]{2,1,0:T(8,128)(2,1)S(1)}, u32[]{:S(2)}) copy-start(bf16[32,64,128]{2,1,0:T(8,128)(2,1)S(1)} %get-tuple-element.66.refs_5_) | copy-start | bytes 1572868
  34.1 18.5 %collective-permute-start.17 = (bf16[18,64,128]{2,1,0:T(8,128)(2,1)S(1)}, bf16[18,64,128]{2,1,0:T(8,128)(2,1)S(1)}, u32[]{:S(2)}, u32[]{:S(2)}) collective-permute-start(bf16[18,64,128]{2,1,0:T(8,128)(2,1)S(1)} %get-tuple-element.64), channel_id=1, source_target_pairs={{8,23},{9,16},{10,17},{11,18},{12,19},{13,20},{14,21},{15,22},{16,... | collective-permute-start | bytes 884744 | tf_op jit(solution)/shard_map/ppermute | solution.py:442
  35.2 20.2 %collective-permute-start.18 = (bf16[18,64,128]{2,1,0:T(8,128)(2,1)S(1)}, bf16[18,64,128]{2,1,0:T(8,128)(2,1)S(1)}, u32[]{:S(2)}, u32[]{:S(2)}) collective-permute-start(bf16[18,64,128]{2,1,0:T(8,128)(2,1)S(1)} %get-tuple-element.65), channel_id=1, source_target_pairs={{8,17},{9,18},{10,19},{11,20},{12,21},{13,22},{14,23},{15,16},{16,... | collective-permute-start | bytes 884744 | tf_op jit(solution)/shard_map/ppermute | solution.py:442
  40.3 15.1 %collective-permute-start.19 = (bf16[32,64,128]{2,1,0:T(8,128)(2,1)S(1)}, bf16[32,64,128]{2,1,0:T(8,128)(2,1)S(1)}, u32[]{:S(2)}, u32[]{:S(2)}) collective-permute-start(bf16[32,64,128]{2,1,0:T(8,128)(2,1)S(1)} %get-tuple-element.66.refs_5_), channel_id=1, source_target_pairs={{8,16},{9,17},{10,18},{11,19},{12,20},{13,21},{14,22},{15,23},{16,... | collective-permute-start | bytes 1572872 | tf_op jit(solution)/shard_map/ppermute | solution.py:442
  43.8 12.4 %copy-start.5 = (bf16[32,64,128]{2,1,0:T(8,128)(2,1)}, bf16[32,64,128]{2,1,0:T(8,128)(2,1)S(1)}, u32[]{:S(2)}) copy-start(bf16[32,64,128]{2,1,0:T(8,128)(2,1)S(1)} %get-tuple-element.54.refs_6_) | copy-start | bytes 1572868
  43.8 17.8 %collective-permute-start.9 = (bf16[19,64,128]{2,1,0:T(8,128)(2,1)S(1)}, bf16[19,64,128]{2,1,0:T(8,128)(2,1)S(1)}, u32[]{:S(2)}, u32[]{:S(2)}) collective-permute-start(bf16[19,64,128]{2,1,0:T(8,128)(2,1)S(1)} %get-tuple-element.52), channel_id=1, source_target_pairs={{16,25},{17,26},{18,27},{19,28},{20,29},{21,30},{22,31},{23,24},{2... | collective-permute-start | bytes 933896 | tf_op jit(solution)/shard_map/ppermute | solution.py:442
  52.5 9.7 %collective-permute-start.10 = (bf16[19,64,128]{2,1,0:T(8,128)(2,1)S(1)}, bf16[19,64,128]{2,1,0:T(8,128)(2,1)S(1)}, u32[]{:S(2)}, u32[]{:S(2)}) collective-permute-start(bf16[19,64,128]{2,1,0:T(8,128)(2,1)S(1)} %get-tuple-element.53), channel_id=1, source_target_pairs={{16,31},{17,24},{18,25},{19,26},{20,27},{21,28},{22,29},{23,30},{2... | collective-permute-start | bytes 933896 | tf_op jit(solution)/shard_map/ppermute | solution.py:442
  52.6 9.6 %collective-permute-start.11 = (bf16[32,64,128]{2,1,0:T(8,128)(2,1)S(1)}, bf16[32,64,128]{2,1,0:T(8,128)(2,1)S(1)}, u32[]{:S(2)}, u32[]{:S(2)}) collective-permute-start(bf16[32,64,128]{2,1,0:T(8,128)(2,1)S(1)} %get-tuple-element.54.refs_6_), channel_id=1, source_target_pairs={{16,24},{17,25},{18,26},{19,27},{20,28},{21,29},{22,30},{23,31},{2... | collective-permute-start | bytes 1572872 | tf_op jit(solution)/shard_map/ppermute | solution.py:442
  56.2 10.3 %copy-start.6 = (bf16[32,64,128]{2,1,0:T(8,128)(2,1)}, bf16[32,64,128]{2,1,0:T(8,128)(2,1)S(1)}, u32[]{:S(2)}) copy-start(bf16[32,64,128]{2,1,0:T(8,128)(2,1)S(1)} %get-tuple-element.69.refs_6_) | copy-start | bytes 1572868
  56.2 10.3 %collective-permute-start.20 = (bf16[18,64,128]{2,1,0:T(8,128)(2,1)S(1)}, bf16[18,64,128]{2,1,0:T(8,128)(2,1)S(1)}, u32[]{:S(2)}, u32[]{:S(2)}) collective-permute-start(bf16[18,64,128]{2,1,0:T(8,128)(2,1)S(1)} %get-tuple-element.67), channel_id=1, source_target_pairs={{16,31},{17,24},{18,25},{19,26},{20,27},{21,28},{22,29},{23,30},{2... | collective-permute-start | bytes 884744 | tf_op jit(solution)/shard_map/ppermute | solution.py:442
  61.5 8.8 %collective-permute-start.21 = (bf16[18,64,128]{2,1,0:T(8,128)(2,1)S(1)}, bf16[18,64,128]{2,1,0:T(8,128)(2,1)S(1)}, u32[]{:S(2)}, u32[]{:S(2)}) collective-permute-start(bf16[18,64,128]{2,1,0:T(8,128)(2,1)S(1)} %get-tuple-element.68), channel_id=1, source_target_pairs={{16,25},{17,26},{18,27},{19,28},{20,29},{21,30},{22,31},{23,24},{2... | collective-permute-start | bytes 884744 | tf_op jit(solution)/shard_map/ppermute | solution.py:442
  61.6 8.8 %collective-permute-start.22 = (bf16[32,64,128]{2,1,0:T(8,128)(2,1)S(1)}, bf16[32,64,128]{2,1,0:T(8,128)(2,1)S(1)}, u32[]{:S(2)}, u32[]{:S(2)}) collective-permute-start(bf16[32,64,128]{2,1,0:T(8,128)(2,1)S(1)} %get-tuple-element.69.refs_6_), channel_id=1, source_target_pairs={{16,24},{17,25},{18,26},{19,27},{20,28},{21,29},{22,30},{23,31},{2... | collective-permute-start | bytes 1572872 | tf_op jit(solution)/shard_map/ppermute | solution.py:442
